TPU v7x, 256 devices: a whole 4x4x8 slice. The times are simulated.
256 devices in a mesh: rep: 4 (over y), fsdp: 64 (over z, x, core).
Axes of the slice: x: 4, y: 4, z: 8, core: 2. Of those that a mesh axis runs over, the one named last changes fastest.
Arguments:
- grads: bfloat16 [4, 256, 512, 512], P('rep', None, 'fsdp'), may hold values from -180 to 180
- left_factors: float32 [4, 64, 2, 512, 512], P('rep', 'fsdp'), may hold values from -1 to 1024, as said below
- right_factors: float32 [4, 64, 2, 512, 512], P('rep', 'fsdp'), may hold values from -1 to 1024, as said below
- owners: int32 [4, 64, 1], replicated, may hold values from 0 to 63; in each aligned block of 64 rows (0 to 63, 64 to 127, ..., all dimensions but the last counted through in order) at most 2 rows name the same one
Outputs:
- update: bfloat16 [256, 512, 512], P(None, 'fsdp')
- new_left: float32 [4, 64, 2, 512, 512], P('rep', 'fsdp')
- new_right: float32 [4, 64, 2, 512, 512], P('rep', 'fsdp')
Inputs may be any that keep to these rules, and one draw needn't show every extreme that they name: `left_factors`: symmetric positive definite. `right_factors`: symmetric positive definite. `owners`: in each replica row at most 2 blocks share an owner, and in every draw some owner of some row has exactly 2.
All inputs are finite; a program needn't handle non-finite values.
Results may differ from a plain program's by a relative error of at most 0.018.
Values may be sent and summed in bfloat16 or wider, within the bound.
No kernel may reach another device: no remote copies, remote signals or barrier semaphores. Data moves between devices by JAX's collectives and lax.ppermute only.
A program may use at most 64 MiB of HBM per device.

v0:
```python
import jax
import jax.numpy as jnp
from jax import lax
from jax.sharding import PartitionSpec as P

ITERS = 3


def routing_table(owner_ids, fsdp_count, capacity):
    count = owner_ids.shape[1]
    position = jnp.arange(count, dtype=jnp.int32)
    same_owner = owner_ids[:, :, None] == owner_ids[:, None, :]
    earlier = position[None, :] < position[:, None]
    slot_rank = jnp.sum((same_owner & earlier[None]).astype(jnp.int32), axis=2)
    routing = (owner_ids[:, :, None, None] == jnp.arange(fsdp_count, dtype=jnp.int32)[:, None]) & (
        slot_rank[:, :, None, None] == jnp.arange(capacity, dtype=jnp.int32)
    )
    return routing.astype(jnp.bfloat16)


def inverse_root(matrix):
    highest = lax.Precision.HIGHEST
    identity = jnp.eye(matrix.shape[-1], dtype=jnp.float32)
    frobenius = jnp.sqrt(jnp.sum(matrix * matrix, axis=(1, 2)) + 1e-06)
    scaled_iterate = matrix / frobenius[:, None, None]
    root_iterate = identity[None]
    for sweep in range(ITERS):
        if sweep == 0:
            correction = 1.5 * identity - 0.5 * scaled_iterate
        else:
            product = jnp.einsum("sij,sjk->sik", root_iterate, scaled_iterate, precision=highest)
            correction = 1.5 * identity - 0.5 * product
        if sweep < ITERS - 1:
            scaled_iterate = jnp.einsum(
                "sij,sjk->sik", scaled_iterate, correction, precision=highest
            )
        if sweep == 0:
            root_iterate = correction
        else:
            root_iterate = jnp.einsum("sij,sjk->sik", correction, root_iterate, precision=highest)
    return root_iterate


def owner_step(arrived, left_slots, right_slots):
    new_left = 0.9 * left_slots + 0.1 * jnp.einsum(
        "sik,sjk->sij", arrived, arrived, preferred_element_type=jnp.float32
    )
    new_right = 0.9 * right_slots + 0.1 * jnp.einsum(
        "ski,skj->sij", arrived, arrived, preferred_element_type=jnp.float32
    )
    root_left = inverse_root(new_left).astype(jnp.bfloat16)
    root_right = inverse_root(new_right).astype(jnp.bfloat16)
    half = jnp.einsum(
        "sij,sjk->sik", root_left, arrived, preferred_element_type=jnp.float32
    ).astype(jnp.bfloat16)
    raw = jnp.einsum("sij,sjk->sik", half, root_right, preferred_element_type=jnp.float32)
    grad_norm = jnp.sum(jnp.square(arrived.astype(jnp.float32)), axis=(1, 2))
    raw_norm = jnp.sum(raw * raw, axis=(1, 2))
    factor = jnp.sqrt(grad_norm) * lax.rsqrt(raw_norm + 1e-06)
    slot_update = (raw * factor[:, None, None]).astype(jnp.bfloat16)
    return (new_left, new_right, slot_update)


def shards(grads, left_factors, right_factors, owners):
    rep_count = lax.axis_size("rep")
    fsdp_count = lax.axis_size("fsdp")
    rep_index = lax.axis_index("rep")
    row_count = grads.shape[2]
    block_width = grads.shape[3]
    capacity = left_factors.shape[2]
    per_row = grads.shape[1] // rep_count
    routing = routing_table(owners[:, :, 0], fsdp_count, capacity)
    my_routing = lax.dynamic_index_in_dim(routing, rep_index, 0, keepdims=False)
    summed = lax.psum_scatter(
        grads[0].astype(jnp.float32).astype(jnp.bfloat16), "rep", scatter_dimension=0, tiled=True
    )
    outgoing = jnp.einsum(
        "joa,jc->oac",
        my_routing,
        summed.reshape(per_row, row_count * block_width),
        preferred_element_type=jnp.float32,
    ).astype(jnp.bfloat16)
    outgoing = outgoing.reshape(fsdp_count, capacity, row_count, block_width)
    arrived = lax.all_to_all(outgoing, "fsdp", split_axis=0, concat_axis=2, tiled=True)[0]
    new_left, new_right, slot_update = owner_step(arrived, left_factors[0, 0], right_factors[0, 0])
    returned = lax.all_to_all(
        slot_update.reshape(capacity, fsdp_count, row_count, block_width),
        "fsdp",
        split_axis=1,
        concat_axis=1,
        tiled=True,
    )
    local_rows = jnp.einsum(
        "joa,aoc->jc",
        my_routing,
        returned.reshape(capacity, fsdp_count, row_count * block_width),
        preferred_element_type=jnp.float32,
    ).astype(jnp.bfloat16)
    update = lax.all_gather(
        local_rows.reshape(per_row, row_count, block_width), "rep", axis=0, tiled=True
    )
    return (update, new_left[None, None], new_right[None, None])


def solution(mesh):
    in_specs = (
        P("rep", None, "fsdp", None),
        P("rep", "fsdp", None, None, None),
        P("rep", "fsdp", None, None, None),
        P(),
    )
    out_specs = (
        P(None, "fsdp", None),
        P("rep", "fsdp", None, None, None),
        P("rep", "fsdp", None, None, None),
    )
    return jax.shard_map(shards, mesh=mesh, in_specs=in_specs, out_specs=out_specs, check_vma=False)
```

profile of v0, /device:TPU:32, one launch (start us, length us, event | category | flops | bytes accessed | tf_op | source)
XLA Modules:
  0.0 219.0 jit_solution(11437758949249228579)
XLA Ops:
  7.2 0.0 copy-start.2
  7.2 0.0 reduce-scatter.2.cloned.1.call-start
  7.2 0.7 reduce-scatter.2.cloned.1.call-update
  7.9 0.0 copy-done.2
  7.9 0.1 convert_reduce_fusion
  8.1 37.3 %reduce-scatter.2.cloned.1.call-done = bf16[64,8,512]{2,1,0:T(8,128)(2,1)} async-done(((bf16[256,8,512]{2,1,0:T(8,128)(2,1)}), bf16[64,8,512]{2,1,0:T(8,128)(2,1)}) %reduce-scatter.2.cloned.1.call-update) | async-done | bytes 524304 | tf_op jit(solution)/shard_map/reduce_scatter | solution.py:74
  45.5 1.3 reshape.84
  46.7 0.4 convolution_convert_fusion
  47.2 0.4 copy.18
  47.6 1.1 copy.9
  48.7 10.4 %all-to-all-start = ((bf16[64,2,8,512]{3,2,1,0:T(8,128)(2,1)}), bf16[64,2,8,512]{3,2,1,0:T(8,128)(2,1)S(1)}, u32[]{:S(2)}, u32[]{:S(2)}) async-start(bf16[64,2,8,512]{3,2,1,0:T(8,128)(2,1)} %copy.9), calls=%async_computation.1 | async-start | bytes 2097152 | tf_op jit(solution)/shard_map/all_to_all | solution.py:84
  59.1 0.6 all-gather.2.cloned.1.call-start
  59.7 0.1 fusion.42
  59.8 27.2 %all-to-all-done = bf16[64,2,8,512]{3,2,1,0:T(8,128)(2,1)S(1)} async-done(((bf16[64,2,8,512]{3,2,1,0:T(8,128)(2,1)}), bf16[64,2,8,512]{3,2,1,0:T(8,128)(2,1)S(1)}, u32[]{:S(2)}, u32[]{:S(2)}) %all-to-all-start) | async-done | bytes 1048608 | tf_op jit(solution)/shard_map/all_to_all | solution.py:84
  87.1 2.7 %multiply_reduce_fusion.3 = (f32[2]{0:T(128)S(1)}, f32[2,512,512]{2,1,0:T(8,128)S(1)}) fusion(f32[1,1,2,512,512]{4,3,2,1,0:T(8,128)} %param.5, bf16[64,2,8,512]{3,2,1,0:T(8,128)(2,1)S(1)} %all-to-all-done), kind=kOutput, calls=%fused_computation.25 | convolution fusion | flops 539492352 | bytes 5242888 | tf_op jit(solution)/shard_map/sik,sjk->sij/dot_general | solution.py:45
  89.7 0.0 copy-start.3
  89.8 3.9 %fusion.12 = f32[2,512,512]{2,1,0:T(8,128)S(1)} fusion(f32[512,512]{1,0:T(8,128)S(1)} %fusion.42, f32[2,512,512]{2,1,0:T(8,128)S(1)} %get-tuple-element.6, f32[2]{0:T(128)S(1)} %add_sqrt_fusion.1), kind=kOutput, calls=%fused_computation.24 | convolution fusion | flops 3223322624 | bytes 5242888 | tf_op jit(solution)/shard_map/sij,sjk->sik/dot_general | solution.py:34
  93.7 3.8 %multiply_subtract_fusion.7 = f32[2,512,512]{2,1,0:T(8,128)S(1)} fusion(f32[2,512,512]{2,1,0:T(8,128)S(1)} %fusion.12, f32[512,512]{1,0:T(8,128)S(1)} %fusion.42, f32[2,512,512]{2,1,0:T(8,128)S(1)} %get-tuple-element.6, f32[2]{0:T(128)S(1)} %add_sqrt_fusion.1), kind=kOutput, calls=%fused_computation.20 | convolution fusion | flops 3223846912 | bytes 7340040 | tf_op jit(solution)/shard_map/sij,sjk->sik/dot_general | solution.py:31
  97.5 3.5 %fusion.65 = f32[2,512,512]{2,1,0:T(8,128)S(1)} fusion(f32[2,512,512]{2,1,0:T(8,128)S(1)} %fusion.12, f32[2,512,512]{2,1,0:T(8,128)S(1)} %multiply_subtract_fusion.7), kind=kOutput, calls=%fused_computation.83 | convolution fusion | flops 3221225472 | bytes 6291456 | tf_op jit(solution)/shard_map/sij,sjk->sik/dot_general | solution.py:34
  101.0 0.0 copy-done.3
  101.0 0.0 copy-start
  101.0 4.1 %fusion.10 = f32[2,512,512]{2,1,0:T(8,128)S(1)} fusion(f32[2,512,512]{2,1,0:T(8,128)S(1)} %multiply_subtract_fusion.7, f32[512,512]{1,0:T(8,128)S(1)} %fusion.42, f32[2,512,512]{2,1,0:T(8,128)S(1)} %get-tuple-element.6, f32[2]{0:T(128)S(1)} %add_sqrt_fusion.1), kind=kOutput, calls=%fused_computation.22 | convolution fusion | flops 3222798336 | bytes 7340040 | tf_op jit(solution)/shard_map/sij,sjk->sik/dot_general | solution.py:40
  105.1 0.0 copy-done
  105.2 1.1 multiply_reduce_fusion.2
  106.2 0.0 copy-start.1
  106.2 3.9 %fusion.6 = f32[2,512,512]{2,1,0:T(8,128)S(1)} fusion(f32[512,512]{1,0:T(8,128)S(1)} %fusion.42, f32[2,512,512]{2,1,0:T(8,128)S(1)} %get-tuple-element.4, f32[2]{0:T(128)S(1)} %add_sqrt_fusion), kind=kOutput, calls=%fused_computation.15 | convolution fusion | flops 3223322624 | bytes 5242888 | tf_op jit(solution)/shard_map/sij,sjk->sik/dot_general | solution.py:34
  110.2 3.8 %multiply_subtract_fusion = f32[2,512,512]{2,1,0:T(8,128)S(1)} fusion(f32[2,512,512]{2,1,0:T(8,128)S(1)} %fusion.6, f32[512,512]{1,0:T(8,128)S(1)} %fusion.42, f32[2,512,512]{2,1,0:T(8,128)S(1)} %get-tuple-element.4, f32[2]{0:T(128)S(1)} %add_sqrt_fusion), kind=kOutput, calls=%fused_computation.11 | convolution fusion | flops 3223846912 | bytes 7340040 | tf_op jit(solution)/shard_map/sij,sjk->sik/dot_general | solution.py:31
  114.0 3.5 %fusion.67 = f32[2,512,512]{2,1,0:T(8,128)S(1)} fusion(f32[2,512,512]{2,1,0:T(8,128)S(1)} %fusion.6, f32[2,512,512]{2,1,0:T(8,128)S(1)} %multiply_subtract_fusion), kind=kOutput, calls=%fused_computation.85 | convolution fusion | flops 3221225472 | bytes 6291456 | tf_op jit(solution)/shard_map/sij,sjk->sik/dot_general | solution.py:34
  117.5 0.0 copy-done.1
  117.5 4.1 %fusion.4 = f32[2,512,512]{2,1,0:T(8,128)S(1)} fusion(f32[2,512,512]{2,1,0:T(8,128)S(1)} %multiply_subtract_fusion, f32[512,512]{1,0:T(8,128)S(1)} %fusion.42, f32[2,512,512]{2,1,0:T(8,128)S(1)} %get-tuple-element.4, f32[2]{0:T(128)S(1)} %add_sqrt_fusion), kind=kOutput, calls=%fused_computation.13 | convolution fusion | flops 3222798336 | bytes 7340040 | tf_op jit(solution)/shard_map/sij,sjk->sik/dot_general | solution.py:40
  121.7 3.5 %fusion.66 = f32[2,512,512]{2,1,0:T(8,128)S(1)} fusion(f32[2,512,512]{2,1,0:T(8,128)S(1)} %fusion.10, f32[2,512,512]{2,1,0:T(8,128)S(1)} %fusion.65), kind=kOutput, calls=%fused_computation.84 | convolution fusion | flops 3221225472 | bytes 6291456 | tf_op jit(solution)/shard_map/sij,sjk->sik/dot_general | solution.py:31
  125.2 4.6 %fusion.13 = bf16[2,512,512]{2,1,0:T(8,128)(2,1)} fusion(f32[2,512,512]{2,1,0:T(8,128)S(1)} %fusion.10, f32[2,512,512]{2,1,0:T(8,128)S(1)} %fusion.66, f32[512,512]{1,0:T(8,128)S(1)} %fusion.42), kind=kOutput, calls=%fused_computation.26 | convolution fusion | flops 3222798336 | bytes 6291456 | tf_op jit(solution)/shard_map/sij,sjk->sik/dot_general | solution.py:40
  129.8 3.5 %fusion.68 = f32[2,512,512]{2,1,0:T(8,128)S(1)} fusion(f32[2,512,512]{2,1,0:T(8,128)S(1)} %fusion.4, f32[2,512,512]{2,1,0:T(8,128)S(1)} %fusion.67), kind=kOutput, calls=%fused_computation.86 | convolution fusion | flops 3221225472 | bytes 6291456 | tf_op jit(solution)/shard_map/sij,sjk->sik/dot_general | solution.py:31
  133.3 4.9 %fusion.16 = bf16[2,512,512]{2,1,0:T(8,128)(2,1)} fusion(f32[2,512,512]{2,1,0:T(8,128)S(1)} %fusion.4, f32[2,512,512]{2,1,0:T(8,128)S(1)} %fusion.68, f32[512,512]{1,0:T(8,128)S(1)} %fusion.42), kind=kOutput, calls=%fused_computation.27 | convolution fusion | flops 3222798336 | bytes 6291456 | tf_op jit(solution)/shard_map/sij,sjk->sik/dot_general | solution.py:40
  138.2 0.4 multiply_reduce_fusion.1
  138.6 3.0 %multiply_reduce_fusion = (f32[2]{0:T(128)S(1)}, f32[2,512,512]{2,1,0:T(8,128)S(1)}) fusion(bf16[2,512,512]{2,1,0:T(8,128)(2,1)} %fusion.16, bf16[2,512,512]{2,1,0:T(8,128)(2,1)} %fusion.13, bf16[64,2,8,512]{3,2,1,0:T(8,128)(2,1)S(1)} %all-to-all-done), kind=kOutput, calls=%fused_computation.6 | convolution fusion | flops 1075314688 | bytes 5242888 | tf_op jit(solution)/shard_map/sij,sjk->sik/dot_general | solution.py:56
  141.7 0.3 fusion.20
  142.0 0.1 copy.12
  142.1 34.2 %all_to_all.20 = bf16[2,64,8,512]{3,2,0,1:T(8,128)(2,1)S(1)} all-to-all(bf16[2,64,8,512]{3,2,0,1:T(8,128)(2,1)S(1)} %copy.12), channel_id=1, replica_groups=mesh['rep'=4,'fsdp'=64] {'fsdp'}, dimensions={1} | all-to-all | bytes 2097152 | tf_op jit(solution)/shard_map/all_to_all | solution.py:86
  176.4 0.8 reshape.87
  177.2 1.3 fusion
  178.5 1.0 copy.19
  179.4 0.0 all-gather.2.cloned.1.call-update
  179.5 29.4 %all-gather.2.cloned.1.call-done = bf16[256,8,512]{2,1,0:T(8,128)(2,1)} async-done(((bf16[64,8,512]{2,1,0:T(8,128)(2,1)}), bf16[256,8,512]{2,1,0:T(8,128)(2,1)}) %all-gather.2.cloned.1.call-update) | async-done | bytes 2097168 | tf_op jit(solution)/shard_map/all_gather | solution.py:99
  208.8 3.0 %copy.42 = bf16[256,8,512]{2,1,0:T(8,128)(2,1)} copy(bf16[256,8,512]{2,1,0:T(8,128)(2,1)} %all-gather.2.cloned.1.call-done) | data formatting | bytes 4194304
  (8 shorter events, 0.1 us)
Async XLA Ops:
  7.2 0.8 copy-start.2
  7.2 38.3 %reduce-scatter.2.cloned.1.call-start = ((), (), s32[]{:S(2)}) async-start(), calls=%async_computation.3 | async-start | bytes 2621440 | tf_op jit(solution)/shard_map/reduce_scatter | solution.py:74
  48.7 38.4 %all-to-all-start = ((bf16[64,2,8,512]{3,2,1,0:T(8,128)(2,1)}), bf16[64,2,8,512]{3,2,1,0:T(8,128)(2,1)S(1)}, u32[]{:S(2)}, u32[]{:S(2)}) async-start(bf16[64,2,8,512]{3,2,1,0:T(8,128)(2,1)} %copy.9), calls=%async_computation.1 | async-start | bytes 2097152 | tf_op jit(solution)/shard_map/all_to_all | solution.py:84
  59.1 149.7 %all-gather.2.cloned.1.call-start = ((), (), s32[]{:S(2)}) async-start(), calls=%async_computation.4 | async-start | bytes 2621440 | tf_op jit(solution)/shard_map/all_gather | solution.py:99
  89.7 11.3 %copy-start.3 = (f32[2,512,512]{2,1,0:T(8,128)}, f32[2,512,512]{2,1,0:T(8,128)S(1)}, u32[]{:S(2)}) copy-start(f32[2,512,512]{2,1,0:T(8,128)S(1)} %get-tuple-element.6) | copy-start | bytes 6291460
  101.0 4.1 %copy-start = (f32[1,1,2,512,512]{4,3,2,1,0:T(8,128)S(1)}, f32[1,1,2,512,512]{4,3,2,1,0:T(8,128)}, u32[]{:S(2)}) copy-start(f32[1,1,2,512,512]{4,3,2,1,0:T(8,128)} %param.6) | copy-start | bytes 6291460
  106.2 11.3 %copy-start.1 = (f32[2,512,512]{2,1,0:T(8,128)}, f32[2,512,512]{2,1,0:T(8,128)S(1)}, u32[]{:S(2)}) copy-start(f32[2,512,512]{2,1,0:T(8,128)S(1)} %get-tuple-element.4) | copy-start | bytes 6291460
Sparse Core Ops, SparseCore 0:
  10.6 34.8 reduce-scatter.1
  179.6 29.2 all-gather.1
where the time goes:
time: 223 us; the launch traced here: 219 us
  waiting for transfers between devices  94.6 us (42%)
  matrix products  55.8 us (25%)
  blocking collectives  34.2 us (15%)
  between operations  14.5 us (7%)
  starting transfers between devices  11.1 us (5%)
  local copies, waits for them, and re-layouts  7.75 us (3%)
    reduce_scatter x1, waiting for transfers between devices, shards(): lax.psum_scatter(grads[0].astype(jnp.float32).astype(jnp.bfloat16), 'rep'...  37.3 us
    all_to_all x1, blocking collectives, shards(): lax.all_to_all(slot_update.reshape(capacity, fsdp_count, row_count, block...  34.2 us
    all_gather x1, waiting for transfers between devices, shards(): lax.all_gather(local_rows.reshape(per_row, row_count, block_width), 'rep'...  29.4 us
    all_to_all x1, waiting for transfers between devices, shards(): lax.all_to_all(outgoing, 'fsdp', split_axis=0, concat_axis=2, tiled=True)[0]  27.2 us
    dot_general x4, matrix products, inverse_root(): jnp.einsum('sij,sjk->sik', correction, root_iterate, precision=highest)  17.7 us
    dot_general x4, matrix products, inverse_root(): jnp.einsum('sij,sjk->sik', scaled_iterate, correction, precision=highest)  14.9 us
    dot_general x4, matrix products, inverse_root(): jnp.einsum('sij,sjk->sik', root_iterate, scaled_iterate, precision=highest)  14.6 us
    all_to_all x1, starting transfers between devices, shards(): lax.all_to_all(outgoing, 'fsdp', split_axis=0, concat_axis=2, tiled=True)[0]  10.4 us
  transfers between devices with their start and end apart: 3, of which 3 were waited for; matrix products, arithmetic and copies ran while one was open for 0% of the time, Pallas kernels for 0%

commit v1 on v0

v1 whole, which is shorter than its diff:
```python
import functools

import jax
import jax.numpy as jnp
from jax import lax
from jax.experimental import pallas as pl
from jax.experimental.pallas import tpu as pltpu
from jax.sharding import PartitionSpec as P

BF16 = jnp.bfloat16
F32 = jnp.float32
VMEM_BYTES = 50 * 1024 * 1024


def routing_tables(owner_ids, fsdp_count, capacity):
    count = owner_ids.shape[0]
    position = jnp.arange(count, dtype=jnp.int32)
    same_owner = owner_ids[:, None] == owner_ids[None, :]
    earlier = position[None, :] < position[:, None]
    slot_rank = jnp.sum((same_owner & earlier).astype(jnp.int32), axis=1)
    slot_of = owner_ids * capacity + slot_rank
    slots = jnp.arange(fsdp_count * capacity, dtype=jnp.int32)
    holds = slot_of[None, :] == slots[:, None]
    block_of = count + jnp.sum(jnp.where(holds, position[None, :] - count, 0), axis=1)
    return block_of.astype(jnp.int32), slot_of.astype(jnp.int32)


def pack_kernel(table, own, first_a, first_b, second_a, second_b, out, held):
    half = first_a.shape[1]
    count = 2 * half
    for k, (first, second) in enumerate(((first_a, second_a), (first_b, second_b))):
        total = own[0, k].astype(F32) + first[0].astype(F32) + second[...].astype(F32)
        held[k * half : (k + 1) * half] = total
    held[count] = jnp.zeros(held.shape[1:], F32)
    owners, capacity = out.shape[0], out.shape[1]

    def move(o, carry):
        for s in range(capacity):
            out[o, s] = held[table[1 + o * capacity + s]].astype(BF16)
        return carry

    lax.fori_loop(0, owners, move, 0, unroll=4)


def dot(a, b, ca=1, cb=0):
    return lax.dot_general(a, b, (((ca,), (cb,)), ((), ())), preferred_element_type=F32)


def inverse_root(matrix, identity):
    y = matrix * lax.rsqrt(jnp.sum(matrix * matrix) + 1e-06)
    yb = y.astype(BF16)
    y2 = dot(yb, yb)
    s = 2.25 * y - 1.5 * y2 + 0.25 * dot(y2.astype(BF16), yb)
    sb = s.astype(BF16)
    s2 = dot(sb, sb)
    q = -2.4375 * s + 1.6875 * s2 + dot(s2.astype(BF16), (0.0625 * s2 - 0.5625 * s).astype(BF16))
    z = 3.375 * identity + 1.5 * q - 1.125 * y - 0.5 * dot(yb, q.astype(BF16))
    return z.astype(BF16)


def owner_kernel(arrived, left, right, new_left, new_right, out):
    n = left.shape[1]
    wide = arrived[:, 0].astype(F32).reshape(n, n)
    grad_norm = jnp.sum(wide * wide)
    grad = wide.astype(BF16)
    row = lax.broadcasted_iota(jnp.int32, (n, n), 0)
    col = lax.broadcasted_iota(jnp.int32, (n, n), 1)
    identity = (row == col).astype(F32)
    nl = 0.9 * left[0] + 0.1 * dot(grad, grad, 1, 1)
    nr = 0.9 * right[0] + 0.1 * dot(grad, grad, 0, 0)
    new_left[0] = nl
    new_right[0] = nr
    root_left = inverse_root(nl, identity)
    root_right = inverse_root(nr, identity)
    half = dot(root_left, grad).astype(BF16)
    raw = dot(half, root_right)
    raw_norm = jnp.sum(raw * raw)
    factor = jnp.sqrt(grad_norm) * lax.rsqrt(raw_norm + 1e-06)
    out[:, 0] = (raw * factor).reshape(out.shape[0], out.shape[2], out.shape[3]).astype(BF16)


def unpack_kernel(table, slots, out_a, out_b):
    half = out_a.shape[0]

    def move(j, carry):
        out_a[j] = slots[table[j]]
        out_b[j] = slots[table[half + j]]
        return carry

    lax.fori_loop(0, half, move, 0, unroll=4)


def place_kernel(table, *refs):
    parts, out, sems = refs[:8], refs[8], refs[9]
    copies = [
        pltpu.make_async_copy(part, out.at[table[i // 2], i % 2], sems.at[i]) for i, part in enumerate(parts)
    ]
    for copy in copies:
        copy.start()
    for copy in copies:
        copy.wait()


def shards(grads, left_factors, right_factors, owners):
    reps = lax.axis_size("rep")
    fsdp = lax.axis_size("fsdp")
    r = lax.axis_index("rep").astype(jnp.int32)
    rows, width = grads.shape[2], grads.shape[3]
    capacity, order = left_factors.shape[2], left_factors.shape[3]
    per_row = grads.shape[1] // reps
    half = per_row // 2
    own_owners = lax.dynamic_index_in_dim(owners[:, :, 0], r, 0, keepdims=False)
    block_of, slot_of = routing_tables(own_owners, fsdp, capacity)

    swap1 = [(i, i ^ 1) for i in range(reps)]
    swap3 = [(i, i ^ 3) for i in range(reps)]
    parts = grads.reshape(reps, 2, half, rows, width)

    def part(k, h):
        return lax.dynamic_index_in_dim(parts[:, h], r ^ k, 0, keepdims=False)

    first_a = lax.ppermute(jnp.stack([part(1, 0), part(2, 0)]), "rep", swap1)
    first_b = lax.ppermute(jnp.stack([part(3, 1), part(2, 1)]), "rep", swap3)
    second_a = lax.ppermute(part(3, 0) + first_a[1], "rep", swap3)
    second_b = lax.ppermute(part(1, 1) + first_b[1], "rep", swap1)

    outgoing = pl.pallas_call(
        pack_kernel,
        out_shape=jax.ShapeDtypeStruct((fsdp, capacity, rows, width), BF16),
        grid_spec=pltpu.PrefetchScalarGridSpec(
            num_scalar_prefetch=1,
            grid=(1,),
            in_specs=[
                pl.BlockSpec((1, 2, half, rows, width), lambda i, t: (t[0], 0, 0, 0, 0)),
                pl.BlockSpec((1, half, rows, width), lambda i, t: (0, 0, 0, 0)),
                pl.BlockSpec((1, half, rows, width), lambda i, t: (0, 0, 0, 0)),
                pl.BlockSpec((half, rows, width), lambda i, t: (0, 0, 0)),
                pl.BlockSpec((half, rows, width), lambda i, t: (0, 0, 0)),
            ],
            out_specs=pl.BlockSpec((fsdp, capacity, rows, width), lambda i, t: (0, 0, 0, 0)),
            scratch_shapes=[pltpu.VMEM((per_row + 1, rows, width), F32)],
        ),
        compiler_params=pltpu.CompilerParams(vmem_limit_bytes=VMEM_BYTES),
        name="pack",
    )(jnp.concatenate([r[None], block_of]), parts, first_a, first_b, second_a, second_b)

    arrived = lax.all_to_all(outgoing, "fsdp", split_axis=0, concat_axis=0, tiled=True)

    factor_spec = pl.BlockSpec((1, order, order), lambda s: (s, 0, 0))
    slot_spec = pl.BlockSpec((fsdp, 1, rows, width), lambda s: (0, s, 0, 0))
    new_left, new_right, slot_update = pl.pallas_call(
        owner_kernel,
        grid=(capacity,),
        in_specs=[slot_spec, factor_spec, factor_spec],
        out_specs=[factor_spec, factor_spec, slot_spec],
        out_shape=[
            jax.ShapeDtypeStruct((capacity, order, order), F32),
            jax.ShapeDtypeStruct((capacity, order, order), F32),
            jax.ShapeDtypeStruct((fsdp, capacity, rows, width), BF16),
        ],
        compiler_params=pltpu.CompilerParams(vmem_limit_bytes=VMEM_BYTES),
        name="owner",
    )(arrived, left_factors[0, 0], right_factors[0, 0])

    returned = lax.all_to_all(slot_update, "fsdp", split_axis=0, concat_axis=0, tiled=True)

    whole = pl.BlockSpec((half, rows, width), lambda i, t: (0, 0, 0))
    mine_a, mine_b = pl.pallas_call(
        unpack_kernel,
        out_shape=[jax.ShapeDtypeStruct((half, rows, width), BF16)] * 2,
        grid_spec=pltpu.PrefetchScalarGridSpec(
            num_scalar_prefetch=1,
            grid=(1,),
            in_specs=[pl.BlockSpec((fsdp * capacity, rows, width), lambda i, t: (0, 0, 0))],
            out_specs=[whole, whole],
        ),
        compiler_params=pltpu.CompilerParams(vmem_limit_bytes=VMEM_BYTES),
        name="unpack",
    )(slot_of, returned.reshape(fsdp * capacity, rows, width))

    plus = [(i, (i + 1) % reps) for i in range(reps)]
    minus = [(i, (i - 1) % reps) for i in range(reps)]
    left_a = lax.ppermute(mine_a, "rep", plus)
    right_b = lax.ppermute(mine_b, "rep", minus)
    left_b = lax.ppermute(mine_b, "rep", plus)
    right_a = lax.ppermute(mine_a, "rep", minus)
    far_a = lax.ppermute(left_a, "rep", plus)
    far_b = lax.ppermute(right_b, "rep", minus)
    places = jnp.stack([r, (r + 3) % reps, (r + 1) % reps, (r + 2) % reps])
    update = pl.pallas_call(
        place_kernel,
        out_shape=jax.ShapeDtypeStruct((reps, 2, half, rows, width), BF16),
        grid_spec=pltpu.PrefetchScalarGridSpec(
            num_scalar_prefetch=1,
            grid=(1,),
            in_specs=[pl.BlockSpec(memory_space=pl.ANY)] * 8,
            out_specs=pl.BlockSpec(memory_space=pl.ANY),
            scratch_shapes=[pltpu.SemaphoreType.DMA((8,))],
        ),
        name="place",
    )(places, mine_a, mine_b, left_a, left_b, right_a, right_b, far_a, far_b)
    return (update.reshape(reps * per_row, rows, width), new_left[None, None], new_right[None, None])


def solution(mesh):
    in_specs = (
        P("rep", None, "fsdp", None),
        P("rep", "fsdp", None, None, None),
        P("rep", "fsdp", None, None, None),
        P(),
    )
    out_specs = (
        P(None, "fsdp", None),
        P("rep", "fsdp", None, None, None),
        P("rep", "fsdp", None, None, None),
    )
    return jax.shard_map(shards, mesh=mesh, in_specs=in_specs, out_specs=out_specs, check_vma=False)
```

time: 223 us -> 206 us (0.924); the launches traced: 219 us -> 205 us
  Pallas kernels: 0 us -> 81.9 us
  waiting for transfers between devices: 94.6 us -> 27.6 us
  matrix products: 55.8 us -> 0 us
  blocking collectives: 34.2 us -> 73.6 us
  between operations: 14.5 us -> 0.81 us
  local copies, waits for them, and re-layouts: 7.75 us -> 3.24 us
  starting transfers between devices: 11.1 us -> 15.6 us
    pallas_call x0 -> x4, Pallas kernels: none -> 81.9 us  [the longest x1 65.4 us: shards(): pl.pallas_call(place_kernel, out_shape=jax.ShapeDtypeStruct((reps, 2, hal...]
    dot_general x17 -> x0, matrix products: 55.8 us -> none  [the longest x4 17.7 us: inverse_root(): jnp.einsum('sij,sjk->sik', correction, root_iterate, precision=highest)]
    all_to_all x1 -> x2, blocking collectives: 34.2 us -> 73.6 us  [the longest x1 39.3 us: shards(): lax.all_to_all(outgoing, 'fsdp', split_axis=0, concat_axis=0, tiled=True)]
    reduce_scatter x1 -> x0, waiting for transfers between devices: 37.3 us -> none  [shards(): lax.psum_scatter(grads[0].astype(jnp.float32).astype(jnp.bfloat16), 'rep'...]
    all_gather x1 -> x0, waiting for transfers between devices: 29.4 us -> none  [shards(): lax.all_gather(local_rows.reshape(per_row, row_count, block_width), 'rep'...]
    ppermute x0 -> x10, waiting for transfers between devices: none -> 27.6 us  [the longest x1 8.93 us: shards(): first_a = lax.ppermute(jnp.stack([part(1, 0), part(2, 0)]), 'rep', swap1)]
    all_to_all x1 -> x0, waiting for transfers between devices: 27.2 us -> none  [shards(): lax.all_to_all(outgoing, 'fsdp', split_axis=0, concat_axis=2, tiled=True)[0]]
    ppermute x0 -> x10, starting transfers between devices: none -> 15.6 us  [the longest x1 3.26 us: shards(): far_b = lax.ppermute(right_b, 'rep', minus)]
  transfers between devices with their start and end apart: 3 -> 10, of which waited for: 3 -> 8; matrix products, arithmetic and copies ran while one was open for 0% -> 1% of each run, Pallas kernels for 0% -> 0%
where the time goes in v1:
time: 206 us; the launch traced here: 205 us
  Pallas kernels  81.9 us (40%)
  blocking collectives  73.6 us (36%)
  waiting for transfers between devices  27.6 us (13%)
  starting transfers between devices  15.6 us (8%)
  local copies, waits for them, and re-layouts  3.24 us (2%)
  other arithmetic  2.77 us (1%)
    pallas_call x1, Pallas kernels, shards(): pl.pallas_call(place_kernel, out_shape=jax.ShapeDtypeStruct((reps, 2, hal...  65.4 us
    all_to_all x1, blocking collectives, shards(): lax.all_to_all(outgoing, 'fsdp', split_axis=0, concat_axis=0, tiled=True)  39.3 us
    all_to_all x1, blocking collectives, shards(): lax.all_to_all(slot_update, 'fsdp', split_axis=0, concat_axis=0, tiled=True)  34.2 us
    pallas_call x1, Pallas kernels, shards(): pl.pallas_call(owner_kernel, grid=(capacity,), in_specs=[slot_spec, facto...  13.8 us
    ppermute x1, waiting for transfers between devices, shards(): first_a = lax.ppermute(jnp.stack([part(1, 0), part(2, 0)]), 'rep', swap1)  8.93 us
    ppermute x1, waiting for transfers between devices, shards(): left_a = lax.ppermute(mine_a, 'rep', plus)  5.08 us
    ppermute x1, waiting for transfers between devices, shards(): second_a = lax.ppermute(part(3, 0) + first_a[1], 'rep', swap3)  5.03 us
    ppermute x1, waiting for transfers between devices, shards(): far_a = lax.ppermute(left_a, 'rep', plus)  4.94 us
  transfers between devices with their start and end apart: 10, of which 8 were waited for; matrix products, arithmetic and copies ran while one was open for 1% of the time, Pallas kernels for 0%

profile of v1, /device:TPU:32, one launch (start us, length us, event | category | flops | bytes accessed | tf_op | source)
XLA Modules:
  0.0 205.4 jit_solution(11164149703814424726)
XLA Ops:
  0.6 1.8 fusion.4
  2.4 0.0 copy-start.8
  2.5 0.8 pad_maximum_fusion
  3.3 1.6 collective-permute-start
  4.9 0.8 pad_maximum_fusion.1
  5.8 2.2 %collective-permute-start.1 = (bf16[2,32,8,512]{3,2,1,0:T(8,128)(2,1)}, bf16[2,32,8,512]{3,2,1,0:T(8,128)(2,1)S(1)}, u32[]{:S(2)}, u32[]{:S(2)}) collective-permute-start(bf16[2,32,8,512]{3,2,1,0:T(8,128)(2,1)} %pad_maximum_fusion.1), channel_id=1, source_target_pairs={{0,192},{64,128},{128,64},{192,0},{1,193},{65,129},{129,65},{193,1... | collective-permute-start | bytes 1572872 | tf_op jit(solution)/shard_map/ppermute | solution.py:123
  8.0 0.0 copy-done.8
  8.0 0.2 convert_reduce_fusion
  8.2 0.1 select_reduce_fusion
  8.3 8.9 %collective-permute-done.first_a = bf16[2,32,8,512]{3,2,1,0:T(8,128)(2,1)S(1)} collective-permute-done((bf16[2,32,8,512]{3,2,1,0:T(8,128)(2,1)}, bf16[2,32,8,512]{3,2,1,0:T(8,128)(2,1)S(1)}, u32[]{:S(2)}, u32[]{:S(2)}) %collective-permute-start) | collective-permute-done | bytes 524320 | tf_op jit(solution)/shard_map/ppermute | solution.py:122
  17.2 3.1 %collective-permute-start.2 = (bf16[32,8,512]{2,1,0:T(8,128)(2,1)S(1)}, bf16[32,8,512]{2,1,0:T(8,128)(2,1)S(1)}, u32[]{:S(2)}, u32[]{:S(2)}) collective-permute-start(bf16[32,8,512]{2,1,0:T(8,128)(2,1)S(1)} %fusion.1), channel_id=1, source_target_pairs={{0,192},{64,128},{128,64},{192,0},{1,193},{65,129},{129,65},{193,1... | collective-permute-start | bytes 786440 | tf_op jit(solution)/shard_map/ppermute | solution.py:124
  20.3 0.6 collective-permute-done.1.first_b
  21.0 0.1 collective-permute-start.3
  21.1 0.1 pad_add_fusion.table
  21.2 5.0 %collective-permute-done.2.second_a = bf16[32,8,512]{2,1,0:T(8,128)(2,1)S(1)} collective-permute-done((bf16[32,8,512]{2,1,0:T(8,128)(2,1)S(1)}, bf16[32,8,512]{2,1,0:T(8,128)(2,1)S(1)}, u32[]{:S(2)}, u32[]{:S(2)}) %collective-permute-start.2) | collective-permute-done | bytes 262176 | tf_op jit(solution)/shard_map/ppermute | solution.py:124
  26.2 1.4 collective-permute-done.3.second_b
  27.6 2.1 %pack.1 = bf16[64,2,8,512]{3,2,1,0:T(8,128)(2,1)S(1)} custom-call(s32[129]{0:T(256)S(1)} %pad_add_fusion.table, bf16[4,2,32,8,512]{4,3,2,1,0:T(8,128)(2,1)} %bitcast.37, bf16[2,32,8,512]{3,2,1,0:T(8,128)(2,1)S(1)} %collective-permute-done.first_a, bf16[2,32,8,512]{3,2,1,0:T(8,128)(2,1)S(1)} %collective-permute-done.1.first_b, ...), custom_call_target="tpu_custom_call" | custom-call | tf_op jit(solution)/shard_map/pack/pallas_call | solution.py:127
  29.6 39.3 %all_to_all.10.arrived = bf16[64,2,8,512]{3,2,1,0:T(8,128)(2,1)S(1)} all-to-all(bf16[64,2,8,512]{3,2,1,0:T(8,128)(2,1)S(1)} %pack.1), channel_id=1, replica_groups=mesh['rep'=4,'fsdp'=64] {'fsdp'}, dimensions={0} | all-to-all | bytes 2097152 | tf_op jit(solution)/shard_map/all_to_all | solution.py:147
  69.0 13.8 %owner.1 = (f32[2,512,512]{2,1,0:T(8,128)}, f32[2,512,512]{2,1,0:T(8,128)}, bf16[64,2,8,512]{3,2,1,0:T(8,128)(2,1)S(1)}) custom-call(bf16[64,2,8,512]{3,2,1,0:T(8,128)(2,1)S(1)} %all_to_all.10.arrived, f32[2,512,512]{2,1,0:T(8,128)} %bitcast.38, f32[2,512,512]{2,1,0:T(8,128)} %bitcast.39), custom_call_target="tpu_custom_call" | custom-call | tf_op jit(solution)/shard_map/owner/pallas_call | solution.py:151
  82.8 34.2 %all_to_all.11 = bf16[64,2,8,512]{3,2,1,0:T(8,128)(2,1)S(1)} all-to-all(bf16[64,2,8,512]{3,2,1,0:T(8,128)(2,1)S(1)} %get-tuple-element.8), channel_id=1, replica_groups=mesh['rep'=4,'fsdp'=64] {'fsdp'}, dimensions={0} | all-to-all | bytes 2097152 | tf_op jit(solution)/shard_map/all_to_all | solution.py:165
  117.0 0.6 unpack.1
  117.6 0.0 copy-start
  117.6 0.0 copy-start.1
  117.7 0.4 collective-permute-start.4
  118.0 2.9 %collective-permute-start.7 = (bf16[32,8,512]{2,1,0:T(8,128)(2,1)S(1)}, bf16[32,8,512]{2,1,0:T(8,128)(2,1)S(1)}, u32[]{:S(2)}, u32[]{:S(2)}) collective-permute-start(bf16[32,8,512]{2,1,0:T(8,128)(2,1)S(1)} %get-tuple-element.10.refs_1_), channel_id=1, source_target_pairs={{0,192},{64,0},{128,64},{192,128},{1,193},{65,1},{129,65},{193,129... | collective-permute-start | bytes 786440 | tf_op jit(solution)/shard_map/ppermute | solution.py:184
  121.0 1.0 collective-permute-start.6
  122.0 1.0 collective-permute-start.5
  123.0 5.1 %collective-permute-done.4.refs_2_ = bf16[32,8,512]{2,1,0:T(8,128)(2,1)S(1)} collective-permute-done((bf16[32,8,512]{2,1,0:T(8,128)(2,1)S(1)}, bf16[32,8,512]{2,1,0:T(8,128)(2,1)S(1)}, u32[]{:S(2)}, u32[]{:S(2)}) %collective-permute-start.4) | collective-permute-done | bytes 262176 | tf_op jit(solution)/shard_map/ppermute | solution.py:183
  128.1 0.0 copy-start.2
  128.1 0.0 collective-permute-start.8
  128.1 0.0 collective-permute-done.7.refs_5_
  128.1 0.0 copy-start.3
  128.1 3.3 %collective-permute-start.9 = (bf16[32,8,512]{2,1,0:T(8,128)(2,1)S(1)}, bf16[32,8,512]{2,1,0:T(8,128)(2,1)S(1)}, u32[]{:S(2)}, u32[]{:S(2)}) collective-permute-start(bf16[32,8,512]{2,1,0:T(8,128)(2,1)S(1)} %collective-permute-done.7.refs_5_), channel_id=1, source_target_pairs={{0,192},{64,0},{128,64},{192,128},{1,193},{65,1},{129,65},{193,129... | collective-permute-start | bytes 786440 | tf_op jit(solution)/shard_map/ppermute | solution.py:188
  131.4 0.7 pad_add_fusion.1.table
  132.0 1.3 collective-permute-done.6.refs_4_
  133.3 0.0 copy-start.4
  133.3 0.4 collective-permute-done.5.refs_3_
  133.7 4.9 %collective-permute-done.8.refs_6_ = bf16[32,8,512]{2,1,0:T(8,128)(2,1)S(1)} collective-permute-done((bf16[32,8,512]{2,1,0:T(8,128)(2,1)S(1)}, bf16[32,8,512]{2,1,0:T(8,128)(2,1)S(1)}, u32[]{:S(2)}, u32[]{:S(2)}) %collective-permute-start.8) | collective-permute-done | bytes 262176 | tf_op jit(solution)/shard_map/ppermute | solution.py:187
  138.6 0.0 collective-permute-done.9.refs_7_
  138.6 0.0 copy-done
  138.6 0.0 copy-done.1
  138.7 0.0 copy-done.2
  138.7 0.0 copy-done.3
  138.7 0.0 copy-done.4
  138.7 0.0 copy-done.5
  138.7 0.6 copy-done.6
  139.3 0.7 copy-done.7
  140.1 65.4 %place.1 = bf16[4,2,32,8,512]{4,3,2,1,0:T(8,128)(2,1)} custom-call(s32[4]{0:T(128)} %pad_add_fusion.1.table, bf16[32,8,512]{2,1,0:T(8,128)(2,1)} %copy-done, bf16[32,8,512]{2,1,0:T(8,128)(2,1)} %copy-done.1, bf16[32,8,512]{2,1,0:T(8,128)(2,1)} %copy-done.2, bf16[32,8,512]{2,1,0:T(8,128)(2,1)} %copy-done.5, bf16[32,8,512]{2,1,0:T(8,128)(2,1)} %copy-done.4, ...), custom_call_target="tpu_custom_call" | custom-call | tf_op jit(solution)/shard_map/place/pallas_call | solution.py:190
  (10 shorter events, 0.2 us)
Async XLA Ops:
  2.4 5.5 %copy-start.8 = (s32[4,64,1]{1,2,0:T(1,128)S(1)}, s32[4,64,1]{1,2,0:T(1,128)}, u32[]{:S(2)}) copy-start(s32[4,64,1]{1,2,0:T(1,128)} %param.7) | copy-start | bytes 3076
  3.3 13.9 %collective-permute-start = (bf16[2,32,8,512]{3,2,1,0:T(8,128)(2,1)}, bf16[2,32,8,512]{3,2,1,0:T(8,128)(2,1)S(1)}, u32[]{:S(2)}, u32[]{:S(2)}) collective-permute-start(bf16[2,32,8,512]{3,2,1,0:T(8,128)(2,1)} %pad_maximum_fusion), channel_id=1, source_target_pairs={{0,64},{64,0},{128,192},{192,128},{1,65},{65,1},{129,193},{193,129... | collective-permute-start | bytes 1572872 | tf_op jit(solution)/shard_map/ppermute | solution.py:122
  5.8 15.2 %collective-permute-start.1 = (bf16[2,32,8,512]{3,2,1,0:T(8,128)(2,1)}, bf16[2,32,8,512]{3,2,1,0:T(8,128)(2,1)S(1)}, u32[]{:S(2)}, u32[]{:S(2)}) collective-permute-start(bf16[2,32,8,512]{3,2,1,0:T(8,128)(2,1)} %pad_maximum_fusion.1), channel_id=1, source_target_pairs={{0,192},{64,128},{128,64},{192,0},{1,193},{65,129},{129,65},{193,1... | collective-permute-start | bytes 1572872 | tf_op jit(solution)/shard_map/ppermute | solution.py:123
  17.2 9.0 %collective-permute-start.2 = (bf16[32,8,512]{2,1,0:T(8,128)(2,1)S(1)}, bf16[32,8,512]{2,1,0:T(8,128)(2,1)S(1)}, u32[]{:S(2)}, u32[]{:S(2)}) collective-permute-start(bf16[32,8,512]{2,1,0:T(8,128)(2,1)S(1)} %fusion.1), channel_id=1, source_target_pairs={{0,192},{64,128},{128,64},{192,0},{1,193},{65,129},{129,65},{193,1... | collective-permute-start | bytes 786440 | tf_op jit(solution)/shard_map/ppermute | solution.py:124
  21.0 6.6 %collective-permute-start.3 = (bf16[32,8,512]{2,1,0:T(8,128)(2,1)S(1)}, bf16[32,8,512]{2,1,0:T(8,128)(2,1)S(1)}, u32[]{:S(2)}, u32[]{:S(2)}) collective-permute-start(bf16[32,8,512]{2,1,0:T(8,128)(2,1)S(1)} %fusion), channel_id=1, source_target_pairs={{0,64},{64,0},{128,192},{192,128},{1,65},{65,1},{129,193},{193,129... | collective-permute-start | bytes 786440 | tf_op jit(solution)/shard_map/ppermute | solution.py:125
  117.6 21.0 %copy-start = (bf16[32,8,512]{2,1,0:T(8,128)(2,1)}, bf16[32,8,512]{2,1,0:T(8,128)(2,1)S(1)}, u32[]{:S(2)}) copy-start(bf16[32,8,512]{2,1,0:T(8,128)(2,1)S(1)} %get-tuple-element.9.refs_0_) | copy-start | bytes 786436
  117.6 21.0 %copy-start.1 = (bf16[32,8,512]{2,1,0:T(8,128)(2,1)}, bf16[32,8,512]{2,1,0:T(8,128)(2,1)S(1)}, u32[]{:S(2)}) copy-start(bf16[32,8,512]{2,1,0:T(8,128)(2,1)S(1)} %get-tuple-element.10.refs_1_) | copy-start | bytes 786436
  117.7 10.4 %collective-permute-start.4 = (bf16[32,8,512]{2,1,0:T(8,128)(2,1)S(1)}, bf16[32,8,512]{2,1,0:T(8,128)(2,1)S(1)}, u32[]{:S(2)}, u32[]{:S(2)}) collective-permute-start(bf16[32,8,512]{2,1,0:T(8,128)(2,1)S(1)} %get-tuple-element.9.refs_0_), channel_id=1, source_target_pairs={{0,64},{64,128},{128,192},{192,0},{1,65},{65,129},{129,193},{193,1... | collective-permute-start | bytes 786440 | tf_op jit(solution)/shard_map/ppermute | solution.py:183
  118.0 10.1 %collective-permute-start.7 = (bf16[32,8,512]{2,1,0:T(8,128)(2,1)S(1)}, bf16[32,8,512]{2,1,0:T(8,128)(2,1)S(1)}, u32[]{:S(2)}, u32[]{:S(2)}) collective-permute-start(bf16[32,8,512]{2,1,0:T(8,128)(2,1)S(1)} %get-tuple-element.10.refs_1_), channel_id=1, source_target_pairs={{0,192},{64,0},{128,64},{192,128},{1,193},{65,1},{129,65},{193,129... | collective-permute-start | bytes 786440 | tf_op jit(solution)/shard_map/ppermute | solution.py:184
  121.0 12.3 %collective-permute-start.6 = (bf16[32,8,512]{2,1,0:T(8,128)(2,1)S(1)}, bf16[32,8,512]{2,1,0:T(8,128)(2,1)S(1)}, u32[]{:S(2)}, u32[]{:S(2)}) collective-permute-start(bf16[32,8,512]{2,1,0:T(8,128)(2,1)S(1)} %get-tuple-element.9.refs_0_), channel_id=1, source_target_pairs={{0,192},{64,0},{128,64},{192,128},{1,193},{65,1},{129,65},{193,129... | collective-permute-start | bytes 786440 | tf_op jit(solution)/shard_map/ppermute | solution.py:186
  122.0 11.7 %collective-permute-start.5 = (bf16[32,8,512]{2,1,0:T(8,128)(2,1)S(1)}, bf16[32,8,512]{2,1,0:T(8,128)(2,1)S(1)}, u32[]{:S(2)}, u32[]{:S(2)}) collective-permute-start(bf16[32,8,512]{2,1,0:T(8,128)(2,1)S(1)} %get-tuple-element.10.refs_1_), channel_id=1, source_target_pairs={{0,64},{64,128},{128,192},{192,0},{1,65},{65,129},{129,193},{193,1... | collective-permute-start | bytes 786440 | tf_op jit(solution)/shard_map/ppermute | solution.py:185
  128.1 10.6 %copy-start.2 = (bf16[32,8,512]{2,1,0:T(8,128)(2,1)}, bf16[32,8,512]{2,1,0:T(8,128)(2,1)S(1)}, u32[]{:S(2)}) copy-start(bf16[32,8,512]{2,1,0:T(8,128)(2,1)S(1)} %collective-permute-done.4.refs_2_) | copy-start | bytes 786436
  128.1 10.6 %collective-permute-start.8 = (bf16[32,8,512]{2,1,0:T(8,128)(2,1)S(1)}, bf16[32,8,512]{2,1,0:T(8,128)(2,1)S(1)}, u32[]{:S(2)}, u32[]{:S(2)}) collective-permute-start(bf16[32,8,512]{2,1,0:T(8,128)(2,1)S(1)} %collective-permute-done.4.refs_2_), channel_id=1, source_target_pairs={{0,64},{64,128},{128,192},{192,0},{1,65},{65,129},{129,193},{193,1... | collective-permute-start | bytes 786440 | tf_op jit(solution)/shard_map/ppermute | solution.py:187
  128.1 10.6 %copy-start.3 = (bf16[32,8,512]{2,1,0:T(8,128)(2,1)}, bf16[32,8,512]{2,1,0:T(8,128)(2,1)S(1)}, u32[]{:S(2)}) copy-start(bf16[32,8,512]{2,1,0:T(8,128)(2,1)S(1)} %collective-permute-done.7.refs_5_) | copy-start | bytes 786436
  128.1 10.5 %collective-permute-start.9 = (bf16[32,8,512]{2,1,0:T(8,128)(2,1)S(1)}, bf16[32,8,512]{2,1,0:T(8,128)(2,1)S(1)}, u32[]{:S(2)}, u32[]{:S(2)}) collective-permute-start(bf16[32,8,512]{2,1,0:T(8,128)(2,1)S(1)} %collective-permute-done.7.refs_5_), channel_id=1, source_target_pairs={{0,192},{64,0},{128,64},{192,128},{1,193},{65,1},{129,65},{193,129... | collective-permute-start | bytes 786440 | tf_op jit(solution)/shard_map/ppermute | solution.py:188
  133.3 5.4 %copy-start.4 = (bf16[32,8,512]{2,1,0:T(8,128)(2,1)}, bf16[32,8,512]{2,1,0:T(8,128)(2,1)S(1)}, u32[]{:S(2)}) copy-start(bf16[32,8,512]{2,1,0:T(8,128)(2,1)S(1)} %collective-permute-done.6.refs_4_) | copy-start | bytes 786436
  133.7 5.0 %copy-start.5 = (bf16[32,8,512]{2,1,0:T(8,128)(2,1)}, bf16[32,8,512]{2,1,0:T(8,128)(2,1)S(1)}, u32[]{:S(2)}) copy-start(bf16[32,8,512]{2,1,0:T(8,128)(2,1)S(1)} %collective-permute-done.5.refs_3_) | copy-start | bytes 786436
  138.6 0.7 copy-start.6
  139.3 0.7 copy-start.7

commit v2 on v1

v2 whole, which is shorter than its diff:
```python
import functools

import jax
import jax.numpy as jnp
from jax import lax
from jax.experimental import pallas as pl
from jax.experimental.pallas import tpu as pltpu
from jax.sharding import PartitionSpec as P

BF16 = jnp.bfloat16
F32 = jnp.float32
VMEM_BYTES = 36 * 1024 * 1024


def routing_tables(owner_ids, fsdp_count, capacity):
    count = owner_ids.shape[0]
    position = jnp.arange(count, dtype=jnp.int32)
    same_owner = owner_ids[:, None] == owner_ids[None, :]
    earlier = position[None, :] < position[:, None]
    slot_rank = jnp.sum((same_owner & earlier).astype(jnp.int32), axis=1)
    slot_of = owner_ids * capacity + slot_rank
    slots = jnp.arange(fsdp_count * capacity, dtype=jnp.int32)
    holds = slot_of[None, :] == slots[:, None]
    block_of = count + jnp.sum(jnp.where(holds, position[None, :] - count, 0), axis=1)
    return block_of.astype(jnp.int32), slot_of.astype(jnp.int32)


def pick_kernel(places, table, parts, *refs):
    outs, sems = refs[:-1], refs[-1]
    copies = []
    for i, (k, h, target, row) in enumerate(places):
        copies.append(pltpu.make_async_copy(parts.at[table[k], h], outs[target].at[row], sems.at[i]))
    for copy in copies:
        copy.start()
    for copy in copies:
        copy.wait()


def relay_kernel(kept, first, out):
    out[...] = (kept[0].astype(F32) + first[1].astype(F32)).astype(BF16)


def presum_kernel(own, first_a, first_b, out):
    half = first_a.shape[1]
    for k, first in enumerate((first_a, first_b)):
        out[k * half : (k + 1) * half] = own[k].astype(F32) + first[0].astype(F32)


def pack_kernel(table, presum, second_a, second_b, out, held):
    half = second_a.shape[0]
    count = 2 * half
    for k, second in enumerate((second_a, second_b)):
        rows = slice(k * half, (k + 1) * half)
        held[rows] = presum[rows] + second[...].astype(F32)
    held[count] = jnp.zeros(held.shape[1:], F32)
    owners, capacity = out.shape[0], out.shape[1]

    def move(o, carry):
        for s in range(capacity):
            out[o, s] = held[table[o * capacity + s]].astype(BF16)
        return carry

    lax.fori_loop(0, owners, move, 0, unroll=4)


def dot(a, b, ca=1, cb=0):
    return lax.dot_general(a, b, (((ca,), (cb,)), ((), ())), preferred_element_type=F32)


def inverse_roots(matrices, identity):
    ys = [m * lax.rsqrt(jnp.sum(m * m) + 1e-06) for m in matrices]
    ybs = [y.astype(BF16) for y in ys]
    y2s = [dot(b, b) for b in ybs]
    ss = [2.25 * y - 1.5 * y2 + 0.25 * dot(y2.astype(BF16), b) for y, y2, b in zip(ys, y2s, ybs)]
    sbs = [s.astype(BF16) for s in ss]
    s2s = [dot(s, s) for s in sbs]
    qs = [
        -2.4375 * s + 1.6875 * s2 + dot(s2.astype(BF16), (0.0625 * s2 - 0.5625 * s).astype(BF16))
        for s, s2 in zip(ss, s2s)
    ]
    zs = [
        3.375 * identity + 1.5 * q - 1.125 * y - 0.5 * dot(b, q.astype(BF16)) for q, y, b in zip(qs, ys, ybs)
    ]
    return [z.astype(BF16) for z in zs]


def owner_kernel(arrived, left, right, new_left, new_right, out, held_left, held_right, sems):
    capacity, n = left.shape[0], left.shape[1]
    row = lax.broadcasted_iota(jnp.int32, (n, n), 0)
    col = lax.broadcasted_iota(jnp.int32, (n, n), 1)
    identity = (row == col).astype(F32)
    copies, grads, norms, factors = [], [], [], []
    for s in range(capacity):
        wide = arrived[:, s].astype(F32).reshape(n, n)
        grad = wide.astype(BF16)
        turned = grad.T
        new = (
            0.9 * left[s] + 0.1 * dot(grad, grad, 1, 1),
            0.9 * right[s] + 0.1 * dot(turned, turned, 1, 1),
        )
        for k, (held, target) in enumerate(((held_left, new_left), (held_right, new_right))):
            held[s] = new[k]
            copies.append(pltpu.make_async_copy(held.at[s], target.at[s], sems.at[2 * s + k]))
            copies[-1].start()
        grads.append(grad)
        norms.append(jnp.sum(wide * wide))
        factors.append(new)
    for s in range(capacity):
        root_left, root_right = inverse_roots(factors[s], identity)
        half = dot(root_left, grads[s]).astype(BF16)
        raw = dot(half, root_right)
        factor = jnp.sqrt(norms[s]) * lax.rsqrt(jnp.sum(raw * raw) + 1e-06)
        out[:, s] = (raw * factor).reshape(out.shape[0], out.shape[2], out.shape[3]).astype(BF16)
    for copy in copies:
        copy.wait()


def unpack_kernel(table, slots, out_a, out_b):
    half = out_a.shape[0]

    def move(j, carry):
        out_a[j] = slots[table[j]]
        out_b[j] = slots[table[half + j]]
        return carry

    lax.fori_loop(0, half, move, 0, unroll=4)


def place_near_kernel(table, *refs):
    parts, out = refs[:6], refs[6]
    for k in range(3):

        @pl.when(pl.program_id(0) == k)
        def _():
            out[0, 0] = parts[2 * k][...]
            out[0, 1] = parts[2 * k + 1][...]


def place_far_kernel(table, far_a, far_b, near, out):
    out[0, 0] = far_a[...]
    out[0, 1] = far_b[...]


def shards(grads, left_factors, right_factors, owners):
    reps = lax.axis_size("rep")
    fsdp = lax.axis_size("fsdp")
    r = lax.axis_index("rep").astype(jnp.int32)
    rows, width = grads.shape[2], grads.shape[3]
    capacity, order = left_factors.shape[2], left_factors.shape[3]
    per_row = grads.shape[1] // reps
    half = per_row // 2
    own_owners = lax.dynamic_index_in_dim(owners[:, :, 0], r, 0, keepdims=False)
    block_of, slot_of = routing_tables(own_owners, fsdp, capacity)

    swap1 = [(i, i ^ 1) for i in range(reps)]
    swap3 = [(i, i ^ 3) for i in range(reps)]
    parts = grads.reshape(reps, 2, half, rows, width)
    params = pltpu.CompilerParams(vmem_limit_bytes=VMEM_BYTES)
    half_shape = jax.ShapeDtypeStruct((half, rows, width), BF16)
    half_spec = pl.BlockSpec((half, rows, width), lambda i, t: (0, 0, 0))

    in_vmem = pl.BlockSpec(memory_space=pltpu.VMEM)
    in_hbm = pl.BlockSpec(memory_space=pltpu.HBM)
    ranks = jnp.stack([r ^ k for k in range(4)])

    def pick(name, *groups):
        places = [(k, h, o, i) for o, group in enumerate(groups) for i, (k, h) in enumerate(group)]
        return pl.pallas_call(
            functools.partial(pick_kernel, places),
            out_shape=[jax.ShapeDtypeStruct((len(group), half, rows, width), BF16) for group in groups],
            grid_spec=pltpu.PrefetchScalarGridSpec(
                num_scalar_prefetch=1,
                grid=(1,),
                in_specs=[in_hbm],
                out_specs=[in_vmem] * len(groups),
                scratch_shapes=[pltpu.SemaphoreType.DMA((len(places),))],
            ),
            compiler_params=params,
            name=name,
        )(ranks, parts)

    (send_a,) = pick("pick_a", [(1, 0), (2, 0)])
    (send_b,) = pick("pick_b", [(3, 1), (2, 1)])
    first_a = lax.ppermute(send_a, "rep", swap1)
    first_b = lax.ppermute(send_b, "rep", swap3)
    kept_a, kept_b, own = pick("pick_kept", [(3, 0)], [(1, 1)], [(0, 0), (0, 1)])

    def relay(kept, first):
        return pl.pallas_call(
            relay_kernel,
            in_specs=[in_vmem] * 2,
            out_specs=in_vmem,
            out_shape=half_shape,
            compiler_params=params,
            name="relay",
        )(kept, first)

    second_a = lax.ppermute(relay(kept_a, first_a), "rep", swap3)
    second_b = lax.ppermute(relay(kept_b, first_b), "rep", swap1)
    presum = pl.pallas_call(
        presum_kernel,
        in_specs=[in_vmem] * 3,
        out_specs=in_vmem,
        out_shape=jax.ShapeDtypeStruct((per_row, rows, width), F32),
        compiler_params=params,
        name="presum",
    )(own, first_a, first_b)

    outgoing = pl.pallas_call(
        pack_kernel,
        out_shape=jax.ShapeDtypeStruct((fsdp, capacity, rows, width), BF16),
        grid_spec=pltpu.PrefetchScalarGridSpec(
            num_scalar_prefetch=1,
            grid=(1,),
            in_specs=[pl.BlockSpec((per_row, rows, width), lambda i, t: (0, 0, 0)), half_spec, half_spec],
            out_specs=pl.BlockSpec((fsdp, capacity, rows, width), lambda i, t: (0, 0, 0, 0)),
            scratch_shapes=[pltpu.VMEM((per_row + 1, rows, width), F32)],
        ),
        compiler_params=params,
        name="pack",
    )(block_of, presum, second_a, second_b)

    arrived = lax.all_to_all(outgoing, "fsdp", split_axis=0, concat_axis=0, tiled=True)

    anywhere = pl.BlockSpec(memory_space=pl.ANY)
    factors = jax.ShapeDtypeStruct((capacity, order, order), F32)
    new_left, new_right, slot_update = pl.pallas_call(
        owner_kernel,
        in_specs=[in_vmem, in_vmem, in_vmem],
        out_specs=[anywhere, anywhere, in_vmem],
        out_shape=[factors, factors, jax.ShapeDtypeStruct((fsdp, capacity, rows, width), BF16)],
        scratch_shapes=[
            pltpu.VMEM((capacity, order, order), F32),
            pltpu.VMEM((capacity, order, order), F32),
            pltpu.SemaphoreType.DMA((2 * capacity,)),
        ],
        compiler_params=params,
        name="owner",
    )(arrived, left_factors[0, 0], right_factors[0, 0])

    returned = lax.all_to_all(slot_update, "fsdp", split_axis=0, concat_axis=0, tiled=True)

    mine_a, mine_b = pl.pallas_call(
        unpack_kernel,
        out_shape=[half_shape] * 2,
        grid_spec=pltpu.PrefetchScalarGridSpec(
            num_scalar_prefetch=1,
            grid=(1,),
            in_specs=[pl.BlockSpec((fsdp * capacity, rows, width), lambda i, t: (0, 0, 0))],
            out_specs=[half_spec, half_spec],
        ),
        compiler_params=params,
        name="unpack",
    )(slot_of, returned.reshape(fsdp * capacity, rows, width))

    plus = [(i, (i + 1) % reps) for i in range(reps)]
    minus = [(i, (i - 1) % reps) for i in range(reps)]
    left_a = lax.ppermute(mine_a, "rep", plus)
    right_b = lax.ppermute(mine_b, "rep", minus)
    left_b = lax.ppermute(mine_b, "rep", plus)
    right_a = lax.ppermute(mine_a, "rep", minus)
    far_a = lax.ppermute(left_a, "rep", plus)
    far_b = lax.ppermute(right_b, "rep", minus)
    update_shape = jax.ShapeDtypeStruct((reps, 2, half, rows, width), BF16)
    row_spec = pl.BlockSpec((1, 2, half, rows, width), lambda i, t: (t[i], 0, 0, 0, 0))
    near = pl.pallas_call(
        place_near_kernel,
        out_shape=update_shape,
        grid_spec=pltpu.PrefetchScalarGridSpec(
            num_scalar_prefetch=1, grid=(3,), in_specs=[half_spec] * 6, out_specs=row_spec
        ),
        compiler_params=params,
        name="place_near",
    )(jnp.stack([r, (r + 3) % reps, (r + 1) % reps]), mine_a, mine_b, left_a, left_b, right_a, right_b)
    update = pl.pallas_call(
        place_far_kernel,
        out_shape=update_shape,
        grid_spec=pltpu.PrefetchScalarGridSpec(
            num_scalar_prefetch=1, grid=(1,), in_specs=[half_spec, half_spec, anywhere], out_specs=row_spec
        ),
        input_output_aliases={3: 0},
        compiler_params=params,
        name="place_far",
    )(((r + 2) % reps)[None], far_a, far_b, near)
    return (update.reshape(reps * per_row, rows, width), new_left[None, None], new_right[None, None])


def solution(mesh):
    in_specs = (
        P("rep", None, "fsdp", None),
        P("rep", "fsdp", None, None, None),
        P("rep", "fsdp", None, None, None),
        P(),
    )
    out_specs = (
        P(None, "fsdp", None),
        P("rep", "fsdp", None, None, None),
        P("rep", "fsdp", None, None, None),
    )
    return jax.shard_map(shards, mesh=mesh, in_specs=in_specs, out_specs=out_specs, check_vma=False)
```

time: 206 us -> 136 us (0.66)
  Pallas kernels: 81.9 us -> 16.6 us
  starting transfers between devices: 15.6 us -> 13.1 us
  other arithmetic: 2.77 us -> 0.44 us
    pallas_call x3 -> x10, Pallas kernels: 79.8 us -> 15.7 us  [the longest x1 9.92 us: shards(): pl.pallas_call(owner_kernel, in_specs=[in_vmem, in_vmem, in_vmem], out_sp...]
    ppermute x4, waiting for transfers between devices: 15.9 us -> 19.1 us  [the longest x1 10.2 us: shards(): first_b = lax.ppermute(send_b, 'rep', swap3)]
    ppermute x4, starting transfers between devices: 6.95 us -> 4.47 us  [the longest x1 3.1 us: shards(): first_b = lax.ppermute(send_b, 'rep', swap3)]
    ppermute x1, waiting for transfers between devices: 4.94 us -> 2.71 us  [shards(): far_a = lax.ppermute(left_a, 'rep', plus)]
    another operation x3 -> x2, other arithmetic: 2.34 us -> 0.15 us  [the longest x1 0.08 us: shards(): ranks = jnp.stack([r ^ k for k in range(4)])]
  transfers between devices with their start and end apart: 10 -> 10, of which waited for: 8 -> 8; matrix products, arithmetic and copies ran while one was open for 1% -> 0% of each run, Pallas kernels for 0% -> 3%
where the time goes in v2:
time: 136 us; the launch traced here: 135 us
  blocking collectives  73.6 us (54%)
  waiting for transfers between devices  29.1 us (21%)
  Pallas kernels  16.6 us (12%)
  starting transfers between devices  13.1 us (10%)
  local copies, waits for them, and re-layouts  1.62 us (1%)
    all_to_all x1, blocking collectives, shards(): lax.all_to_all(outgoing, 'fsdp', split_axis=0, concat_axis=0, tiled=True)  39.3 us
    all_to_all x1, blocking collectives, shards(): lax.all_to_all(slot_update, 'fsdp', split_axis=0, concat_axis=0, tiled=True)  34.2 us
    ppermute x1, waiting for transfers between devices, shards(): first_b = lax.ppermute(send_b, 'rep', swap3)  10.2 us
    pallas_call x1, Pallas kernels, shards(): pl.pallas_call(owner_kernel, in_specs=[in_vmem, in_vmem, in_vmem], out_sp...  9.92 us
    ppermute x1, waiting for transfers between devices, shards(): left_a = lax.ppermute(mine_a, 'rep', plus)  5.08 us
    ppermute x1, waiting for transfers between devices, shards(): second_b = lax.ppermute(relay(kept_b, first_b), 'rep', swap1)  4.24 us
    ppermute x1, starting transfers between devices, shards(): far_b = lax.ppermute(right_b, 'rep', minus)  3.27 us
    ppermute x1, starting transfers between devices, shards(): right_b = lax.ppermute(mine_b, 'rep', minus)  3.22 us
  transfers between devices with their start and end apart: 10, of which 8 were waited for; matrix products, arithmetic and copies ran while one was open for 0% of the time, Pallas kernels for 3%

profile of v2, /device:TPU:32, one launch (start us, length us, event | category | flops | bytes accessed | tf_op | source)
XLA Modules:
  0.0 135.2 jit_solution(3526117161623923018)
XLA Ops:
  0.6 0.1 pad_add_fusion.table
  0.7 0.0 copy-start
  0.7 1.6 %copy-done = bf16[1,256,8,512]{3,2,1,0:T(8,128)(2,1)S(1)} copy-done((bf16[1,256,8,512]{3,2,1,0:T(8,128)(2,1)S(1)}, bf16[1,256,8,512]{3,2,1,0:T(8,128)(2,1)}, u32[]{:S(2)}) %copy-start) | copy-done | bytes 2097176
  2.3 0.6 pick_b.1
  2.9 0.0 copy-start.3
  2.9 3.1 %collective-permute-start.1 = (bf16[2,32,8,512]{3,2,1,0:T(8,128)(2,1)S(1)}, bf16[2,32,8,512]{3,2,1,0:T(8,128)(2,1)S(1)}, u32[]{:S(2)}, u32[]{:S(2)}) collective-permute-start(bf16[2,32,8,512]{3,2,1,0:T(8,128)(2,1)S(1)} %pick_b.1), channel_id=1, source_target_pairs={{0,192},{64,128},{128,64},{192,0},{1,193},{65,129},{129,65},{193,1... | collective-permute-start | bytes 1572872 | tf_op jit(solution)/shard_map/ppermute | solution.py:185
  6.0 0.6 pick_a.1
  6.6 0.2 collective-permute-start
  6.9 0.7 pick_kept.1
  7.5 0.0 copy-done.3
  7.6 0.2 convert_reduce_fusion
  7.8 10.2 %collective-permute-done.1.first_b.first = bf16[2,32,8,512]{3,2,1,0:T(8,128)(2,1)S(1)} collective-permute-done((bf16[2,32,8,512]{3,2,1,0:T(8,128)(2,1)S(1)}, bf16[2,32,8,512]{3,2,1,0:T(8,128)(2,1)S(1)}, u32[]{:S(2)}, u32[]{:S(2)}) %collective-permute-start.1) | collective-permute-done | bytes 524320 | tf_op jit(solution)/shard_map/ppermute | solution.py:185
  18.0 0.1 relay.3
  18.0 0.4 collective-permute-start.3
  18.4 2.0 %collective-permute-done.first_a.first = bf16[2,32,8,512]{3,2,1,0:T(8,128)(2,1)S(1)} collective-permute-done((bf16[2,32,8,512]{3,2,1,0:T(8,128)(2,1)S(1)}, bf16[2,32,8,512]{3,2,1,0:T(8,128)(2,1)S(1)}, u32[]{:S(2)}, u32[]{:S(2)}) %collective-permute-start) | collective-permute-done | bytes 524320 | tf_op jit(solution)/shard_map/ppermute | solution.py:184
  20.4 0.1 relay.2
  20.5 0.8 collective-permute-start.2
  21.2 0.1 select_reduce_fusion
  21.3 0.1 presum.1
  21.5 0.0 copy-start.1
  21.5 0.0 copy-start.2
  21.5 4.2 %collective-permute-done.3.second_b = bf16[32,8,512]{2,1,0:T(8,128)(2,1)S(1)} collective-permute-done((bf16[32,8,512]{2,1,0:T(8,128)(2,1)S(1)}, bf16[32,8,512]{2,1,0:T(8,128)(2,1)S(1)}, u32[]{:S(2)}, u32[]{:S(2)}) %collective-permute-start.3) | collective-permute-done | bytes 262176 | tf_op jit(solution)/shard_map/ppermute | solution.py:199
  25.7 2.6 %collective-permute-done.2.second_a = bf16[32,8,512]{2,1,0:T(8,128)(2,1)S(1)} collective-permute-done((bf16[32,8,512]{2,1,0:T(8,128)(2,1)S(1)}, bf16[32,8,512]{2,1,0:T(8,128)(2,1)S(1)}, u32[]{:S(2)}, u32[]{:S(2)}) %collective-permute-start.2) | collective-permute-done | bytes 262176 | tf_op jit(solution)/shard_map/ppermute | solution.py:198
  28.3 0.9 pack.1
  29.2 39.3 %all_to_all.10.arrived = bf16[64,2,8,512]{3,2,1,0:T(8,128)(2,1)S(1)} all-to-all(bf16[64,2,8,512]{3,2,1,0:T(8,128)(2,1)S(1)} %pack.1), channel_id=1, replica_groups=mesh['rep'=4,'fsdp'=64] {'fsdp'}, dimensions={0} | all-to-all | bytes 2097152 | tf_op jit(solution)/shard_map/all_to_all | solution.py:223
  68.5 0.0 copy-done.1
  68.5 0.0 copy-done.2
  68.6 9.9 %owner.1 = (f32[2,512,512]{2,1,0:T(8,128)}, f32[2,512,512]{2,1,0:T(8,128)}, bf16[64,2,8,512]{3,2,1,0:T(8,128)(2,1)S(1)}) custom-call(bf16[64,2,8,512]{3,2,1,0:T(8,128)(2,1)S(1)} %all_to_all.10.arrived, f32[2,512,512]{2,1,0:T(8,128)S(1)} %bitcast.22, f32[2,512,512]{2,1,0:T(8,128)S(1)} %bitcast.23), custom_call_target="tpu_custom_call" | custom-call | tf_op jit(solution)/shard_map/owner/pallas_call | solution.py:227
  78.5 34.2 %all_to_all.11 = bf16[64,2,8,512]{3,2,1,0:T(8,128)(2,1)S(1)} all-to-all(bf16[64,2,8,512]{3,2,1,0:T(8,128)(2,1)S(1)} %get-tuple-element.14), channel_id=1, replica_groups=mesh['rep'=4,'fsdp'=64] {'fsdp'}, dimensions={0} | all-to-all | bytes 2097152 | tf_op jit(solution)/shard_map/all_to_all | solution.py:241
  112.7 0.6 unpack.1
  113.4 0.1 collective-permute-start.4
  113.5 3.2 %collective-permute-start.6 = (bf16[32,8,512]{2,1,0:T(8,128)(2,1)S(1)}, bf16[32,8,512]{2,1,0:T(8,128)(2,1)S(1)}, u32[]{:S(2)}, u32[]{:S(2)}) collective-permute-start(bf16[32,8,512]{2,1,0:T(8,128)(2,1)S(1)} %get-tuple-element.16.refs_1_), channel_id=1, source_target_pairs={{0,192},{64,0},{128,64},{192,128},{1,193},{65,1},{129,65},{193,129... | collective-permute-start | bytes 786440 | tf_op jit(solution)/shard_map/ppermute | solution.py:259
  116.7 0.1 collective-permute-start.9
  116.8 1.9 %collective-permute-start.8 = (bf16[32,8,512]{2,1,0:T(8,128)(2,1)S(1)}, bf16[32,8,512]{2,1,0:T(8,128)(2,1)S(1)}, u32[]{:S(2)}, u32[]{:S(2)}) collective-permute-start(bf16[32,8,512]{2,1,0:T(8,128)(2,1)S(1)} %get-tuple-element.16.refs_1_), channel_id=1, source_target_pairs={{0,64},{64,128},{128,192},{192,0},{1,65},{65,129},{129,193},{193,1... | collective-permute-start | bytes 786440 | tf_op jit(solution)/shard_map/ppermute | solution.py:260
  118.7 5.1 %collective-permute-done.4.refs_2_ = bf16[32,8,512]{2,1,0:T(8,128)(2,1)S(1)} collective-permute-done((bf16[32,8,512]{2,1,0:T(8,128)(2,1)S(1)}, bf16[32,8,512]{2,1,0:T(8,128)(2,1)S(1)}, u32[]{:S(2)}, u32[]{:S(2)}) %collective-permute-start.4) | collective-permute-done | bytes 262176 | tf_op jit(solution)/shard_map/ppermute | solution.py:258
  123.8 0.0 collective-permute-start.5
  123.8 0.0 collective-permute-done.6.refs_5_
  123.8 3.3 %collective-permute-start.7 = (bf16[32,8,512]{2,1,0:T(8,128)(2,1)S(1)}, bf16[32,8,512]{2,1,0:T(8,128)(2,1)S(1)}, u32[]{:S(2)}, u32[]{:S(2)}) collective-permute-start(bf16[32,8,512]{2,1,0:T(8,128)(2,1)S(1)} %collective-permute-done.6.refs_5_), channel_id=1, source_target_pairs={{0,192},{64,0},{128,64},{192,128},{1,193},{65,1},{129,65},{193,129... | collective-permute-start | bytes 786440 | tf_op jit(solution)/shard_map/ppermute | solution.py:263
  127.1 0.1 pad_add_fusion.1.table
  127.2 1.8 %collective-permute-done.9.refs_4_ = bf16[32,8,512]{2,1,0:T(8,128)(2,1)S(1)} collective-permute-done((bf16[32,8,512]{2,1,0:T(8,128)(2,1)S(1)}, bf16[32,8,512]{2,1,0:T(8,128)(2,1)S(1)}, u32[]{:S(2)}, u32[]{:S(2)}) %collective-permute-start.9) | collective-permute-done | bytes 262176 | tf_op jit(solution)/shard_map/ppermute | solution.py:261
  129.0 0.4 collective-permute-done.8.refs_3_
  129.4 2.2 %place_near.1.near = bf16[4,2,32,8,512]{4,3,2,1,0:T(8,128)(2,1)} custom-call(s32[3]{0:T(128)S(1)} %pad_add_fusion.1.table, bf16[32,8,512]{2,1,0:T(8,128)(2,1)S(1)} %get-tuple-element.15.refs_0_, bf16[32,8,512]{2,1,0:T(8,128)(2,1)S(1)} %get-tuple-element.16.refs_1_, bf16[32,8,512]{2,1,0:T(8,128)(2,1)S(1)} %collective-permute-done.4.refs_2_, ...), custom_call_target="tpu_custom_call" | custom-call | tf_op jit(solution)/shard_map/place_near/pallas_call | solution.py:266
  131.6 2.7 %collective-permute-done.5.far_a = bf16[32,8,512]{2,1,0:T(8,128)(2,1)S(1)} collective-permute-done((bf16[32,8,512]{2,1,0:T(8,128)(2,1)S(1)}, bf16[32,8,512]{2,1,0:T(8,128)(2,1)S(1)}, u32[]{:S(2)}, u32[]{:S(2)}) %collective-permute-start.5) | collective-permute-done | bytes 262176 | tf_op jit(solution)/shard_map/ppermute | solution.py:262
  134.4 0.0 collective-permute-done.7.far_b
  134.4 0.8 place_far.1
  (3 shorter events, 0.0 us)
Async XLA Ops:
  0.7 1.6 %copy-start = (bf16[1,256,8,512]{3,2,1,0:T(8,128)(2,1)S(1)}, bf16[1,256,8,512]{3,2,1,0:T(8,128)(2,1)}, u32[]{:S(2)}) copy-start(bf16[1,256,8,512]{3,2,1,0:T(8,128)(2,1)} %param.4) | copy-start | bytes 6291460
  2.9 4.6 %copy-start.3 = (s32[4,64,1]{1,2,0:T(1,128)S(1)}, s32[4,64,1]{1,2,0:T(1,128)}, u32[]{:S(2)}) copy-start(s32[4,64,1]{1,2,0:T(1,128)} %param.7) | copy-start | bytes 3076
  2.9 15.0 %collective-permute-start.1 = (bf16[2,32,8,512]{3,2,1,0:T(8,128)(2,1)S(1)}, bf16[2,32,8,512]{3,2,1,0:T(8,128)(2,1)S(1)}, u32[]{:S(2)}, u32[]{:S(2)}) collective-permute-start(bf16[2,32,8,512]{3,2,1,0:T(8,128)(2,1)S(1)} %pick_b.1), channel_id=1, source_target_pairs={{0,192},{64,128},{128,64},{192,0},{1,193},{65,129},{129,65},{193,1... | collective-permute-start | bytes 1572872 | tf_op jit(solution)/shard_map/ppermute | solution.py:185
  6.6 13.8 %collective-permute-start = (bf16[2,32,8,512]{3,2,1,0:T(8,128)(2,1)S(1)}, bf16[2,32,8,512]{3,2,1,0:T(8,128)(2,1)S(1)}, u32[]{:S(2)}, u32[]{:S(2)}) collective-permute-start(bf16[2,32,8,512]{3,2,1,0:T(8,128)(2,1)S(1)} %pick_a.1), channel_id=1, source_target_pairs={{0,64},{64,0},{128,192},{192,128},{1,65},{65,1},{129,193},{193,129... | collective-permute-start | bytes 1572872 | tf_op jit(solution)/shard_map/ppermute | solution.py:184
  18.0 7.7 %collective-permute-start.3 = (bf16[32,8,512]{2,1,0:T(8,128)(2,1)S(1)}, bf16[32,8,512]{2,1,0:T(8,128)(2,1)S(1)}, u32[]{:S(2)}, u32[]{:S(2)}) collective-permute-start(bf16[32,8,512]{2,1,0:T(8,128)(2,1)S(1)} %relay.3), channel_id=1, source_target_pairs={{0,64},{64,0},{128,192},{192,128},{1,65},{65,1},{129,193},{193,129... | collective-permute-start | bytes 786440 | tf_op jit(solution)/shard_map/ppermute | solution.py:199
  20.5 7.8 %collective-permute-start.2 = (bf16[32,8,512]{2,1,0:T(8,128)(2,1)S(1)}, bf16[32,8,512]{2,1,0:T(8,128)(2,1)S(1)}, u32[]{:S(2)}, u32[]{:S(2)}) collective-permute-start(bf16[32,8,512]{2,1,0:T(8,128)(2,1)S(1)} %relay.2), channel_id=1, source_target_pairs={{0,192},{64,128},{128,64},{192,0},{1,193},{65,129},{129,65},{193,1... | collective-permute-start | bytes 786440 | tf_op jit(solution)/shard_map/ppermute | solution.py:198
  21.5 47.1 %copy-start.1 = (f32[1,1,2,512,512]{4,3,2,1,0:T(8,128)S(1)}, f32[1,1,2,512,512]{4,3,2,1,0:T(8,128)}, u32[]{:S(2)}) copy-start(f32[1,1,2,512,512]{4,3,2,1,0:T(8,128)} %param.5) | copy-start | bytes 6291460
  21.5 47.1 %copy-start.2 = (f32[1,1,2,512,512]{4,3,2,1,0:T(8,128)S(1)}, f32[1,1,2,512,512]{4,3,2,1,0:T(8,128)}, u32[]{:S(2)}) copy-start(f32[1,1,2,512,512]{4,3,2,1,0:T(8,128)} %param.6) | copy-start | bytes 6291460
  113.4 10.4 %collective-permute-start.4 = (bf16[32,8,512]{2,1,0:T(8,128)(2,1)S(1)}, bf16[32,8,512]{2,1,0:T(8,128)(2,1)S(1)}, u32[]{:S(2)}, u32[]{:S(2)}) collective-permute-start(bf16[32,8,512]{2,1,0:T(8,128)(2,1)S(1)} %get-tuple-element.15.refs_0_), channel_id=1, source_target_pairs={{0,64},{64,128},{128,192},{192,0},{1,65},{65,129},{129,193},{193,1... | collective-permute-start | bytes 786440 | tf_op jit(solution)/shard_map/ppermute | solution.py:258
  113.5 10.3 %collective-permute-start.6 = (bf16[32,8,512]{2,1,0:T(8,128)(2,1)S(1)}, bf16[32,8,512]{2,1,0:T(8,128)(2,1)S(1)}, u32[]{:S(2)}, u32[]{:S(2)}) collective-permute-start(bf16[32,8,512]{2,1,0:T(8,128)(2,1)S(1)} %get-tuple-element.16.refs_1_), channel_id=1, source_target_pairs={{0,192},{64,0},{128,64},{192,128},{1,193},{65,1},{129,65},{193,129... | collective-permute-start | bytes 786440 | tf_op jit(solution)/shard_map/ppermute | solution.py:259
  116.7 12.3 %collective-permute-start.9 = (bf16[32,8,512]{2,1,0:T(8,128)(2,1)S(1)}, bf16[32,8,512]{2,1,0:T(8,128)(2,1)S(1)}, u32[]{:S(2)}, u32[]{:S(2)}) collective-permute-start(bf16[32,8,512]{2,1,0:T(8,128)(2,1)S(1)} %get-tuple-element.15.refs_0_), channel_id=1, source_target_pairs={{0,192},{64,0},{128,64},{192,128},{1,193},{65,1},{129,65},{193,129... | collective-permute-start | bytes 786440 | tf_op jit(solution)/shard_map/ppermute | solution.py:261
  116.8 12.6 %collective-permute-start.8 = (bf16[32,8,512]{2,1,0:T(8,128)(2,1)S(1)}, bf16[32,8,512]{2,1,0:T(8,128)(2,1)S(1)}, u32[]{:S(2)}, u32[]{:S(2)}) collective-permute-start(bf16[32,8,512]{2,1,0:T(8,128)(2,1)S(1)} %get-tuple-element.16.refs_1_), channel_id=1, source_target_pairs={{0,64},{64,128},{128,192},{192,0},{1,65},{65,129},{129,193},{193,1... | collective-permute-start | bytes 786440 | tf_op jit(solution)/shard_map/ppermute | solution.py:260
  123.8 10.6 %collective-permute-start.5 = (bf16[32,8,512]{2,1,0:T(8,128)(2,1)S(1)}, bf16[32,8,512]{2,1,0:T(8,128)(2,1)S(1)}, u32[]{:S(2)}, u32[]{:S(2)}) collective-permute-start(bf16[32,8,512]{2,1,0:T(8,128)(2,1)S(1)} %collective-permute-done.4.refs_2_), channel_id=1, source_target_pairs={{0,64},{64,128},{128,192},{192,0},{1,65},{65,129},{129,193},{193,1... | collective-permute-start | bytes 786440 | tf_op jit(solution)/shard_map/ppermute | solution.py:262
  123.8 10.6 %collective-permute-start.7 = (bf16[32,8,512]{2,1,0:T(8,128)(2,1)S(1)}, bf16[32,8,512]{2,1,0:T(8,128)(2,1)S(1)}, u32[]{:S(2)}, u32[]{:S(2)}) collective-permute-start(bf16[32,8,512]{2,1,0:T(8,128)(2,1)S(1)} %collective-permute-done.6.refs_5_), channel_id=1, source_target_pairs={{0,192},{64,0},{128,64},{192,128},{1,193},{65,1},{129,65},{193,129... | collective-permute-start | bytes 786440 | tf_op jit(solution)/shard_map/ppermute | solution.py:263

commit v3 on v2

--- a/solution.py
+++ b/solution.py
@@ -36,14 +36,14 @@
         copy.wait()
 
 
-def relay_kernel(kept, first, out):
-    out[...] = (kept[0].astype(F32) + first[1].astype(F32)).astype(BF16)
-
-
-def presum_kernel(own, first_a, first_b, out):
-    half = first_a.shape[1]
-    for k, first in enumerate((first_a, first_b)):
-        out[k * half : (k + 1) * half] = own[k].astype(F32) + first[0].astype(F32)
+def relay_kernel(kept, relayed, out):
+    out[...] = (kept[0].astype(F32) + relayed[...].astype(F32)).astype(BF16)
+
+
+def presum_kernel(own, direct_a, direct_b, out):
+    half = direct_a.shape[1]
+    for k, direct in enumerate((direct_a, direct_b)):
+        out[k * half : (k + 1) * half] = own[k].astype(F32) + direct[0].astype(F32)
 
 
 def pack_kernel(table, presum, second_a, second_b, out, held):
@@ -179,13 +179,18 @@
             name=name,
         )(ranks, parts)
 
-    (send_a,) = pick("pick_a", [(1, 0), (2, 0)])
-    (send_b,) = pick("pick_b", [(3, 1), (2, 1)])
-    first_a = lax.ppermute(send_a, "rep", swap1)
-    first_b = lax.ppermute(send_b, "rep", swap3)
-    kept_a, kept_b, own = pick("pick_kept", [(3, 0)], [(1, 1)], [(0, 0), (0, 1)])
-
-    def relay(kept, first):
+    def opposite(h):
+        return lax.dynamic_slice(parts, (r ^ 2, h, 0, 0, 0), (1, 1, half, rows, width))[0, 0]
+
+    relayed_a = lax.ppermute(opposite(0), "rep", swap1)
+    relayed_b = lax.ppermute(opposite(1), "rep", swap3)
+    send_a, send_b, kept_a, kept_b, own = pick(
+        "pick", [(1, 0)], [(3, 1)], [(3, 0)], [(1, 1)], [(0, 0), (0, 1)]
+    )
+    direct_a = lax.ppermute(send_a, "rep", swap1)
+    direct_b = lax.ppermute(send_b, "rep", swap3)
+
+    def relay(kept, relayed):
         return pl.pallas_call(
             relay_kernel,
             in_specs=[in_vmem] * 2,
@@ -193,10 +198,10 @@
             out_shape=half_shape,
             compiler_params=params,
             name="relay",
-        )(kept, first)
-
-    second_a = lax.ppermute(relay(kept_a, first_a), "rep", swap3)
-    second_b = lax.ppermute(relay(kept_b, first_b), "rep", swap1)
+        )(kept, relayed)
+
+    second_a = lax.ppermute(relay(kept_a, relayed_a), "rep", swap3)
+    second_b = lax.ppermute(relay(kept_b, relayed_b), "rep", swap1)
     presum = pl.pallas_call(
         presum_kernel,
         in_specs=[in_vmem] * 3,
@@ -204,7 +209,7 @@
         out_shape=jax.ShapeDtypeStruct((per_row, rows, width), F32),
         compiler_params=params,
         name="presum",
-    )(own, first_a, first_b)
+    )(own, direct_a, direct_b)
 
     outgoing = pl.pallas_call(
         pack_kernel,

time: 136 us -> 131 us (0.963)
  waiting for transfers between devices: 29.1 us -> 23 us
  starting transfers between devices: 13.1 us -> 14.8 us
    ppermute x4 -> x6, waiting for transfers between devices: 19.1 us -> 12.9 us  [the longest x1 4.61 us: shards(): direct_a = lax.ppermute(send_a, 'rep', swap1)]
    ppermute x4 -> x6, starting transfers between devices: 4.47 us -> 6.2 us  [the longest x1 3.1 us: shards(): relayed_b = lax.ppermute(opposite(1), 'rep', swap3)]
  transfers between devices with their start and end apart: 10 -> 12, of which waited for: 8 -> 9; matrix products, arithmetic and copies ran while one was open for 0% -> 0% of each run, Pallas kernels for 3% -> 2%
where the time goes in v3:
time: 131 us
  blocking collectives  73.6 us (56%)
  waiting for transfers between devices  23 us (18%)
  Pallas kernels  15.4 us (12%)
  starting transfers between devices  14.8 us (11%)
  local copies, waits for them, and re-layouts  2.68 us (2%)
    all_to_all x1, blocking collectives, shards(): lax.all_to_all(outgoing, 'fsdp', split_axis=0, concat_axis=0, tiled=True)  39.3 us
    all_to_all x1, blocking collectives, shards(): lax.all_to_all(slot_update, 'fsdp', split_axis=0, concat_axis=0, tiled=True)  34.3 us
    pallas_call x1, Pallas kernels, shards(): pl.pallas_call(owner_kernel, in_specs=[in_vmem, in_vmem, in_vmem], out_sp...  9.91 us
    ppermute x1, waiting for transfers between devices, shards(): left_a = lax.ppermute(mine_a, 'rep', plus)  5.08 us
    ppermute x1, waiting for transfers between devices, shards(): direct_a = lax.ppermute(send_a, 'rep', swap1)  4.61 us
    ppermute x1, waiting for transfers between devices, shards(): relayed_a = lax.ppermute(opposite(0), 'rep', swap1)  4.3 us
    ppermute x1, waiting for transfers between devices, shards(): second_a = lax.ppermute(relay(kept_a, relayed_a), 'rep', swap3)  3.44 us
    ppermute x1, starting transfers between devices, shards(): far_b = lax.ppermute(right_b, 'rep', minus)  3.27 us
  transfers between devices with their start and end apart: 12, of which 9 were waited for; matrix products, arithmetic and copies ran while one was open for 0% of the time, Pallas kernels for 2%

profile of v3, /device:TPU:32, one launch (start us, length us, event | category | flops | bytes accessed | tf_op | source)
XLA Modules:
  0.0 130.7 jit_solution(17905688912697709642)
XLA Ops:
  0.6 0.0 copy-start.3
  0.7 1.1 dynamic-slice_bitcast_fusion
  1.7 3.1 %collective-permute-start.4 = (bf16[32,8,512]{2,1,0:T(8,128)(2,1)S(1)}, bf16[32,8,512]{2,1,0:T(8,128)(2,1)S(1)}, u32[]{:S(2)}, u32[]{:S(2)}) collective-permute-start(bf16[32,8,512]{2,1,0:T(8,128)(2,1)S(1)} %get-tuple-element.23), channel_id=1, source_target_pairs={{0,192},{64,128},{128,64},{192,0},{1,193},{65,129},{129,65},{193,1... | collective-permute-start | bytes 786440 | tf_op jit(solution)/shard_map/ppermute | solution.py:186
  4.8 0.1 collective-permute-start.2
  5.0 0.1 pad_add_fusion.table
  5.0 0.0 copy-start
  5.0 1.6 %copy-done = bf16[1,256,8,512]{3,2,1,0:T(8,128)(2,1)S(1)} copy-done((bf16[1,256,8,512]{3,2,1,0:T(8,128)(2,1)S(1)}, bf16[1,256,8,512]{3,2,1,0:T(8,128)(2,1)}, u32[]{:S(2)}) %copy-start) | copy-done | bytes 2097176
  6.6 0.7 pick.1
  7.4 2.0 %collective-permute-start = (bf16[1,32,8,512]{3,2,1,0:T(8,128)(2,1)S(1)}, bf16[1,32,8,512]{3,2,1,0:T(8,128)(2,1)S(1)}, u32[]{:S(2)}, u32[]{:S(2)}) collective-permute-start(bf16[1,32,8,512]{3,2,1,0:T(8,128)(2,1)S(1)} %get-tuple-element.14), channel_id=1, source_target_pairs={{0,64},{64,0},{128,192},{192,128},{1,65},{65,1},{129,193},{193,129... | collective-permute-start | bytes 786440 | tf_op jit(solution)/shard_map/ppermute | solution.py:190
  9.3 0.2 collective-permute-start.1
  9.6 0.0 copy-done.3
  9.6 0.2 convert_reduce_fusion
  9.8 4.3 %collective-permute-done.2.relayed = bf16[32,8,512]{2,1,0:T(8,128)(2,1)S(1)} collective-permute-done((bf16[32,8,512]{2,1,0:T(8,128)(2,1)S(1)}, bf16[32,8,512]{2,1,0:T(8,128)(2,1)S(1)}, u32[]{:S(2)}, u32[]{:S(2)}) %collective-permute-start.2) | collective-permute-done | bytes 262176 | tf_op jit(solution)/shard_map/ppermute | solution.py:185
  14.1 0.1 relay.2
  14.1 0.3 collective-permute-start.3
  14.4 0.0 collective-permute-done.4.relayed
  14.4 0.1 relay.3
  14.5 0.5 collective-permute-start.5
  15.0 0.1 select_reduce_fusion
  15.1 4.6 %collective-permute-done.direct_a = bf16[1,32,8,512]{3,2,1,0:T(8,128)(2,1)S(1)} collective-permute-done((bf16[1,32,8,512]{3,2,1,0:T(8,128)(2,1)S(1)}, bf16[1,32,8,512]{3,2,1,0:T(8,128)(2,1)S(1)}, u32[]{:S(2)}, u32[]{:S(2)}) %collective-permute-start) | collective-permute-done | bytes 262176 | tf_op jit(solution)/shard_map/ppermute | solution.py:190
  19.7 0.1 collective-permute-done.1.direct_b
  19.8 0.1 presum.1
  19.9 0.0 copy-start.1
  19.9 0.0 copy-start.2
  19.9 3.4 %collective-permute-done.3.second_a = bf16[32,8,512]{2,1,0:T(8,128)(2,1)S(1)} collective-permute-done((bf16[32,8,512]{2,1,0:T(8,128)(2,1)S(1)}, bf16[32,8,512]{2,1,0:T(8,128)(2,1)S(1)}, u32[]{:S(2)}, u32[]{:S(2)}) %collective-permute-start.3) | collective-permute-done | bytes 262176 | tf_op jit(solution)/shard_map/ppermute | solution.py:203
  23.4 0.5 collective-permute-done.5.second_b
  23.8 0.9 pack.1
  24.7 39.3 %all_to_all.10.arrived = bf16[64,2,8,512]{3,2,1,0:T(8,128)(2,1)S(1)} all-to-all(bf16[64,2,8,512]{3,2,1,0:T(8,128)(2,1)S(1)} %pack.1), channel_id=1, replica_groups=mesh['rep'=4,'fsdp'=64] {'fsdp'}, dimensions={0} | all-to-all | bytes 2097152 | tf_op jit(solution)/shard_map/all_to_all | solution.py:228
  64.0 0.0 copy-done.1
  64.0 0.0 copy-done.2
  64.0 9.9 %owner.1 = (f32[2,512,512]{2,1,0:T(8,128)}, f32[2,512,512]{2,1,0:T(8,128)}, bf16[64,2,8,512]{3,2,1,0:T(8,128)(2,1)S(1)}) custom-call(bf16[64,2,8,512]{3,2,1,0:T(8,128)(2,1)S(1)} %all_to_all.10.arrived, f32[2,512,512]{2,1,0:T(8,128)S(1)} %bitcast.25, f32[2,512,512]{2,1,0:T(8,128)S(1)} %bitcast.26), custom_call_target="tpu_custom_call" | custom-call | tf_op jit(solution)/shard_map/owner/pallas_call | solution.py:232
  74.0 34.3 %all_to_all.11 = bf16[64,2,8,512]{3,2,1,0:T(8,128)(2,1)S(1)} all-to-all(bf16[64,2,8,512]{3,2,1,0:T(8,128)(2,1)S(1)} %get-tuple-element.18), channel_id=1, replica_groups=mesh['rep'=4,'fsdp'=64] {'fsdp'}, dimensions={0} | all-to-all | bytes 2097152 | tf_op jit(solution)/shard_map/all_to_all | solution.py:246
  108.2 0.6 unpack.1
  108.9 0.4 collective-permute-start.6
  109.2 2.9 %collective-permute-start.8 = (bf16[32,8,512]{2,1,0:T(8,128)(2,1)S(1)}, bf16[32,8,512]{2,1,0:T(8,128)(2,1)S(1)}, u32[]{:S(2)}, u32[]{:S(2)}) collective-permute-start(bf16[32,8,512]{2,1,0:T(8,128)(2,1)S(1)} %get-tuple-element.20.refs_1_), channel_id=1, source_target_pairs={{0,192},{64,0},{128,64},{192,128},{1,193},{65,1},{129,65},{193,129... | collective-permute-start | bytes 786440 | tf_op jit(solution)/shard_map/ppermute | solution.py:264
  112.2 0.3 collective-permute-start.11
  112.5 1.7 %collective-permute-start.10 = (bf16[32,8,512]{2,1,0:T(8,128)(2,1)S(1)}, bf16[32,8,512]{2,1,0:T(8,128)(2,1)S(1)}, u32[]{:S(2)}, u32[]{:S(2)}) collective-permute-start(bf16[32,8,512]{2,1,0:T(8,128)(2,1)S(1)} %get-tuple-element.20.refs_1_), channel_id=1, source_target_pairs={{0,64},{64,128},{128,192},{192,0},{1,65},{65,129},{129,193},{193,1... | collective-permute-start | bytes 786440 | tf_op jit(solution)/shard_map/ppermute | solution.py:265
  114.2 5.1 %collective-permute-done.6.refs_2_ = bf16[32,8,512]{2,1,0:T(8,128)(2,1)S(1)} collective-permute-done((bf16[32,8,512]{2,1,0:T(8,128)(2,1)S(1)}, bf16[32,8,512]{2,1,0:T(8,128)(2,1)S(1)}, u32[]{:S(2)}, u32[]{:S(2)}) %collective-permute-start.6) | collective-permute-done | bytes 262176 | tf_op jit(solution)/shard_map/ppermute | solution.py:263
  119.3 0.0 collective-permute-start.7
  119.3 0.0 collective-permute-done.8.refs_5_
  119.3 3.3 %collective-permute-start.9 = (bf16[32,8,512]{2,1,0:T(8,128)(2,1)S(1)}, bf16[32,8,512]{2,1,0:T(8,128)(2,1)S(1)}, u32[]{:S(2)}, u32[]{:S(2)}) collective-permute-start(bf16[32,8,512]{2,1,0:T(8,128)(2,1)S(1)} %collective-permute-done.8.refs_5_), channel_id=1, source_target_pairs={{0,192},{64,0},{128,64},{192,128},{1,193},{65,1},{129,65},{193,129... | collective-permute-start | bytes 786440 | tf_op jit(solution)/shard_map/ppermute | solution.py:268
  122.6 0.1 pad_add_fusion.1.table
  122.7 1.8 %collective-permute-done.11.refs_4_ = bf16[32,8,512]{2,1,0:T(8,128)(2,1)S(1)} collective-permute-done((bf16[32,8,512]{2,1,0:T(8,128)(2,1)S(1)}, bf16[32,8,512]{2,1,0:T(8,128)(2,1)S(1)}, u32[]{:S(2)}, u32[]{:S(2)}) %collective-permute-start.11) | collective-permute-done | bytes 262176 | tf_op jit(solution)/shard_map/ppermute | solution.py:266
  124.5 0.4 collective-permute-done.10.refs_3_
  124.9 2.2 %place_near.1.near = bf16[4,2,32,8,512]{4,3,2,1,0:T(8,128)(2,1)} custom-call(s32[3]{0:T(128)S(1)} %pad_add_fusion.1.table, bf16[32,8,512]{2,1,0:T(8,128)(2,1)S(1)} %get-tuple-element.19.refs_0_, bf16[32,8,512]{2,1,0:T(8,128)(2,1)S(1)} %get-tuple-element.20.refs_1_, bf16[32,8,512]{2,1,0:T(8,128)(2,1)S(1)} %collective-permute-done.6.refs_2_, ...), custom_call_target="tpu_custom_call" | custom-call | tf_op jit(solution)/shard_map/place_near/pallas_call | solution.py:271
  127.1 2.7 %collective-permute-done.7.far_a = bf16[32,8,512]{2,1,0:T(8,128)(2,1)S(1)} collective-permute-done((bf16[32,8,512]{2,1,0:T(8,128)(2,1)S(1)}, bf16[32,8,512]{2,1,0:T(8,128)(2,1)S(1)}, u32[]{:S(2)}, u32[]{:S(2)}) %collective-permute-start.7) | collective-permute-done | bytes 262176 | tf_op jit(solution)/shard_map/ppermute | solution.py:267
  129.9 0.0 collective-permute-done.9.far_b
  129.9 0.8 place_far.1
  (3 shorter events, 0.0 us)
Async XLA Ops:
  0.6 8.9 %copy-start.3 = (s32[4,64,1]{1,2,0:T(1,128)S(1)}, s32[4,64,1]{1,2,0:T(1,128)}, u32[]{:S(2)}) copy-start(s32[4,64,1]{1,2,0:T(1,128)} %param.7) | copy-start | bytes 3076
  1.7 12.7 %collective-permute-start.4 = (bf16[32,8,512]{2,1,0:T(8,128)(2,1)S(1)}, bf16[32,8,512]{2,1,0:T(8,128)(2,1)S(1)}, u32[]{:S(2)}, u32[]{:S(2)}) collective-permute-start(bf16[32,8,512]{2,1,0:T(8,128)(2,1)S(1)} %get-tuple-element.23), channel_id=1, source_target_pairs={{0,192},{64,128},{128,64},{192,0},{1,193},{65,129},{129,65},{193,1... | collective-permute-start | bytes 786440 | tf_op jit(solution)/shard_map/ppermute | solution.py:186
  4.8 9.2 %collective-permute-start.2 = (bf16[32,8,512]{2,1,0:T(8,128)(2,1)S(1)}, bf16[32,8,512]{2,1,0:T(8,128)(2,1)S(1)}, u32[]{:S(2)}, u32[]{:S(2)}) collective-permute-start(bf16[32,8,512]{2,1,0:T(8,128)(2,1)S(1)} %get-tuple-element.24), channel_id=1, source_target_pairs={{0,64},{64,0},{128,192},{192,128},{1,65},{65,1},{129,193},{193,129... | collective-permute-start | bytes 786440 | tf_op jit(solution)/shard_map/ppermute | solution.py:185
  5.0 1.6 %copy-start = (bf16[1,256,8,512]{3,2,1,0:T(8,128)(2,1)S(1)}, bf16[1,256,8,512]{3,2,1,0:T(8,128)(2,1)}, u32[]{:S(2)}) copy-start(bf16[1,256,8,512]{3,2,1,0:T(8,128)(2,1)} %param.4) | copy-start | bytes 6291460
  7.4 12.3 %collective-permute-start = (bf16[1,32,8,512]{3,2,1,0:T(8,128)(2,1)S(1)}, bf16[1,32,8,512]{3,2,1,0:T(8,128)(2,1)S(1)}, u32[]{:S(2)}, u32[]{:S(2)}) collective-permute-start(bf16[1,32,8,512]{3,2,1,0:T(8,128)(2,1)S(1)} %get-tuple-element.14), channel_id=1, source_target_pairs={{0,64},{64,0},{128,192},{192,128},{1,65},{65,1},{129,193},{193,129... | collective-permute-start | bytes 786440 | tf_op jit(solution)/shard_map/ppermute | solution.py:190
  9.3 10.5 %collective-permute-start.1 = (bf16[1,32,8,512]{3,2,1,0:T(8,128)(2,1)S(1)}, bf16[1,32,8,512]{3,2,1,0:T(8,128)(2,1)S(1)}, u32[]{:S(2)}, u32[]{:S(2)}) collective-permute-start(bf16[1,32,8,512]{3,2,1,0:T(8,128)(2,1)S(1)} %get-tuple-element.15), channel_id=1, source_target_pairs={{0,192},{64,128},{128,64},{192,0},{1,193},{65,129},{129,65},{193,1... | collective-permute-start | bytes 786440 | tf_op jit(solution)/shard_map/ppermute | solution.py:191
  14.1 9.2 %collective-permute-start.3 = (bf16[32,8,512]{2,1,0:T(8,128)(2,1)S(1)}, bf16[32,8,512]{2,1,0:T(8,128)(2,1)S(1)}, u32[]{:S(2)}, u32[]{:S(2)}) collective-permute-start(bf16[32,8,512]{2,1,0:T(8,128)(2,1)S(1)} %relay.2), channel_id=1, source_target_pairs={{0,192},{64,128},{128,64},{192,0},{1,193},{65,129},{129,65},{193,1... | collective-permute-start | bytes 786440 | tf_op jit(solution)/shard_map/ppermute | solution.py:203
  14.5 9.3 %collective-permute-start.5 = (bf16[32,8,512]{2,1,0:T(8,128)(2,1)S(1)}, bf16[32,8,512]{2,1,0:T(8,128)(2,1)S(1)}, u32[]{:S(2)}, u32[]{:S(2)}) collective-permute-start(bf16[32,8,512]{2,1,0:T(8,128)(2,1)S(1)} %relay.3), channel_id=1, source_target_pairs={{0,64},{64,0},{128,192},{192,128},{1,65},{65,1},{129,193},{193,129... | collective-permute-start | bytes 786440 | tf_op jit(solution)/shard_map/ppermute | solution.py:204
  19.9 44.1 %copy-start.1 = (f32[1,1,2,512,512]{4,3,2,1,0:T(8,128)S(1)}, f32[1,1,2,512,512]{4,3,2,1,0:T(8,128)}, u32[]{:S(2)}) copy-start(f32[1,1,2,512,512]{4,3,2,1,0:T(8,128)} %param.5) | copy-start | bytes 6291460
  19.9 44.1 %copy-start.2 = (f32[1,1,2,512,512]{4,3,2,1,0:T(8,128)S(1)}, f32[1,1,2,512,512]{4,3,2,1,0:T(8,128)}, u32[]{:S(2)}) copy-start(f32[1,1,2,512,512]{4,3,2,1,0:T(8,128)} %param.6) | copy-start | bytes 6291460
  108.9 10.4 %collective-permute-start.6 = (bf16[32,8,512]{2,1,0:T(8,128)(2,1)S(1)}, bf16[32,8,512]{2,1,0:T(8,128)(2,1)S(1)}, u32[]{:S(2)}, u32[]{:S(2)}) collective-permute-start(bf16[32,8,512]{2,1,0:T(8,128)(2,1)S(1)} %get-tuple-element.19.refs_0_), channel_id=1, source_target_pairs={{0,64},{64,128},{128,192},{192,0},{1,65},{65,129},{129,193},{193,1... | collective-permute-start | bytes 786440 | tf_op jit(solution)/shard_map/ppermute | solution.py:263
  109.2 10.1 %collective-permute-start.8 = (bf16[32,8,512]{2,1,0:T(8,128)(2,1)S(1)}, bf16[32,8,512]{2,1,0:T(8,128)(2,1)S(1)}, u32[]{:S(2)}, u32[]{:S(2)}) collective-permute-start(bf16[32,8,512]{2,1,0:T(8,128)(2,1)S(1)} %get-tuple-element.20.refs_1_), channel_id=1, source_target_pairs={{0,192},{64,0},{128,64},{192,128},{1,193},{65,1},{129,65},{193,129... | collective-permute-start | bytes 786440 | tf_op jit(solution)/shard_map/ppermute | solution.py:264
  112.2 12.3 %collective-permute-start.11 = (bf16[32,8,512]{2,1,0:T(8,128)(2,1)S(1)}, bf16[32,8,512]{2,1,0:T(8,128)(2,1)S(1)}, u32[]{:S(2)}, u32[]{:S(2)}) collective-permute-start(bf16[32,8,512]{2,1,0:T(8,128)(2,1)S(1)} %get-tuple-element.19.refs_0_), channel_id=1, source_target_pairs={{0,192},{64,0},{128,64},{192,128},{1,193},{65,1},{129,65},{193,129... | collective-permute-start | bytes 786440 | tf_op jit(solution)/shard_map/ppermute | solution.py:266
  112.5 12.4 %collective-permute-start.10 = (bf16[32,8,512]{2,1,0:T(8,128)(2,1)S(1)}, bf16[32,8,512]{2,1,0:T(8,128)(2,1)S(1)}, u32[]{:S(2)}, u32[]{:S(2)}) collective-permute-start(bf16[32,8,512]{2,1,0:T(8,128)(2,1)S(1)} %get-tuple-element.20.refs_1_), channel_id=1, source_target_pairs={{0,64},{64,128},{128,192},{192,0},{1,65},{65,129},{129,193},{193,1... | collective-permute-start | bytes 786440 | tf_op jit(solution)/shard_map/ppermute | solution.py:265
  119.3 10.6 %collective-permute-start.7 = (bf16[32,8,512]{2,1,0:T(8,128)(2,1)S(1)}, bf16[32,8,512]{2,1,0:T(8,128)(2,1)S(1)}, u32[]{:S(2)}, u32[]{:S(2)}) collective-permute-start(bf16[32,8,512]{2,1,0:T(8,128)(2,1)S(1)} %collective-permute-done.6.refs_2_), channel_id=1, source_target_pairs={{0,64},{64,128},{128,192},{192,0},{1,65},{65,129},{129,193},{193,1... | collective-permute-start | bytes 786440 | tf_op jit(solution)/shard_map/ppermute | solution.py:267
  119.3 10.6 %collective-permute-start.9 = (bf16[32,8,512]{2,1,0:T(8,128)(2,1)S(1)}, bf16[32,8,512]{2,1,0:T(8,128)(2,1)S(1)}, u32[]{:S(2)}, u32[]{:S(2)}) collective-permute-start(bf16[32,8,512]{2,1,0:T(8,128)(2,1)S(1)} %collective-permute-done.8.refs_5_), channel_id=1, source_target_pairs={{0,192},{64,0},{128,64},{192,128},{1,193},{65,1},{129,65},{193,129... | collective-permute-start | bytes 786440 | tf_op jit(solution)/shard_map/ppermute | solution.py:268

commit v4 on v3

--- a/solution.py
+++ b/solution.py
@@ -126,19 +126,16 @@
     lax.fori_loop(0, half, move, 0, unroll=4)
 
 
-def place_near_kernel(table, *refs):
-    parts, out = refs[:6], refs[6]
-    for k in range(3):
-
-        @pl.when(pl.program_id(0) == k)
-        def _():
-            out[0, 0] = parts[2 * k][...]
-            out[0, 1] = parts[2 * k + 1][...]
-
-
-def place_far_kernel(table, far_a, far_b, near, out):
-    out[0, 0] = far_a[...]
-    out[0, 1] = far_b[...]
+def place_kernel(places, table, *refs):
+    parts, out, sems = refs[: len(places)], refs[-2], refs[-1]
+    copies = [
+        pltpu.make_async_copy(part, out.at[table[k], h], sems.at[i])
+        for i, (part, (k, h)) in enumerate(zip(parts, places))
+    ]
+    for copy in copies:
+        copy.start()
+    for copy in copies:
+        copy.wait()
 
 
 def shards(grads, left_factors, right_factors, owners):
@@ -157,7 +154,6 @@
     parts = grads.reshape(reps, 2, half, rows, width)
     params = pltpu.CompilerParams(vmem_limit_bytes=VMEM_BYTES)
     half_shape = jax.ShapeDtypeStruct((half, rows, width), BF16)
-    half_spec = pl.BlockSpec((half, rows, width), lambda i, t: (0, 0, 0))
 
     in_vmem = pl.BlockSpec(memory_space=pltpu.VMEM)
     in_hbm = pl.BlockSpec(memory_space=pltpu.HBM)
@@ -217,8 +213,8 @@
         grid_spec=pltpu.PrefetchScalarGridSpec(
             num_scalar_prefetch=1,
             grid=(1,),
-            in_specs=[pl.BlockSpec((per_row, rows, width), lambda i, t: (0, 0, 0)), half_spec, half_spec],
-            out_specs=pl.BlockSpec((fsdp, capacity, rows, width), lambda i, t: (0, 0, 0, 0)),
+            in_specs=[in_vmem] * 3,
+            out_specs=in_vmem,
             scratch_shapes=[pltpu.VMEM((per_row + 1, rows, width), F32)],
         ),
         compiler_params=params,
@@ -251,8 +247,8 @@
         grid_spec=pltpu.PrefetchScalarGridSpec(
             num_scalar_prefetch=1,
             grid=(1,),
-            in_specs=[pl.BlockSpec((fsdp * capacity, rows, width), lambda i, t: (0, 0, 0))],
-            out_specs=[half_spec, half_spec],
+            in_specs=[in_vmem],
+            out_specs=[in_vmem, in_vmem],
         ),
         compiler_params=params,
         name="unpack",
@@ -267,26 +263,28 @@
     far_a = lax.ppermute(left_a, "rep", plus)
     far_b = lax.ppermute(right_b, "rep", minus)
     update_shape = jax.ShapeDtypeStruct((reps, 2, half, rows, width), BF16)
-    row_spec = pl.BlockSpec((1, 2, half, rows, width), lambda i, t: (t[i], 0, 0, 0, 0))
-    near = pl.pallas_call(
-        place_near_kernel,
-        out_shape=update_shape,
-        grid_spec=pltpu.PrefetchScalarGridSpec(
-            num_scalar_prefetch=1, grid=(3,), in_specs=[half_spec] * 6, out_specs=row_spec
-        ),
-        compiler_params=params,
-        name="place_near",
-    )(jnp.stack([r, (r + 3) % reps, (r + 1) % reps]), mine_a, mine_b, left_a, left_b, right_a, right_b)
-    update = pl.pallas_call(
-        place_far_kernel,
-        out_shape=update_shape,
-        grid_spec=pltpu.PrefetchScalarGridSpec(
-            num_scalar_prefetch=1, grid=(1,), in_specs=[half_spec, half_spec, anywhere], out_specs=row_spec
-        ),
-        input_output_aliases={3: 0},
-        compiler_params=params,
-        name="place_far",
-    )(((r + 2) % reps)[None], far_a, far_b, near)
+    turns = jnp.stack([(r + k) % reps for k in range(4)])
+
+    def place(name, places, values, before=None):
+        held = [] if before is None else [before]
+        return pl.pallas_call(
+            functools.partial(place_kernel, places),
+            out_shape=update_shape,
+            grid_spec=pltpu.PrefetchScalarGridSpec(
+                num_scalar_prefetch=1,
+                grid=(1,),
+                in_specs=[in_vmem] * len(values) + [anywhere] * len(held),
+                out_specs=anywhere,
+                scratch_shapes=[pltpu.SemaphoreType.DMA((len(places),))],
+            ),
+            input_output_aliases={len(values) + 1: 0} if held else {},
+            compiler_params=params,
+            name=name,
+        )(turns, *values, *held)
+
+    update = place("place_first", [(0, 0), (0, 1), (3, 0), (1, 1)], [mine_a, mine_b, left_a, right_b])
+    update = place("place_second", [(3, 1), (1, 0)], [left_b, right_a], update)
+    update = place("place_far", [(2, 0), (2, 1)], [far_a, far_b], update)
     return (update.reshape(reps * per_row, rows, width), new_left[None, None], new_right[None, None])
 
 

time: 131 us -> 132 us (level)
    ppermute x1, waiting for transfers between devices: 1.85 us -> 0.3 us  [shards(): right_a = lax.ppermute(mine_a, 'rep', minus)]
    pallas_call x2 -> x3, Pallas kernels: 3.06 us -> 4.23 us  [place(): pl.pallas_call(functools.partial(place_kernel, places), out_shape=update_...]
  transfers between devices with their start and end apart: 12 -> 12, of which waited for: 9 -> 9; matrix products, arithmetic and copies ran while one was open for 0% -> 0% of each run, Pallas kernels for 2% -> 3%
where the time goes in v4:
time: 132 us; the launch traced here: 131 us
  blocking collectives  73.6 us (56%)
  waiting for transfers between devices  22.3 us (17%)
  Pallas kernels  16.6 us (13%)
  starting transfers between devices  14.8 us (11%)
  local copies, waits for them, and re-layouts  2.68 us (2%)
    all_to_all x1, blocking collectives, shards(): lax.all_to_all(outgoing, 'fsdp', split_axis=0, concat_axis=0, tiled=True)  39.3 us
    all_to_all x1, blocking collectives, shards(): lax.all_to_all(slot_update, 'fsdp', split_axis=0, concat_axis=0, tiled=True)  34.3 us
    pallas_call x1, Pallas kernels, shards(): pl.pallas_call(owner_kernel, in_specs=[in_vmem, in_vmem, in_vmem], out_sp...  9.91 us
    ppermute x1, waiting for transfers between devices, shards(): left_a = lax.ppermute(mine_a, 'rep', plus)  5.08 us
    ppermute x1, waiting for transfers between devices, shards(): direct_a = lax.ppermute(send_a, 'rep', swap1)  4.61 us
    ppermute x1, waiting for transfers between devices, shards(): relayed_a = lax.ppermute(opposite(0), 'rep', swap1)  4.3 us
    pallas_call x3, Pallas kernels, place(): pl.pallas_call(functools.partial(place_kernel, places), out_shape=update_...  4.23 us
    ppermute x1, waiting for transfers between devices, shards(): far_a = lax.ppermute(left_a, 'rep', plus)  3.59 us
  transfers between devices with their start and end apart: 12, of which 9 were waited for; matrix products, arithmetic and copies ran while one was open for 0% of the time, Pallas kernels for 3%

profile of v4, /device:TPU:32, one launch (start us, length us, event | category | flops | bytes accessed | tf_op | source)
XLA Modules:
  0.0 131.4 jit_solution(17062486242792865391)
XLA Ops:
  0.6 0.0 copy-start.3
  0.7 1.1 dynamic-slice_bitcast_fusion
  1.7 3.1 %collective-permute-start.4 = (bf16[32,8,512]{2,1,0:T(8,128)(2,1)S(1)}, bf16[32,8,512]{2,1,0:T(8,128)(2,1)S(1)}, u32[]{:S(2)}, u32[]{:S(2)}) collective-permute-start(bf16[32,8,512]{2,1,0:T(8,128)(2,1)S(1)} %get-tuple-element.23), channel_id=1, source_target_pairs={{0,192},{64,128},{128,64},{192,0},{1,193},{65,129},{129,65},{193,1... | collective-permute-start | bytes 786440 | tf_op jit(solution)/shard_map/ppermute | solution.py:182
  4.8 0.1 collective-permute-start.2
  5.0 0.1 pad_add_fusion.1.table
  5.0 1.6 %copy-done = bf16[1,256,8,512]{3,2,1,0:T(8,128)(2,1)S(1)} copy-done((bf16[1,256,8,512]{3,2,1,0:T(8,128)(2,1)S(1)}, bf16[1,256,8,512]{3,2,1,0:T(8,128)(2,1)}, u32[]{:S(2)}) %copy-start) | copy-done | bytes 2097176
  6.6 0.7 pick.1
  7.4 2.0 %collective-permute-start = (bf16[1,32,8,512]{3,2,1,0:T(8,128)(2,1)S(1)}, bf16[1,32,8,512]{3,2,1,0:T(8,128)(2,1)S(1)}, u32[]{:S(2)}, u32[]{:S(2)}) collective-permute-start(bf16[1,32,8,512]{3,2,1,0:T(8,128)(2,1)S(1)} %get-tuple-element.14), channel_id=1, source_target_pairs={{0,64},{64,0},{128,192},{192,128},{1,65},{65,1},{129,193},{193,129... | collective-permute-start | bytes 786440 | tf_op jit(solution)/shard_map/ppermute | solution.py:186
  9.3 0.2 collective-permute-start.1
  9.6 0.0 copy-done.3
  9.6 0.2 convert_reduce_fusion
  9.8 4.3 %collective-permute-done.2.relayed = bf16[32,8,512]{2,1,0:T(8,128)(2,1)S(1)} collective-permute-done((bf16[32,8,512]{2,1,0:T(8,128)(2,1)S(1)}, bf16[32,8,512]{2,1,0:T(8,128)(2,1)S(1)}, u32[]{:S(2)}, u32[]{:S(2)}) %collective-permute-start.2) | collective-permute-done | bytes 262176 | tf_op jit(solution)/shard_map/ppermute | solution.py:181
  14.1 0.1 relay.2
  14.1 0.3 collective-permute-start.3
  14.4 0.0 collective-permute-done.4.relayed
  14.4 0.1 relay.3
  14.5 0.5 collective-permute-start.5
  15.0 0.1 select_reduce_fusion
  15.1 4.6 %collective-permute-done.direct_a = bf16[1,32,8,512]{3,2,1,0:T(8,128)(2,1)S(1)} collective-permute-done((bf16[1,32,8,512]{3,2,1,0:T(8,128)(2,1)S(1)}, bf16[1,32,8,512]{3,2,1,0:T(8,128)(2,1)S(1)}, u32[]{:S(2)}, u32[]{:S(2)}) %collective-permute-start) | collective-permute-done | bytes 262176 | tf_op jit(solution)/shard_map/ppermute | solution.py:186
  19.7 0.1 collective-permute-done.1.direct_b
  19.8 0.1 presum.1
  19.9 0.0 copy-start.1
  19.9 0.0 copy-start.2
  19.9 3.4 %collective-permute-done.3.second_a = bf16[32,8,512]{2,1,0:T(8,128)(2,1)S(1)} collective-permute-done((bf16[32,8,512]{2,1,0:T(8,128)(2,1)S(1)}, bf16[32,8,512]{2,1,0:T(8,128)(2,1)S(1)}, u32[]{:S(2)}, u32[]{:S(2)}) %collective-permute-start.3) | collective-permute-done | bytes 262176 | tf_op jit(solution)/shard_map/ppermute | solution.py:199
  23.4 0.5 collective-permute-done.5.second_b
  23.8 0.9 pack.1
  24.7 39.3 %all_to_all.10.arrived = bf16[64,2,8,512]{3,2,1,0:T(8,128)(2,1)S(1)} all-to-all(bf16[64,2,8,512]{3,2,1,0:T(8,128)(2,1)S(1)} %pack.1), channel_id=1, replica_groups=mesh['rep'=4,'fsdp'=64] {'fsdp'}, dimensions={0} | all-to-all | bytes 2097152 | tf_op jit(solution)/shard_map/all_to_all | solution.py:224
  64.0 0.0 copy-done.1
  64.0 0.0 copy-done.2
  64.0 9.9 %owner.1 = (f32[2,512,512]{2,1,0:T(8,128)}, f32[2,512,512]{2,1,0:T(8,128)}, bf16[64,2,8,512]{3,2,1,0:T(8,128)(2,1)S(1)}) custom-call(bf16[64,2,8,512]{3,2,1,0:T(8,128)(2,1)S(1)} %all_to_all.10.arrived, f32[2,512,512]{2,1,0:T(8,128)S(1)} %bitcast.26, f32[2,512,512]{2,1,0:T(8,128)S(1)} %bitcast.27), custom_call_target="tpu_custom_call" | custom-call | tf_op jit(solution)/shard_map/owner/pallas_call | solution.py:228
  74.0 34.3 %all_to_all.11 = bf16[64,2,8,512]{3,2,1,0:T(8,128)(2,1)S(1)} all-to-all(bf16[64,2,8,512]{3,2,1,0:T(8,128)(2,1)S(1)} %get-tuple-element.18), channel_id=1, replica_groups=mesh['rep'=4,'fsdp'=64] {'fsdp'}, dimensions={0} | all-to-all | bytes 2097152 | tf_op jit(solution)/shard_map/all_to_all | solution.py:242
  108.2 0.6 unpack.1
  108.9 0.4 collective-permute-start.6
  109.2 2.9 %collective-permute-start.8 = (bf16[32,8,512]{2,1,0:T(8,128)(2,1)S(1)}, bf16[32,8,512]{2,1,0:T(8,128)(2,1)S(1)}, u32[]{:S(2)}, u32[]{:S(2)}) collective-permute-start(bf16[32,8,512]{2,1,0:T(8,128)(2,1)S(1)} %get-tuple-element.20.refs_1_), channel_id=1, source_target_pairs={{0,192},{64,0},{128,64},{192,128},{1,193},{65,1},{129,65},{193,129... | collective-permute-start | bytes 786440 | tf_op jit(solution)/shard_map/ppermute | solution.py:260
  112.2 0.3 collective-permute-start.11
  112.5 1.7 %collective-permute-start.10 = (bf16[32,8,512]{2,1,0:T(8,128)(2,1)S(1)}, bf16[32,8,512]{2,1,0:T(8,128)(2,1)S(1)}, u32[]{:S(2)}, u32[]{:S(2)}) collective-permute-start(bf16[32,8,512]{2,1,0:T(8,128)(2,1)S(1)} %get-tuple-element.20.refs_1_), channel_id=1, source_target_pairs={{0,64},{64,128},{128,192},{192,0},{1,65},{65,129},{129,193},{193,1... | collective-permute-start | bytes 786440 | tf_op jit(solution)/shard_map/ppermute | solution.py:261
  114.2 5.1 %collective-permute-done.6.refs_2_ = bf16[32,8,512]{2,1,0:T(8,128)(2,1)S(1)} collective-permute-done((bf16[32,8,512]{2,1,0:T(8,128)(2,1)S(1)}, bf16[32,8,512]{2,1,0:T(8,128)(2,1)S(1)}, u32[]{:S(2)}, u32[]{:S(2)}) %collective-permute-start.6) | collective-permute-done | bytes 262176 | tf_op jit(solution)/shard_map/ppermute | solution.py:259
  119.3 0.0 collective-permute-start.7
  119.3 0.0 collective-permute-done.8.refs_3_
  119.3 3.3 %collective-permute-start.9 = (bf16[32,8,512]{2,1,0:T(8,128)(2,1)S(1)}, bf16[32,8,512]{2,1,0:T(8,128)(2,1)S(1)}, u32[]{:S(2)}, u32[]{:S(2)}) collective-permute-start(bf16[32,8,512]{2,1,0:T(8,128)(2,1)S(1)} %collective-permute-done.8.refs_3_), channel_id=1, source_target_pairs={{0,192},{64,0},{128,64},{192,128},{1,193},{65,1},{129,65},{193,129... | collective-permute-start | bytes 786440 | tf_op jit(solution)/shard_map/ppermute | solution.py:264
  122.6 0.1 pad_add_fusion.table
  122.7 1.5 %place_first.1.refs_2_ = bf16[4,2,32,8,512]{4,3,2,1,0:T(8,128)(2,1)} custom-call(s32[4]{0:T(128)S(1)} %pad_add_fusion.table, bf16[32,8,512]{2,1,0:T(8,128)(2,1)S(1)} %get-tuple-element.19.refs_0_, bf16[32,8,512]{2,1,0:T(8,128)(2,1)S(1)} %get-tuple-element.20.refs_1_, bf16[32,8,512]{2,1,0:T(8,128)(2,1)S(1)} %collective-permute-done.6.refs_2_, ...), custom_call_target="tpu_custom_call" | custom-call | tf_op jit(solution)/shard_map/place_first/pallas_call | solution.py:270
  124.2 0.3 collective-permute-done.11.refs_1_
  124.5 0.4 collective-permute-done.10.refs_0_
  124.9 1.3 %place_second.1.refs_2_ = bf16[4,2,32,8,512]{4,3,2,1,0:T(8,128)(2,1)} custom-call(s32[4]{0:T(128)S(1)} %pad_add_fusion.table, bf16[32,8,512]{2,1,0:T(8,128)(2,1)S(1)} %collective-permute-done.10.refs_0_, bf16[32,8,512]{2,1,0:T(8,128)(2,1)S(1)} %collective-permute-done.11.refs_1_, ...), custom_call_target="tpu_custom_call", output_to_operand_aliasing={{}: (3, {})} | custom-call | tf_op jit(solution)/shard_map/place_second/pallas_call | solution.py:270
  126.3 3.6 %collective-permute-done.7.refs_0_ = bf16[32,8,512]{2,1,0:T(8,128)(2,1)S(1)} collective-permute-done((bf16[32,8,512]{2,1,0:T(8,128)(2,1)S(1)}, bf16[32,8,512]{2,1,0:T(8,128)(2,1)S(1)}, u32[]{:S(2)}, u32[]{:S(2)}) %collective-permute-start.7) | collective-permute-done | bytes 262176 | tf_op jit(solution)/shard_map/ppermute | solution.py:263
  129.9 0.0 collective-permute-done.9.refs_1_
  129.9 1.3 %place_far.1 = bf16[4,2,32,8,512]{4,3,2,1,0:T(8,128)(2,1)} custom-call(s32[4]{0:T(128)S(1)} %pad_add_fusion.table, bf16[32,8,512]{2,1,0:T(8,128)(2,1)S(1)} %collective-permute-done.7.refs_0_, bf16[32,8,512]{2,1,0:T(8,128)(2,1)S(1)} %collective-permute-done.9.refs_1_, bf16[4,2,32,8,512]{4,3,2,1,0:T(8,128)(2,1)} %place_second.1.refs_2_), custom_call_target="tpu_custom_call", output_to_operand_aliasing={{}: (3, {})} | custom-call | tf_op jit(solution)/shard_map/place_far/pallas_call | solution.py:270
  (4 shorter events, 0.0 us)
Async XLA Ops:
  0.6 8.9 %copy-start.3 = (s32[4,64,1]{1,2,0:T(1,128)S(1)}, s32[4,64,1]{1,2,0:T(1,128)}, u32[]{:S(2)}) copy-start(s32[4,64,1]{1,2,0:T(1,128)} %param.7) | copy-start | bytes 3076
  1.7 12.7 %collective-permute-start.4 = (bf16[32,8,512]{2,1,0:T(8,128)(2,1)S(1)}, bf16[32,8,512]{2,1,0:T(8,128)(2,1)S(1)}, u32[]{:S(2)}, u32[]{:S(2)}) collective-permute-start(bf16[32,8,512]{2,1,0:T(8,128)(2,1)S(1)} %get-tuple-element.23), channel_id=1, source_target_pairs={{0,192},{64,128},{128,64},{192,0},{1,193},{65,129},{129,65},{193,1... | collective-permute-start | bytes 786440 | tf_op jit(solution)/shard_map/ppermute | solution.py:182
  4.8 9.2 %collective-permute-start.2 = (bf16[32,8,512]{2,1,0:T(8,128)(2,1)S(1)}, bf16[32,8,512]{2,1,0:T(8,128)(2,1)S(1)}, u32[]{:S(2)}, u32[]{:S(2)}) collective-permute-start(bf16[32,8,512]{2,1,0:T(8,128)(2,1)S(1)} %get-tuple-element.24), channel_id=1, source_target_pairs={{0,64},{64,0},{128,192},{192,128},{1,65},{65,1},{129,193},{193,129... | collective-permute-start | bytes 786440 | tf_op jit(solution)/shard_map/ppermute | solution.py:181
  5.0 1.6 %copy-start = (bf16[1,256,8,512]{3,2,1,0:T(8,128)(2,1)S(1)}, bf16[1,256,8,512]{3,2,1,0:T(8,128)(2,1)}, u32[]{:S(2)}) copy-start(bf16[1,256,8,512]{3,2,1,0:T(8,128)(2,1)} %param.4) | copy-start | bytes 6291460
  7.4 12.3 %collective-permute-start = (bf16[1,32,8,512]{3,2,1,0:T(8,128)(2,1)S(1)}, bf16[1,32,8,512]{3,2,1,0:T(8,128)(2,1)S(1)}, u32[]{:S(2)}, u32[]{:S(2)}) collective-permute-start(bf16[1,32,8,512]{3,2,1,0:T(8,128)(2,1)S(1)} %get-tuple-element.14), channel_id=1, source_target_pairs={{0,64},{64,0},{128,192},{192,128},{1,65},{65,1},{129,193},{193,129... | collective-permute-start | bytes 786440 | tf_op jit(solution)/shard_map/ppermute | solution.py:186
  9.3 10.5 %collective-permute-start.1 = (bf16[1,32,8,512]{3,2,1,0:T(8,128)(2,1)S(1)}, bf16[1,32,8,512]{3,2,1,0:T(8,128)(2,1)S(1)}, u32[]{:S(2)}, u32[]{:S(2)}) collective-permute-start(bf16[1,32,8,512]{3,2,1,0:T(8,128)(2,1)S(1)} %get-tuple-element.15), channel_id=1, source_target_pairs={{0,192},{64,128},{128,64},{192,0},{1,193},{65,129},{129,65},{193,1... | collective-permute-start | bytes 786440 | tf_op jit(solution)/shard_map/ppermute | solution.py:187
  14.1 9.2 %collective-permute-start.3 = (bf16[32,8,512]{2,1,0:T(8,128)(2,1)S(1)}, bf16[32,8,512]{2,1,0:T(8,128)(2,1)S(1)}, u32[]{:S(2)}, u32[]{:S(2)}) collective-permute-start(bf16[32,8,512]{2,1,0:T(8,128)(2,1)S(1)} %relay.2), channel_id=1, source_target_pairs={{0,192},{64,128},{128,64},{192,0},{1,193},{65,129},{129,65},{193,1... | collective-permute-start | bytes 786440 | tf_op jit(solution)/shard_map/ppermute | solution.py:199
  14.5 9.3 %collective-permute-start.5 = (bf16[32,8,512]{2,1,0:T(8,128)(2,1)S(1)}, bf16[32,8,512]{2,1,0:T(8,128)(2,1)S(1)}, u32[]{:S(2)}, u32[]{:S(2)}) collective-permute-start(bf16[32,8,512]{2,1,0:T(8,128)(2,1)S(1)} %relay.3), channel_id=1, source_target_pairs={{0,64},{64,0},{128,192},{192,128},{1,65},{65,1},{129,193},{193,129... | collective-permute-start | bytes 786440 | tf_op jit(solution)/shard_map/ppermute | solution.py:200
  19.9 44.1 %copy-start.1 = (f32[1,1,2,512,512]{4,3,2,1,0:T(8,128)S(1)}, f32[1,1,2,512,512]{4,3,2,1,0:T(8,128)}, u32[]{:S(2)}) copy-start(f32[1,1,2,512,512]{4,3,2,1,0:T(8,128)} %param.5) | copy-start | bytes 6291460
  19.9 44.1 %copy-start.2 = (f32[1,1,2,512,512]{4,3,2,1,0:T(8,128)S(1)}, f32[1,1,2,512,512]{4,3,2,1,0:T(8,128)}, u32[]{:S(2)}) copy-start(f32[1,1,2,512,512]{4,3,2,1,0:T(8,128)} %param.6) | copy-start | bytes 6291460
  108.9 10.4 %collective-permute-start.6 = (bf16[32,8,512]{2,1,0:T(8,128)(2,1)S(1)}, bf16[32,8,512]{2,1,0:T(8,128)(2,1)S(1)}, u32[]{:S(2)}, u32[]{:S(2)}) collective-permute-start(bf16[32,8,512]{2,1,0:T(8,128)(2,1)S(1)} %get-tuple-element.19.refs_0_), channel_id=1, source_target_pairs={{0,64},{64,128},{128,192},{192,0},{1,65},{65,129},{129,193},{193,1... | collective-permute-start | bytes 786440 | tf_op jit(solution)/shard_map/ppermute | solution.py:259
  109.2 10.1 %collective-permute-start.8 = (bf16[32,8,512]{2,1,0:T(8,128)(2,1)S(1)}, bf16[32,8,512]{2,1,0:T(8,128)(2,1)S(1)}, u32[]{:S(2)}, u32[]{:S(2)}) collective-permute-start(bf16[32,8,512]{2,1,0:T(8,128)(2,1)S(1)} %get-tuple-element.20.refs_1_), channel_id=1, source_target_pairs={{0,192},{64,0},{128,64},{192,128},{1,193},{65,1},{129,65},{193,129... | collective-permute-start | bytes 786440 | tf_op jit(solution)/shard_map/ppermute | solution.py:260
  112.2 12.3 %collective-permute-start.11 = (bf16[32,8,512]{2,1,0:T(8,128)(2,1)S(1)}, bf16[32,8,512]{2,1,0:T(8,128)(2,1)S(1)}, u32[]{:S(2)}, u32[]{:S(2)}) collective-permute-start(bf16[32,8,512]{2,1,0:T(8,128)(2,1)S(1)} %get-tuple-element.19.refs_0_), channel_id=1, source_target_pairs={{0,192},{64,0},{128,64},{192,128},{1,193},{65,1},{129,65},{193,129... | collective-permute-start | bytes 786440 | tf_op jit(solution)/shard_map/ppermute | solution.py:262
  112.5 12.4 %collective-permute-start.10 = (bf16[32,8,512]{2,1,0:T(8,128)(2,1)S(1)}, bf16[32,8,512]{2,1,0:T(8,128)(2,1)S(1)}, u32[]{:S(2)}, u32[]{:S(2)}) collective-permute-start(bf16[32,8,512]{2,1,0:T(8,128)(2,1)S(1)} %get-tuple-element.20.refs_1_), channel_id=1, source_target_pairs={{0,64},{64,128},{128,192},{192,0},{1,65},{65,129},{129,193},{193,1... | collective-permute-start | bytes 786440 | tf_op jit(solution)/shard_map/ppermute | solution.py:261
  119.3 10.6 %collective-permute-start.7 = (bf16[32,8,512]{2,1,0:T(8,128)(2,1)S(1)}, bf16[32,8,512]{2,1,0:T(8,128)(2,1)S(1)}, u32[]{:S(2)}, u32[]{:S(2)}) collective-permute-start(bf16[32,8,512]{2,1,0:T(8,128)(2,1)S(1)} %collective-permute-done.6.refs_2_), channel_id=1, source_target_pairs={{0,64},{64,128},{128,192},{192,0},{1,65},{65,129},{129,193},{193,1... | collective-permute-start | bytes 786440 | tf_op jit(solution)/shard_map/ppermute | solution.py:263
  119.3 10.6 %collective-permute-start.9 = (bf16[32,8,512]{2,1,0:T(8,128)(2,1)S(1)}, bf16[32,8,512]{2,1,0:T(8,128)(2,1)S(1)}, u32[]{:S(2)}, u32[]{:S(2)}) collective-permute-start(bf16[32,8,512]{2,1,0:T(8,128)(2,1)S(1)} %collective-permute-done.8.refs_3_), channel_id=1, source_target_pairs={{0,192},{64,0},{128,64},{192,128},{1,193},{65,1},{129,65},{193,129... | collective-permute-start | bytes 786440 | tf_op jit(solution)/shard_map/ppermute | solution.py:264

commit v5 on v4

--- a/solution.py
+++ b/solution.py
@@ -12,17 +12,12 @@
 VMEM_BYTES = 36 * 1024 * 1024
 
 
-def routing_tables(owner_ids, fsdp_count, capacity):
-    count = owner_ids.shape[0]
-    position = jnp.arange(count, dtype=jnp.int32)
+def slots_of_blocks(owner_ids, capacity):
+    position = jnp.arange(owner_ids.shape[0], dtype=jnp.int32)
     same_owner = owner_ids[:, None] == owner_ids[None, :]
     earlier = position[None, :] < position[:, None]
     slot_rank = jnp.sum((same_owner & earlier).astype(jnp.int32), axis=1)
-    slot_of = owner_ids * capacity + slot_rank
-    slots = jnp.arange(fsdp_count * capacity, dtype=jnp.int32)
-    holds = slot_of[None, :] == slots[:, None]
-    block_of = count + jnp.sum(jnp.where(holds, position[None, :] - count, 0), axis=1)
-    return block_of.astype(jnp.int32), slot_of.astype(jnp.int32)
+    return owner_ids * capacity + slot_rank
 
 
 def pick_kernel(places, table, parts, *refs):
@@ -46,21 +41,17 @@
         out[k * half : (k + 1) * half] = own[k].astype(F32) + direct[0].astype(F32)
 
 
-def pack_kernel(table, presum, second_a, second_b, out, held):
+def pack_kernel(table, presum, second_a, second_b, out):
     half = second_a.shape[0]
-    count = 2 * half
+    out[...] = jnp.zeros(out.shape, out.dtype)
     for k, second in enumerate((second_a, second_b)):
-        rows = slice(k * half, (k + 1) * half)
-        held[rows] = presum[rows] + second[...].astype(F32)
-    held[count] = jnp.zeros(held.shape[1:], F32)
-    owners, capacity = out.shape[0], out.shape[1]
-
-    def move(o, carry):
-        for s in range(capacity):
-            out[o, s] = held[table[o * capacity + s]].astype(BF16)
-        return carry
-
-    lax.fori_loop(0, owners, move, 0, unroll=4)
+
+        def move(j, carry, k=k, second=second):
+            total = presum[k * half + j] + second[j].astype(F32)
+            out[table[k * half + j]] = total.astype(BF16)
+            return carry
+
+        lax.fori_loop(0, half, move, 0, unroll=8)
 
 
 def dot(a, b, ca=1, cb=0):
@@ -126,16 +117,13 @@
     lax.fori_loop(0, half, move, 0, unroll=4)
 
 
-def place_kernel(places, table, *refs):
-    parts, out, sems = refs[: len(places)], refs[-2], refs[-1]
-    copies = [
-        pltpu.make_async_copy(part, out.at[table[k], h], sems.at[i])
-        for i, (part, (k, h)) in enumerate(zip(parts, places))
-    ]
-    for copy in copies:
-        copy.start()
-    for copy in copies:
-        copy.wait()
+def place_kernel(count, table, *refs):
+    parts, out = refs[:count], refs[-1]
+    for k, part in enumerate(parts):
+
+        @pl.when(pl.program_id(0) == k)
+        def _():
+            out[0, 0] = part[...]
 
 
 def shards(grads, left_factors, right_factors, owners):
@@ -147,7 +135,7 @@
     per_row = grads.shape[1] // reps
     half = per_row // 2
     own_owners = lax.dynamic_index_in_dim(owners[:, :, 0], r, 0, keepdims=False)
-    block_of, slot_of = routing_tables(own_owners, fsdp, capacity)
+    slot_of = slots_of_blocks(own_owners, capacity)
 
     swap1 = [(i, i ^ 1) for i in range(reps)]
     swap3 = [(i, i ^ 3) for i in range(reps)]
@@ -209,17 +197,13 @@
 
     outgoing = pl.pallas_call(
         pack_kernel,
-        out_shape=jax.ShapeDtypeStruct((fsdp, capacity, rows, width), BF16),
+        out_shape=jax.ShapeDtypeStruct((fsdp * capacity, rows, width), BF16),
         grid_spec=pltpu.PrefetchScalarGridSpec(
-            num_scalar_prefetch=1,
-            grid=(1,),
-            in_specs=[in_vmem] * 3,
-            out_specs=in_vmem,
-            scratch_shapes=[pltpu.VMEM((per_row + 1, rows, width), F32)],
+            num_scalar_prefetch=1, grid=(1,), in_specs=[in_vmem] * 3, out_specs=in_vmem
         ),
         compiler_params=params,
         name="pack",
-    )(block_of, presum, second_a, second_b)
+    )(slot_of, presum, second_a, second_b).reshape(fsdp, capacity, rows, width)
 
     arrived = lax.all_to_all(outgoing, "fsdp", split_axis=0, concat_axis=0, tiled=True)
 
@@ -263,24 +247,24 @@
     far_a = lax.ppermute(left_a, "rep", plus)
     far_b = lax.ppermute(right_b, "rep", minus)
     update_shape = jax.ShapeDtypeStruct((reps, 2, half, rows, width), BF16)
-    turns = jnp.stack([(r + k) % reps for k in range(4)])
 
     def place(name, places, values, before=None):
         held = [] if before is None else [before]
+        count = len(values)
+        table = jnp.stack([(r + k) % reps for k, _ in places] + [jnp.int32(h) for _, h in places])
         return pl.pallas_call(
-            functools.partial(place_kernel, places),
+            functools.partial(place_kernel, count),
             out_shape=update_shape,
             grid_spec=pltpu.PrefetchScalarGridSpec(
                 num_scalar_prefetch=1,
-                grid=(1,),
-                in_specs=[in_vmem] * len(values) + [anywhere] * len(held),
-                out_specs=anywhere,
-                scratch_shapes=[pltpu.SemaphoreType.DMA((len(places),))],
+                grid=(count,),
+                in_specs=[in_vmem] * count + [anywhere] * len(held),
+                out_specs=pl.BlockSpec((1, 1, half, rows, width), lambda i, t: (t[i], t[count + i], 0, 0, 0)),
             ),
-            input_output_aliases={len(values) + 1: 0} if held else {},
+            input_output_aliases={count + 1: 0} if held else {},
             compiler_params=params,
             name=name,
-        )(turns, *values, *held)
+        )(table, *values, *held)
 
     update = place("place_first", [(0, 0), (0, 1), (3, 0), (1, 1)], [mine_a, mine_b, left_a, right_b])
     update = place("place_second", [(3, 1), (1, 0)], [left_b, right_a], update)

time: 132 us -> 131 us (level)
  waiting for transfers between devices: 22.3 us -> 18 us
  starting transfers between devices: 14.8 us -> 18.3 us
    ppermute x1, starting transfers between devices: 0.29 us -> 4.25 us  [shards(): second_a = lax.ppermute(relay(kept_a, relayed_a), 'rep', swap3)]
    ppermute x1, waiting for transfers between devices: 4.3 us -> 0.51 us  [shards(): relayed_a = lax.ppermute(opposite(0), 'rep', swap1)]
    ppermute x1, waiting for transfers between devices: 4.61 us -> 1.89 us  [shards(): direct_a = lax.ppermute(send_a, 'rep', swap1)]
    ppermute x1, waiting for transfers between devices: 0.12 us -> 2.63 us  [shards(): direct_b = lax.ppermute(send_b, 'rep', swap3)]
    ppermute x1, starting transfers between devices: 0.14 us -> 1.66 us  [shards(): relayed_a = lax.ppermute(opposite(0), 'rep', swap1)]
  transfers between devices with their start and end apart: 12 -> 12, of which waited for: 9 -> 6; matrix products, arithmetic and copies ran while one was open for 0% -> 0% of each run, Pallas kernels for 3% -> 3%
where the time goes in v5:
time: 131 us
  blocking collectives  73.6 us (56%)
  starting transfers between devices  18.3 us (14%)
  waiting for transfers between devices  18 us (14%)
  Pallas kernels  17.2 us (13%)
  local copies, waits for them, and re-layouts  2.76 us (2%)
    all_to_all x1, blocking collectives, shards(): lax.all_to_all(outgoing, 'fsdp', split_axis=0, concat_axis=0, tiled=True)  39.3 us
    all_to_all x1, blocking collectives, shards(): lax.all_to_all(slot_update, 'fsdp', split_axis=0, concat_axis=0, tiled=True)  34.2 us
    pallas_call x1, Pallas kernels, shards(): pl.pallas_call(owner_kernel, in_specs=[in_vmem, in_vmem, in_vmem], out_sp...  9.93 us
    ppermute x1, waiting for transfers between devices, shards(): left_a = lax.ppermute(mine_a, 'rep', plus)  5.08 us
    pallas_call x3, Pallas kernels, place(): pl.pallas_call(functools.partial(place_kernel, count), out_shape=update_s...  4.9 us
    ppermute x1, waiting for transfers between devices, shards(): second_a = lax.ppermute(relay(kept_a, relayed_a), 'rep', swap3)  4.28 us
    ppermute x1, starting transfers between devices, shards(): second_a = lax.ppermute(relay(kept_a, relayed_a), 'rep', swap3)  4.25 us
    ppermute x1, waiting for transfers between devices, shards(): far_a = lax.ppermute(left_a, 'rep', plus)  3.56 us
  transfers between devices with their start and end apart: 12, of which 6 were waited for; matrix products, arithmetic and copies ran while one was open for 0% of the time, Pallas kernels for 3%

profile of v5, /device:TPU:32, one launch (start us, length us, event | category | flops | bytes accessed | tf_op | source)
XLA Modules:
  0.0 130.9 jit_solution(2256831679948788667)
XLA Ops:
  0.6 0.0 copy-start.3
  0.7 1.1 dynamic-slice_bitcast_fusion
  1.7 1.7 %collective-permute-start.2 = (bf16[32,8,512]{2,1,0:T(8,128)(2,1)S(1)}, bf16[32,8,512]{2,1,0:T(8,128)(2,1)S(1)}, u32[]{:S(2)}, u32[]{:S(2)}) collective-permute-start(bf16[32,8,512]{2,1,0:T(8,128)(2,1)S(1)} %get-tuple-element.24), channel_id=1, source_target_pairs={{0,64},{64,0},{128,192},{192,128},{1,65},{65,1},{129,193},{193,129... | collective-permute-start | bytes 786440 | tf_op jit(solution)/shard_map/ppermute | solution.py:169
  3.4 2.2 %collective-permute-start.4 = (bf16[32,8,512]{2,1,0:T(8,128)(2,1)S(1)}, bf16[32,8,512]{2,1,0:T(8,128)(2,1)S(1)}, u32[]{:S(2)}, u32[]{:S(2)}) collective-permute-start(bf16[32,8,512]{2,1,0:T(8,128)(2,1)S(1)} %get-tuple-element.23), channel_id=1, source_target_pairs={{0,192},{64,128},{128,64},{192,0},{1,193},{65,129},{129,65},{193,1... | collective-permute-start | bytes 786440 | tf_op jit(solution)/shard_map/ppermute | solution.py:170
  5.6 0.1 pad_add_fusion.1.table
  5.6 1.6 %copy-done = bf16[1,256,8,512]{3,2,1,0:T(8,128)(2,1)S(1)} copy-done((bf16[1,256,8,512]{3,2,1,0:T(8,128)(2,1)S(1)}, bf16[1,256,8,512]{3,2,1,0:T(8,128)(2,1)}, u32[]{:S(2)}) %copy-start) | copy-done | bytes 2097176
  7.2 0.7 pick.1
  8.0 0.8 collective-permute-start
  8.7 0.6 collective-permute-start.1
  9.3 0.0 copy-done.3
  9.3 0.5 collective-permute-done.2.relayed
  9.9 0.1 relay.2
  9.9 4.2 %collective-permute-start.3 = (bf16[32,8,512]{2,1,0:T(8,128)(2,1)S(1)}, bf16[32,8,512]{2,1,0:T(8,128)(2,1)S(1)}, u32[]{:S(2)}, u32[]{:S(2)}) collective-permute-start(bf16[32,8,512]{2,1,0:T(8,128)(2,1)S(1)} %relay.2), channel_id=1, source_target_pairs={{0,192},{64,128},{128,64},{192,0},{1,193},{65,129},{129,65},{193,1... | collective-permute-start | bytes 786440 | tf_op jit(solution)/shard_map/ppermute | solution.py:187
  14.2 0.0 collective-permute-done.4.relayed
  14.2 0.1 relay.3
  14.2 0.2 collective-permute-start.5
  14.5 0.2 convert_reduce_fusion
  14.7 1.9 %collective-permute-done.direct_a = bf16[1,32,8,512]{3,2,1,0:T(8,128)(2,1)S(1)} collective-permute-done((bf16[1,32,8,512]{3,2,1,0:T(8,128)(2,1)S(1)}, bf16[1,32,8,512]{3,2,1,0:T(8,128)(2,1)S(1)}, u32[]{:S(2)}, u32[]{:S(2)}) %collective-permute-start) | collective-permute-done | bytes 262176 | tf_op jit(solution)/shard_map/ppermute | solution.py:174
  16.6 2.6 %collective-permute-done.1.direct_b = bf16[1,32,8,512]{3,2,1,0:T(8,128)(2,1)S(1)} collective-permute-done((bf16[1,32,8,512]{3,2,1,0:T(8,128)(2,1)S(1)}, bf16[1,32,8,512]{3,2,1,0:T(8,128)(2,1)S(1)}, u32[]{:S(2)}, u32[]{:S(2)}) %collective-permute-start.1) | collective-permute-done | bytes 262176 | tf_op jit(solution)/shard_map/ppermute | solution.py:175
  19.2 0.1 presum.1
  19.3 0.0 copy-start.1
  19.3 0.0 copy-start.2
  19.3 4.3 %collective-permute-done.3.second_a = bf16[32,8,512]{2,1,0:T(8,128)(2,1)S(1)} collective-permute-done((bf16[32,8,512]{2,1,0:T(8,128)(2,1)S(1)}, bf16[32,8,512]{2,1,0:T(8,128)(2,1)S(1)}, u32[]{:S(2)}, u32[]{:S(2)}) %collective-permute-start.3) | collective-permute-done | bytes 262176 | tf_op jit(solution)/shard_map/ppermute | solution.py:187
  23.6 0.0 collective-permute-done.5.second_b
  23.6 0.7 pack.1
  24.3 39.3 %all_to_all.10.arrived = bf16[64,2,8,512]{3,2,1,0:T(8,128)(2,1)S(1)} all-to-all(bf16[64,2,8,512]{3,2,1,0:T(8,128)(2,1)S(1)} %bitcast.25), channel_id=1, replica_groups=mesh['rep'=4,'fsdp'=64] {'fsdp'}, dimensions={0} | all-to-all | bytes 2097152 | tf_op jit(solution)/shard_map/all_to_all | solution.py:208
  63.7 0.0 copy-done.1
  63.7 0.0 copy-done.2
  63.7 9.9 %owner.1 = (f32[2,512,512]{2,1,0:T(8,128)}, f32[2,512,512]{2,1,0:T(8,128)}, bf16[64,2,8,512]{3,2,1,0:T(8,128)(2,1)S(1)}) custom-call(bf16[64,2,8,512]{3,2,1,0:T(8,128)(2,1)S(1)} %all_to_all.10.arrived, f32[2,512,512]{2,1,0:T(8,128)S(1)} %bitcast.28, f32[2,512,512]{2,1,0:T(8,128)S(1)} %bitcast.29), custom_call_target="tpu_custom_call" | custom-call | tf_op jit(solution)/shard_map/owner/pallas_call | solution.py:212
  73.6 34.2 %all_to_all.11 = bf16[64,2,8,512]{3,2,1,0:T(8,128)(2,1)S(1)} all-to-all(bf16[64,2,8,512]{3,2,1,0:T(8,128)(2,1)S(1)} %get-tuple-element.18), channel_id=1, replica_groups=mesh['rep'=4,'fsdp'=64] {'fsdp'}, dimensions={0} | all-to-all | bytes 2097152 | tf_op jit(solution)/shard_map/all_to_all | solution.py:226
  107.9 0.6 unpack.1
  108.5 0.1 collective-permute-start.6
  108.6 3.2 %collective-permute-start.8 = (bf16[32,8,512]{2,1,0:T(8,128)(2,1)S(1)}, bf16[32,8,512]{2,1,0:T(8,128)(2,1)S(1)}, u32[]{:S(2)}, u32[]{:S(2)}) collective-permute-start(bf16[32,8,512]{2,1,0:T(8,128)(2,1)S(1)} %get-tuple-element.20.refs_1_), channel_id=1, source_target_pairs={{0,192},{64,0},{128,64},{192,128},{1,193},{65,1},{129,65},{193,129... | collective-permute-start | bytes 786440 | tf_op jit(solution)/shard_map/ppermute | solution.py:244
  111.8 1.0 collective-permute-start.11
  112.8 1.1 collective-permute-start.10
  113.9 5.1 %collective-permute-done.6.refs_2_ = bf16[32,8,512]{2,1,0:T(8,128)(2,1)S(1)} collective-permute-done((bf16[32,8,512]{2,1,0:T(8,128)(2,1)S(1)}, bf16[32,8,512]{2,1,0:T(8,128)(2,1)S(1)}, u32[]{:S(2)}, u32[]{:S(2)}) %collective-permute-start.6) | collective-permute-done | bytes 262176 | tf_op jit(solution)/shard_map/ppermute | solution.py:243
  118.9 0.0 collective-permute-start.7
  118.9 0.0 collective-permute-done.8.refs_3_
  118.9 3.3 %collective-permute-start.9 = (bf16[32,8,512]{2,1,0:T(8,128)(2,1)S(1)}, bf16[32,8,512]{2,1,0:T(8,128)(2,1)S(1)}, u32[]{:S(2)}, u32[]{:S(2)}) collective-permute-start(bf16[32,8,512]{2,1,0:T(8,128)(2,1)S(1)} %collective-permute-done.8.refs_3_), channel_id=1, source_target_pairs={{0,192},{64,0},{128,64},{192,128},{1,193},{65,1},{129,65},{193,129... | collective-permute-start | bytes 786440 | tf_op jit(solution)/shard_map/ppermute | solution.py:248
  122.2 0.1 stack.51.table
  122.3 0.1 pad_add_fusion
  122.4 2.1 %place_first.1.refs_2_ = bf16[4,2,32,8,512]{4,3,2,1,0:T(8,128)(2,1)} custom-call(s32[8]{0:T(128)S(1)} %stack.51.table, bf16[32,8,512]{2,1,0:T(8,128)(2,1)S(1)} %get-tuple-element.19.refs_0_, bf16[32,8,512]{2,1,0:T(8,128)(2,1)S(1)} %get-tuple-element.20.refs_1_, bf16[32,8,512]{2,1,0:T(8,128)(2,1)S(1)} %collective-permute-done.6.refs_2_, ...), custom_call_target="tpu_custom_call" | custom-call | tf_op jit(solution)/shard_map/place_first/pallas_call | solution.py:255
  124.5 0.0 collective-permute-done.11.refs_1_
  124.5 0.0 collective-permute-done.10.refs_0_
  124.6 1.4 %place_second.1.refs_2_ = bf16[4,2,32,8,512]{4,3,2,1,0:T(8,128)(2,1)} custom-call(s32[4]{0:T(128)S(1)} %get-tuple-element.26.table, bf16[32,8,512]{2,1,0:T(8,128)(2,1)S(1)} %collective-permute-done.10.refs_0_, bf16[32,8,512]{2,1,0:T(8,128)(2,1)S(1)} %collective-permute-done.11.refs_1_, ...), custom_call_target="tpu_custom_call", output_to_operand_aliasing={{}: (3, {})} | custom-call | tf_op jit(solution)/shard_map/place_second/pallas_call | solution.py:255
  125.9 3.6 %collective-permute-done.7.refs_0_ = bf16[32,8,512]{2,1,0:T(8,128)(2,1)S(1)} collective-permute-done((bf16[32,8,512]{2,1,0:T(8,128)(2,1)S(1)}, bf16[32,8,512]{2,1,0:T(8,128)(2,1)S(1)}, u32[]{:S(2)}, u32[]{:S(2)}) %collective-permute-start.7) | collective-permute-done | bytes 262176 | tf_op jit(solution)/shard_map/ppermute | solution.py:247
  129.5 0.0 collective-permute-done.9.refs_1_
  129.5 1.4 %place_far.1 = bf16[4,2,32,8,512]{4,3,2,1,0:T(8,128)(2,1)} custom-call(s32[4]{0:T(128)S(1)} %get-tuple-element.25.table, bf16[32,8,512]{2,1,0:T(8,128)(2,1)S(1)} %collective-permute-done.7.refs_0_, bf16[32,8,512]{2,1,0:T(8,128)(2,1)S(1)} %collective-permute-done.9.refs_1_, ...), custom_call_target="tpu_custom_call", output_to_operand_aliasing={{}: (3, {})} | custom-call | tf_op jit(solution)/shard_map/place_far/pallas_call | solution.py:255
  (3 shorter events, 0.0 us)
Async XLA Ops:
  0.6 8.7 %copy-start.3 = (s32[4,64,1]{1,2,0:T(1,128)S(1)}, s32[4,64,1]{1,2,0:T(1,128)}, u32[]{:S(2)}) copy-start(s32[4,64,1]{1,2,0:T(1,128)} %param.7) | copy-start | bytes 3076
  1.7 8.1 %collective-permute-start.2 = (bf16[32,8,512]{2,1,0:T(8,128)(2,1)S(1)}, bf16[32,8,512]{2,1,0:T(8,128)(2,1)S(1)}, u32[]{:S(2)}, u32[]{:S(2)}) collective-permute-start(bf16[32,8,512]{2,1,0:T(8,128)(2,1)S(1)} %get-tuple-element.24), channel_id=1, source_target_pairs={{0,64},{64,0},{128,192},{192,128},{1,65},{65,1},{129,193},{193,129... | collective-permute-start | bytes 786440 | tf_op jit(solution)/shard_map/ppermute | solution.py:169
  3.4 10.8 %collective-permute-start.4 = (bf16[32,8,512]{2,1,0:T(8,128)(2,1)S(1)}, bf16[32,8,512]{2,1,0:T(8,128)(2,1)S(1)}, u32[]{:S(2)}, u32[]{:S(2)}) collective-permute-start(bf16[32,8,512]{2,1,0:T(8,128)(2,1)S(1)} %get-tuple-element.23), channel_id=1, source_target_pairs={{0,192},{64,128},{128,64},{192,0},{1,193},{65,129},{129,65},{193,1... | collective-permute-start | bytes 786440 | tf_op jit(solution)/shard_map/ppermute | solution.py:170
  5.6 1.6 %copy-start = (bf16[1,256,8,512]{3,2,1,0:T(8,128)(2,1)S(1)}, bf16[1,256,8,512]{3,2,1,0:T(8,128)(2,1)}, u32[]{:S(2)}) copy-start(bf16[1,256,8,512]{3,2,1,0:T(8,128)(2,1)} %param.4) | copy-start | bytes 6291460
  8.0 8.6 %collective-permute-start = (bf16[1,32,8,512]{3,2,1,0:T(8,128)(2,1)S(1)}, bf16[1,32,8,512]{3,2,1,0:T(8,128)(2,1)S(1)}, u32[]{:S(2)}, u32[]{:S(2)}) collective-permute-start(bf16[1,32,8,512]{3,2,1,0:T(8,128)(2,1)S(1)} %get-tuple-element.14), channel_id=1, source_target_pairs={{0,64},{64,0},{128,192},{192,128},{1,65},{65,1},{129,193},{193,129... | collective-permute-start | bytes 786440 | tf_op jit(solution)/shard_map/ppermute | solution.py:174
  8.7 10.5 %collective-permute-start.1 = (bf16[1,32,8,512]{3,2,1,0:T(8,128)(2,1)S(1)}, bf16[1,32,8,512]{3,2,1,0:T(8,128)(2,1)S(1)}, u32[]{:S(2)}, u32[]{:S(2)}) collective-permute-start(bf16[1,32,8,512]{3,2,1,0:T(8,128)(2,1)S(1)} %get-tuple-element.15), channel_id=1, source_target_pairs={{0,192},{64,128},{128,64},{192,0},{1,193},{65,129},{129,65},{193,1... | collective-permute-start | bytes 786440 | tf_op jit(solution)/shard_map/ppermute | solution.py:175
  9.9 13.7 %collective-permute-start.3 = (bf16[32,8,512]{2,1,0:T(8,128)(2,1)S(1)}, bf16[32,8,512]{2,1,0:T(8,128)(2,1)S(1)}, u32[]{:S(2)}, u32[]{:S(2)}) collective-permute-start(bf16[32,8,512]{2,1,0:T(8,128)(2,1)S(1)} %relay.2), channel_id=1, source_target_pairs={{0,192},{64,128},{128,64},{192,0},{1,193},{65,129},{129,65},{193,1... | collective-permute-start | bytes 786440 | tf_op jit(solution)/shard_map/ppermute | solution.py:187
  14.2 9.4 %collective-permute-start.5 = (bf16[32,8,512]{2,1,0:T(8,128)(2,1)S(1)}, bf16[32,8,512]{2,1,0:T(8,128)(2,1)S(1)}, u32[]{:S(2)}, u32[]{:S(2)}) collective-permute-start(bf16[32,8,512]{2,1,0:T(8,128)(2,1)S(1)} %relay.3), channel_id=1, source_target_pairs={{0,64},{64,0},{128,192},{192,128},{1,65},{65,1},{129,193},{193,129... | collective-permute-start | bytes 786440 | tf_op jit(solution)/shard_map/ppermute | solution.py:188
  19.3 44.4 %copy-start.1 = (f32[1,1,2,512,512]{4,3,2,1,0:T(8,128)S(1)}, f32[1,1,2,512,512]{4,3,2,1,0:T(8,128)}, u32[]{:S(2)}) copy-start(f32[1,1,2,512,512]{4,3,2,1,0:T(8,128)} %param.5) | copy-start | bytes 6291460
  19.3 44.4 %copy-start.2 = (f32[1,1,2,512,512]{4,3,2,1,0:T(8,128)S(1)}, f32[1,1,2,512,512]{4,3,2,1,0:T(8,128)}, u32[]{:S(2)}) copy-start(f32[1,1,2,512,512]{4,3,2,1,0:T(8,128)} %param.6) | copy-start | bytes 6291460
  108.5 10.4 %collective-permute-start.6 = (bf16[32,8,512]{2,1,0:T(8,128)(2,1)S(1)}, bf16[32,8,512]{2,1,0:T(8,128)(2,1)S(1)}, u32[]{:S(2)}, u32[]{:S(2)}) collective-permute-start(bf16[32,8,512]{2,1,0:T(8,128)(2,1)S(1)} %get-tuple-element.19.refs_0_), channel_id=1, source_target_pairs={{0,64},{64,128},{128,192},{192,0},{1,65},{65,129},{129,193},{193,1... | collective-permute-start | bytes 786440 | tf_op jit(solution)/shard_map/ppermute | solution.py:243
  108.6 10.3 %collective-permute-start.8 = (bf16[32,8,512]{2,1,0:T(8,128)(2,1)S(1)}, bf16[32,8,512]{2,1,0:T(8,128)(2,1)S(1)}, u32[]{:S(2)}, u32[]{:S(2)}) collective-permute-start(bf16[32,8,512]{2,1,0:T(8,128)(2,1)S(1)} %get-tuple-element.20.refs_1_), channel_id=1, source_target_pairs={{0,192},{64,0},{128,64},{192,128},{1,193},{65,1},{129,65},{193,129... | collective-permute-start | bytes 786440 | tf_op jit(solution)/shard_map/ppermute | solution.py:244
  111.8 12.7 %collective-permute-start.11 = (bf16[32,8,512]{2,1,0:T(8,128)(2,1)S(1)}, bf16[32,8,512]{2,1,0:T(8,128)(2,1)S(1)}, u32[]{:S(2)}, u32[]{:S(2)}) collective-permute-start(bf16[32,8,512]{2,1,0:T(8,128)(2,1)S(1)} %get-tuple-element.19.refs_0_), channel_id=1, source_target_pairs={{0,192},{64,0},{128,64},{192,128},{1,193},{65,1},{129,65},{193,129... | collective-permute-start | bytes 786440 | tf_op jit(solution)/shard_map/ppermute | solution.py:246
  112.8 11.8 %collective-permute-start.10 = (bf16[32,8,512]{2,1,0:T(8,128)(2,1)S(1)}, bf16[32,8,512]{2,1,0:T(8,128)(2,1)S(1)}, u32[]{:S(2)}, u32[]{:S(2)}) collective-permute-start(bf16[32,8,512]{2,1,0:T(8,128)(2,1)S(1)} %get-tuple-element.20.refs_1_), channel_id=1, source_target_pairs={{0,64},{64,128},{128,192},{192,0},{1,65},{65,129},{129,193},{193,1... | collective-permute-start | bytes 786440 | tf_op jit(solution)/shard_map/ppermute | solution.py:245
  118.9 10.6 %collective-permute-start.7 = (bf16[32,8,512]{2,1,0:T(8,128)(2,1)S(1)}, bf16[32,8,512]{2,1,0:T(8,128)(2,1)S(1)}, u32[]{:S(2)}, u32[]{:S(2)}) collective-permute-start(bf16[32,8,512]{2,1,0:T(8,128)(2,1)S(1)} %collective-permute-done.6.refs_2_), channel_id=1, source_target_pairs={{0,64},{64,128},{128,192},{192,0},{1,65},{65,129},{129,193},{193,1... | collective-permute-start | bytes 786440 | tf_op jit(solution)/shard_map/ppermute | solution.py:247
  118.9 10.6 %collective-permute-start.9 = (bf16[32,8,512]{2,1,0:T(8,128)(2,1)S(1)}, bf16[32,8,512]{2,1,0:T(8,128)(2,1)S(1)}, u32[]{:S(2)}, u32[]{:S(2)}) collective-permute-start(bf16[32,8,512]{2,1,0:T(8,128)(2,1)S(1)} %collective-permute-done.8.refs_3_), channel_id=1, source_target_pairs={{0,192},{64,0},{128,64},{192,128},{1,193},{65,1},{129,65},{193,129... | collective-permute-start | bytes 786440 | tf_op jit(solution)/shard_map/ppermute | solution.py:248

commit v6 on v5

--- a/solution.py
+++ b/solution.py
@@ -117,13 +117,14 @@
     lax.fori_loop(0, half, move, 0, unroll=4)
 
 
-def place_kernel(count, table, *refs):
-    parts, out = refs[:count], refs[-1]
-    for k, part in enumerate(parts):
+def place_kernel(steps, table, *refs):
+    out = refs[-1]
+    for k, step in enumerate(steps):
 
         @pl.when(pl.program_id(0) == k)
         def _():
-            out[0, 0] = part[...]
+            for i, part in enumerate(step):
+                out[0, i] = refs[part][...]
 
 
 def shards(grads, left_factors, right_factors, owners):
@@ -248,27 +249,32 @@
     far_b = lax.ppermute(right_b, "rep", minus)
     update_shape = jax.ShapeDtypeStruct((reps, 2, half, rows, width), BF16)
 
-    def place(name, places, values, before=None):
+    def place(name, places, steps, values, before=None):
         held = [] if before is None else [before]
-        count = len(values)
         table = jnp.stack([(r + k) % reps for k, _ in places] + [jnp.int32(h) for _, h in places])
+        count, size = len(steps), len(steps[0])
         return pl.pallas_call(
-            functools.partial(place_kernel, count),
+            functools.partial(place_kernel, steps),
             out_shape=update_shape,
             grid_spec=pltpu.PrefetchScalarGridSpec(
                 num_scalar_prefetch=1,
                 grid=(count,),
-                in_specs=[in_vmem] * count + [anywhere] * len(held),
-                out_specs=pl.BlockSpec((1, 1, half, rows, width), lambda i, t: (t[i], t[count + i], 0, 0, 0)),
+                in_specs=[in_vmem] * len(values) + [anywhere] * len(held),
+                out_specs=pl.BlockSpec(
+                    (1, size, half, rows, width), lambda i, t: (t[i], t[count + i], 0, 0, 0)
+                ),
             ),
-            input_output_aliases={count + 1: 0} if held else {},
+            input_output_aliases={len(values) + 1: 0} if held else {},
             compiler_params=params,
             name=name,
         )(table, *values, *held)
 
-    update = place("place_first", [(0, 0), (0, 1), (3, 0), (1, 1)], [mine_a, mine_b, left_a, right_b])
-    update = place("place_second", [(3, 1), (1, 0)], [left_b, right_a], update)
-    update = place("place_far", [(2, 0), (2, 1)], [far_a, far_b], update)
+    singles = [(0,), (1,), (2,), (3,)]
+    update = place(
+        "place_first", [(0, 0), (0, 1), (3, 0), (1, 1)], singles, [mine_a, mine_b, left_a, right_b]
+    )
+    update = place("place_second", [(3, 1), (1, 0)], singles[:2], [left_b, right_a], update)
+    update = place("place_far", [(2, 0)], [(0, 1)], [far_a, far_b], update)
     return (update.reshape(reps * per_row, rows, width), new_left[None, None], new_right[None, None])
 
 

time: 131 us -> 131 us (level)
  no operation moved by 1% of the time
where the time goes in v6:
time: 131 us
  blocking collectives  73.6 us (56%)
  starting transfers between devices  18.3 us (14%)
  waiting for transfers between devices  17.9 us (14%)
  Pallas kernels  17.1 us (13%)
  local copies, waits for them, and re-layouts  2.76 us (2%)
    all_to_all x1, blocking collectives, shards(): lax.all_to_all(outgoing, 'fsdp', split_axis=0, concat_axis=0, tiled=True)  39.3 us
    all_to_all x1, blocking collectives, shards(): lax.all_to_all(slot_update, 'fsdp', split_axis=0, concat_axis=0, tiled=True)  34.2 us
    pallas_call x1, Pallas kernels, shards(): pl.pallas_call(owner_kernel, in_specs=[in_vmem, in_vmem, in_vmem], out_sp...  9.93 us
    ppermute x1, waiting for transfers between devices, shards(): left_a = lax.ppermute(mine_a, 'rep', plus)  5.08 us
    pallas_call x3, Pallas kernels, place(): pl.pallas_call(functools.partial(place_kernel, steps), out_shape=update_s...  4.88 us
    ppermute x1, waiting for transfers between devices, shards(): second_a = lax.ppermute(relay(kept_a, relayed_a), 'rep', swap3)  4.28 us
    ppermute x1, starting transfers between devices, shards(): second_a = lax.ppermute(relay(kept_a, relayed_a), 'rep', swap3)  4.25 us
    ppermute x1, waiting for transfers between devices, shards(): far_a = lax.ppermute(left_a, 'rep', plus)  3.52 us
  transfers between devices with their start and end apart: 12, of which 6 were waited for; matrix products, arithmetic and copies ran while one was open for 0% of the time, Pallas kernels for 3%

profile of v6, /device:TPU:32, one launch (start us, length us, event | category | flops | bytes accessed | tf_op | source)
XLA Modules:
  0.0 130.9 jit_solution(14965518172500114065)
XLA Ops:
  0.6 0.0 copy-start.3
  0.7 1.1 dynamic-slice_bitcast_fusion
  1.7 1.7 %collective-permute-start.2 = (bf16[32,8,512]{2,1,0:T(8,128)(2,1)S(1)}, bf16[32,8,512]{2,1,0:T(8,128)(2,1)S(1)}, u32[]{:S(2)}, u32[]{:S(2)}) collective-permute-start(bf16[32,8,512]{2,1,0:T(8,128)(2,1)S(1)} %get-tuple-element.24), channel_id=1, source_target_pairs={{0,64},{64,0},{128,192},{192,128},{1,65},{65,1},{129,193},{193,129... | collective-permute-start | bytes 786440 | tf_op jit(solution)/shard_map/ppermute | solution.py:170
  3.4 2.2 %collective-permute-start.4 = (bf16[32,8,512]{2,1,0:T(8,128)(2,1)S(1)}, bf16[32,8,512]{2,1,0:T(8,128)(2,1)S(1)}, u32[]{:S(2)}, u32[]{:S(2)}) collective-permute-start(bf16[32,8,512]{2,1,0:T(8,128)(2,1)S(1)} %get-tuple-element.23), channel_id=1, source_target_pairs={{0,192},{64,128},{128,64},{192,0},{1,193},{65,129},{129,65},{193,1... | collective-permute-start | bytes 786440 | tf_op jit(solution)/shard_map/ppermute | solution.py:171
  5.6 0.1 pad_add_fusion.1.table
  5.6 1.6 %copy-done = bf16[1,256,8,512]{3,2,1,0:T(8,128)(2,1)S(1)} copy-done((bf16[1,256,8,512]{3,2,1,0:T(8,128)(2,1)S(1)}, bf16[1,256,8,512]{3,2,1,0:T(8,128)(2,1)}, u32[]{:S(2)}) %copy-start) | copy-done | bytes 2097176
  7.2 0.7 pick.1
  8.0 0.8 collective-permute-start
  8.7 0.6 collective-permute-start.1
  9.3 0.0 copy-done.3
  9.3 0.5 collective-permute-done.2.relayed
  9.9 0.1 relay.2
  9.9 4.2 %collective-permute-start.3 = (bf16[32,8,512]{2,1,0:T(8,128)(2,1)S(1)}, bf16[32,8,512]{2,1,0:T(8,128)(2,1)S(1)}, u32[]{:S(2)}, u32[]{:S(2)}) collective-permute-start(bf16[32,8,512]{2,1,0:T(8,128)(2,1)S(1)} %relay.2), channel_id=1, source_target_pairs={{0,192},{64,128},{128,64},{192,0},{1,193},{65,129},{129,65},{193,1... | collective-permute-start | bytes 786440 | tf_op jit(solution)/shard_map/ppermute | solution.py:188
  14.2 0.0 collective-permute-done.4.relayed
  14.2 0.1 relay.3
  14.2 0.2 collective-permute-start.5
  14.5 0.2 convert_reduce_fusion
  14.7 1.9 %collective-permute-done.direct_a = bf16[1,32,8,512]{3,2,1,0:T(8,128)(2,1)S(1)} collective-permute-done((bf16[1,32,8,512]{3,2,1,0:T(8,128)(2,1)S(1)}, bf16[1,32,8,512]{3,2,1,0:T(8,128)(2,1)S(1)}, u32[]{:S(2)}, u32[]{:S(2)}) %collective-permute-start) | collective-permute-done | bytes 262176 | tf_op jit(solution)/shard_map/ppermute | solution.py:175
  16.6 2.6 %collective-permute-done.1.direct_b = bf16[1,32,8,512]{3,2,1,0:T(8,128)(2,1)S(1)} collective-permute-done((bf16[1,32,8,512]{3,2,1,0:T(8,128)(2,1)S(1)}, bf16[1,32,8,512]{3,2,1,0:T(8,128)(2,1)S(1)}, u32[]{:S(2)}, u32[]{:S(2)}) %collective-permute-start.1) | collective-permute-done | bytes 262176 | tf_op jit(solution)/shard_map/ppermute | solution.py:176
  19.2 0.1 presum.1
  19.3 0.0 copy-start.1
  19.3 0.0 copy-start.2
  19.3 4.3 %collective-permute-done.3.second_a = bf16[32,8,512]{2,1,0:T(8,128)(2,1)S(1)} collective-permute-done((bf16[32,8,512]{2,1,0:T(8,128)(2,1)S(1)}, bf16[32,8,512]{2,1,0:T(8,128)(2,1)S(1)}, u32[]{:S(2)}, u32[]{:S(2)}) %collective-permute-start.3) | collective-permute-done | bytes 262176 | tf_op jit(solution)/shard_map/ppermute | solution.py:188
  23.6 0.0 collective-permute-done.5.second_b
  23.6 0.7 pack.1
  24.3 39.3 %all_to_all.10.arrived = bf16[64,2,8,512]{3,2,1,0:T(8,128)(2,1)S(1)} all-to-all(bf16[64,2,8,512]{3,2,1,0:T(8,128)(2,1)S(1)} %bitcast.25), channel_id=1, replica_groups=mesh['rep'=4,'fsdp'=64] {'fsdp'}, dimensions={0} | all-to-all | bytes 2097152 | tf_op jit(solution)/shard_map/all_to_all | solution.py:209
  63.7 0.0 copy-done.2
  63.7 9.9 %owner.1 = (f32[2,512,512]{2,1,0:T(8,128)}, f32[2,512,512]{2,1,0:T(8,128)}, bf16[64,2,8,512]{3,2,1,0:T(8,128)(2,1)S(1)}) custom-call(bf16[64,2,8,512]{3,2,1,0:T(8,128)(2,1)S(1)} %all_to_all.10.arrived, f32[2,512,512]{2,1,0:T(8,128)S(1)} %bitcast.28, f32[2,512,512]{2,1,0:T(8,128)S(1)} %bitcast.29), custom_call_target="tpu_custom_call" | custom-call | tf_op jit(solution)/shard_map/owner/pallas_call | solution.py:213
  73.6 34.2 %all_to_all.11 = bf16[64,2,8,512]{3,2,1,0:T(8,128)(2,1)S(1)} all-to-all(bf16[64,2,8,512]{3,2,1,0:T(8,128)(2,1)S(1)} %get-tuple-element.18), channel_id=1, replica_groups=mesh['rep'=4,'fsdp'=64] {'fsdp'}, dimensions={0} | all-to-all | bytes 2097152 | tf_op jit(solution)/shard_map/all_to_all | solution.py:227
  107.9 0.6 unpack.1
  108.5 0.1 collective-permute-start.6
  108.6 3.2 %collective-permute-start.8 = (bf16[32,8,512]{2,1,0:T(8,128)(2,1)S(1)}, bf16[32,8,512]{2,1,0:T(8,128)(2,1)S(1)}, u32[]{:S(2)}, u32[]{:S(2)}) collective-permute-start(bf16[32,8,512]{2,1,0:T(8,128)(2,1)S(1)} %get-tuple-element.20.refs_1_), channel_id=1, source_target_pairs={{0,192},{64,0},{128,64},{192,128},{1,193},{65,1},{129,65},{193,129... | collective-permute-start | bytes 786440 | tf_op jit(solution)/shard_map/ppermute | solution.py:245
  111.8 1.0 collective-permute-start.11
  112.8 1.1 collective-permute-start.10
  113.9 5.1 %collective-permute-done.6.refs_2_ = bf16[32,8,512]{2,1,0:T(8,128)(2,1)S(1)} collective-permute-done((bf16[32,8,512]{2,1,0:T(8,128)(2,1)S(1)}, bf16[32,8,512]{2,1,0:T(8,128)(2,1)S(1)}, u32[]{:S(2)}, u32[]{:S(2)}) %collective-permute-start.6) | collective-permute-done | bytes 262176 | tf_op jit(solution)/shard_map/ppermute | solution.py:244
  118.9 0.0 collective-permute-start.7
  118.9 0.0 collective-permute-done.8.refs_3_
  118.9 3.3 %collective-permute-start.9 = (bf16[32,8,512]{2,1,0:T(8,128)(2,1)S(1)}, bf16[32,8,512]{2,1,0:T(8,128)(2,1)S(1)}, u32[]{:S(2)}, u32[]{:S(2)}) collective-permute-start(bf16[32,8,512]{2,1,0:T(8,128)(2,1)S(1)} %collective-permute-done.8.refs_3_), channel_id=1, source_target_pairs={{0,192},{64,0},{128,64},{192,128},{1,193},{65,1},{129,65},{193,129... | collective-permute-start | bytes 786440 | tf_op jit(solution)/shard_map/ppermute | solution.py:249
  122.2 0.1 stack.50.table
  122.3 0.1 pad_add_fusion.2.table
  122.4 0.1 pad_add_fusion.table
  122.5 2.1 %place_first.1.refs_2_ = bf16[4,2,32,8,512]{4,3,2,1,0:T(8,128)(2,1)} custom-call(s32[8]{0:T(128)S(1)} %stack.50.table, bf16[32,8,512]{2,1,0:T(8,128)(2,1)S(1)} %get-tuple-element.19.refs_0_, bf16[32,8,512]{2,1,0:T(8,128)(2,1)S(1)} %get-tuple-element.20.refs_1_, bf16[32,8,512]{2,1,0:T(8,128)(2,1)S(1)} %collective-permute-done.6.refs_2_, ...), custom_call_target="tpu_custom_call" | custom-call | tf_op jit(solution)/shard_map/place_first/pallas_call | solution.py:256
  124.6 0.0 collective-permute-done.11.refs_1_
  124.6 0.0 collective-permute-done.10.refs_0_
  124.6 1.4 %place_second.1.refs_2_ = bf16[4,2,32,8,512]{4,3,2,1,0:T(8,128)(2,1)} custom-call(s32[4]{0:T(128)S(1)} %pad_add_fusion.2.table, bf16[32,8,512]{2,1,0:T(8,128)(2,1)S(1)} %collective-permute-done.10.refs_0_, bf16[32,8,512]{2,1,0:T(8,128)(2,1)S(1)} %collective-permute-done.11.refs_1_, ...), custom_call_target="tpu_custom_call", output_to_operand_aliasing={{}: (3, {})} | custom-call | tf_op jit(solution)/shard_map/place_second/pallas_call | solution.py:256
  126.0 3.5 %collective-permute-done.7.refs_0_ = bf16[32,8,512]{2,1,0:T(8,128)(2,1)S(1)} collective-permute-done((bf16[32,8,512]{2,1,0:T(8,128)(2,1)S(1)}, bf16[32,8,512]{2,1,0:T(8,128)(2,1)S(1)}, u32[]{:S(2)}, u32[]{:S(2)}) %collective-permute-start.7) | collective-permute-done | bytes 262176 | tf_op jit(solution)/shard_map/ppermute | solution.py:248
  129.5 0.0 collective-permute-done.9.refs_1_
  129.5 1.4 %place_far.1 = bf16[4,2,32,8,512]{4,3,2,1,0:T(8,128)(2,1)} custom-call(s32[2]{0:T(128)S(1)} %pad_add_fusion.table, bf16[32,8,512]{2,1,0:T(8,128)(2,1)S(1)} %collective-permute-done.7.refs_0_, bf16[32,8,512]{2,1,0:T(8,128)(2,1)S(1)} %collective-permute-done.9.refs_1_, bf16[4,2,32,8,512]{4,3,2,1,0:T(8,128)(2,1)} %place_second.1.refs_2_), custom_call_target="tpu_custom_call", output_to_operand_aliasing={{}: (3, {})} | custom-call | tf_op jit(solution)/shard_map/place_far/pallas_call | solution.py:256
  (4 shorter events, 0.0 us)
Async XLA Ops:
  0.6 8.7 %copy-start.3 = (s32[4,64,1]{1,2,0:T(1,128)S(1)}, s32[4,64,1]{1,2,0:T(1,128)}, u32[]{:S(2)}) copy-start(s32[4,64,1]{1,2,0:T(1,128)} %param.7) | copy-start | bytes 3076
  1.7 8.1 %collective-permute-start.2 = (bf16[32,8,512]{2,1,0:T(8,128)(2,1)S(1)}, bf16[32,8,512]{2,1,0:T(8,128)(2,1)S(1)}, u32[]{:S(2)}, u32[]{:S(2)}) collective-permute-start(bf16[32,8,512]{2,1,0:T(8,128)(2,1)S(1)} %get-tuple-element.24), channel_id=1, source_target_pairs={{0,64},{64,0},{128,192},{192,128},{1,65},{65,1},{129,193},{193,129... | collective-permute-start | bytes 786440 | tf_op jit(solution)/shard_map/ppermute | solution.py:170
  3.4 10.8 %collective-permute-start.4 = (bf16[32,8,512]{2,1,0:T(8,128)(2,1)S(1)}, bf16[32,8,512]{2,1,0:T(8,128)(2,1)S(1)}, u32[]{:S(2)}, u32[]{:S(2)}) collective-permute-start(bf16[32,8,512]{2,1,0:T(8,128)(2,1)S(1)} %get-tuple-element.23), channel_id=1, source_target_pairs={{0,192},{64,128},{128,64},{192,0},{1,193},{65,129},{129,65},{193,1... | collective-permute-start | bytes 786440 | tf_op jit(solution)/shard_map/ppermute | solution.py:171
  5.6 1.6 %copy-start = (bf16[1,256,8,512]{3,2,1,0:T(8,128)(2,1)S(1)}, bf16[1,256,8,512]{3,2,1,0:T(8,128)(2,1)}, u32[]{:S(2)}) copy-start(bf16[1,256,8,512]{3,2,1,0:T(8,128)(2,1)} %param.4) | copy-start | bytes 6291460
  8.0 8.6 %collective-permute-start = (bf16[1,32,8,512]{3,2,1,0:T(8,128)(2,1)S(1)}, bf16[1,32,8,512]{3,2,1,0:T(8,128)(2,1)S(1)}, u32[]{:S(2)}, u32[]{:S(2)}) collective-permute-start(bf16[1,32,8,512]{3,2,1,0:T(8,128)(2,1)S(1)} %get-tuple-element.14), channel_id=1, source_target_pairs={{0,64},{64,0},{128,192},{192,128},{1,65},{65,1},{129,193},{193,129... | collective-permute-start | bytes 786440 | tf_op jit(solution)/shard_map/ppermute | solution.py:175
  8.7 10.5 %collective-permute-start.1 = (bf16[1,32,8,512]{3,2,1,0:T(8,128)(2,1)S(1)}, bf16[1,32,8,512]{3,2,1,0:T(8,128)(2,1)S(1)}, u32[]{:S(2)}, u32[]{:S(2)}) collective-permute-start(bf16[1,32,8,512]{3,2,1,0:T(8,128)(2,1)S(1)} %get-tuple-element.15), channel_id=1, source_target_pairs={{0,192},{64,128},{128,64},{192,0},{1,193},{65,129},{129,65},{193,1... | collective-permute-start | bytes 786440 | tf_op jit(solution)/shard_map/ppermute | solution.py:176
  9.9 13.7 %collective-permute-start.3 = (bf16[32,8,512]{2,1,0:T(8,128)(2,1)S(1)}, bf16[32,8,512]{2,1,0:T(8,128)(2,1)S(1)}, u32[]{:S(2)}, u32[]{:S(2)}) collective-permute-start(bf16[32,8,512]{2,1,0:T(8,128)(2,1)S(1)} %relay.2), channel_id=1, source_target_pairs={{0,192},{64,128},{128,64},{192,0},{1,193},{65,129},{129,65},{193,1... | collective-permute-start | bytes 786440 | tf_op jit(solution)/shard_map/ppermute | solution.py:188
  14.2 9.4 %collective-permute-start.5 = (bf16[32,8,512]{2,1,0:T(8,128)(2,1)S(1)}, bf16[32,8,512]{2,1,0:T(8,128)(2,1)S(1)}, u32[]{:S(2)}, u32[]{:S(2)}) collective-permute-start(bf16[32,8,512]{2,1,0:T(8,128)(2,1)S(1)} %relay.3), channel_id=1, source_target_pairs={{0,64},{64,0},{128,192},{192,128},{1,65},{65,1},{129,193},{193,129... | collective-permute-start | bytes 786440 | tf_op jit(solution)/shard_map/ppermute | solution.py:189
  19.3 44.4 %copy-start.1 = (f32[1,1,2,512,512]{4,3,2,1,0:T(8,128)S(1)}, f32[1,1,2,512,512]{4,3,2,1,0:T(8,128)}, u32[]{:S(2)}) copy-start(f32[1,1,2,512,512]{4,3,2,1,0:T(8,128)} %param.5) | copy-start | bytes 6291460
  19.3 44.4 %copy-start.2 = (f32[1,1,2,512,512]{4,3,2,1,0:T(8,128)S(1)}, f32[1,1,2,512,512]{4,3,2,1,0:T(8,128)}, u32[]{:S(2)}) copy-start(f32[1,1,2,512,512]{4,3,2,1,0:T(8,128)} %param.6) | copy-start | bytes 6291460
  108.5 10.4 %collective-permute-start.6 = (bf16[32,8,512]{2,1,0:T(8,128)(2,1)S(1)}, bf16[32,8,512]{2,1,0:T(8,128)(2,1)S(1)}, u32[]{:S(2)}, u32[]{:S(2)}) collective-permute-start(bf16[32,8,512]{2,1,0:T(8,128)(2,1)S(1)} %get-tuple-element.19.refs_0_), channel_id=1, source_target_pairs={{0,64},{64,128},{128,192},{192,0},{1,65},{65,129},{129,193},{193,1... | collective-permute-start | bytes 786440 | tf_op jit(solution)/shard_map/ppermute | solution.py:244
  108.6 10.3 %collective-permute-start.8 = (bf16[32,8,512]{2,1,0:T(8,128)(2,1)S(1)}, bf16[32,8,512]{2,1,0:T(8,128)(2,1)S(1)}, u32[]{:S(2)}, u32[]{:S(2)}) collective-permute-start(bf16[32,8,512]{2,1,0:T(8,128)(2,1)S(1)} %get-tuple-element.20.refs_1_), channel_id=1, source_target_pairs={{0,192},{64,0},{128,64},{192,128},{1,193},{65,1},{129,65},{193,129... | collective-permute-start | bytes 786440 | tf_op jit(solution)/shard_map/ppermute | solution.py:245
  111.8 12.8 %collective-permute-start.11 = (bf16[32,8,512]{2,1,0:T(8,128)(2,1)S(1)}, bf16[32,8,512]{2,1,0:T(8,128)(2,1)S(1)}, u32[]{:S(2)}, u32[]{:S(2)}) collective-permute-start(bf16[32,8,512]{2,1,0:T(8,128)(2,1)S(1)} %get-tuple-element.19.refs_0_), channel_id=1, source_target_pairs={{0,192},{64,0},{128,64},{192,128},{1,193},{65,1},{129,65},{193,129... | collective-permute-start | bytes 786440 | tf_op jit(solution)/shard_map/ppermute | solution.py:247
  112.8 11.8 %collective-permute-start.10 = (bf16[32,8,512]{2,1,0:T(8,128)(2,1)S(1)}, bf16[32,8,512]{2,1,0:T(8,128)(2,1)S(1)}, u32[]{:S(2)}, u32[]{:S(2)}) collective-permute-start(bf16[32,8,512]{2,1,0:T(8,128)(2,1)S(1)} %get-tuple-element.20.refs_1_), channel_id=1, source_target_pairs={{0,64},{64,128},{128,192},{192,0},{1,65},{65,129},{129,193},{193,1... | collective-permute-start | bytes 786440 | tf_op jit(solution)/shard_map/ppermute | solution.py:246
  118.9 10.6 %collective-permute-start.7 = (bf16[32,8,512]{2,1,0:T(8,128)(2,1)S(1)}, bf16[32,8,512]{2,1,0:T(8,128)(2,1)S(1)}, u32[]{:S(2)}, u32[]{:S(2)}) collective-permute-start(bf16[32,8,512]{2,1,0:T(8,128)(2,1)S(1)} %collective-permute-done.6.refs_2_), channel_id=1, source_target_pairs={{0,64},{64,128},{128,192},{192,0},{1,65},{65,129},{129,193},{193,1... | collective-permute-start | bytes 786440 | tf_op jit(solution)/shard_map/ppermute | solution.py:248
  118.9 10.6 %collective-permute-start.9 = (bf16[32,8,512]{2,1,0:T(8,128)(2,1)S(1)}, bf16[32,8,512]{2,1,0:T(8,128)(2,1)S(1)}, u32[]{:S(2)}, u32[]{:S(2)}) collective-permute-start(bf16[32,8,512]{2,1,0:T(8,128)(2,1)S(1)} %collective-permute-done.8.refs_3_), channel_id=1, source_target_pairs={{0,192},{64,0},{128,64},{192,128},{1,193},{65,1},{129,65},{193,129... | collective-permute-start | bytes 786440 | tf_op jit(solution)/shard_map/ppermute | solution.py:249

commit v7 on v6

--- a/solution.py
+++ b/solution.py
@@ -24,7 +24,7 @@
     outs, sems = refs[:-1], refs[-1]
     copies = []
     for i, (k, h, target, row) in enumerate(places):
-        copies.append(pltpu.make_async_copy(parts.at[table[k], h], outs[target].at[row], sems.at[i]))
+        copies.append(pltpu.make_async_copy(parts.at[table[0] ^ k, h], outs[target].at[row], sems.at[i]))
     for copy in copies:
         copy.start()
     for copy in copies:
@@ -146,7 +146,6 @@
 
     in_vmem = pl.BlockSpec(memory_space=pltpu.VMEM)
     in_hbm = pl.BlockSpec(memory_space=pltpu.HBM)
-    ranks = jnp.stack([r ^ k for k in range(4)])
 
     def pick(name, *groups):
         places = [(k, h, o, i) for o, group in enumerate(groups) for i, (k, h) in enumerate(group)]
@@ -162,7 +161,7 @@
             ),
             compiler_params=params,
             name=name,
-        )(ranks, parts)
+        )(r[None], parts)
 
     def opposite(h):
         return lax.dynamic_slice(parts, (r ^ 2, h, 0, 0, 0), (1, 1, half, rows, width))[0, 0]
@@ -249,32 +248,34 @@
     far_b = lax.ppermute(right_b, "rep", minus)
     update_shape = jax.ShapeDtypeStruct((reps, 2, half, rows, width), BF16)
 
-    def place(name, places, steps, values, before=None):
+    def place(name, turns, halves, steps, values, before=None):
         held = [] if before is None else [before]
-        table = jnp.stack([(r + k) % reps for k, _ in places] + [jnp.int32(h) for _, h in places])
-        count, size = len(steps), len(steps[0])
+        size = len(steps[0])
+
+        def where(i, t):
+            turn, first = turns[-1], halves[-1]
+            for k in range(len(steps) - 1):
+                turn, first = jnp.where(i == k, turns[k], turn), jnp.where(i == k, halves[k], first)
+            return lax.rem(t[0] + turn, reps), first, 0, 0, 0
+
         return pl.pallas_call(
             functools.partial(place_kernel, steps),
             out_shape=update_shape,
             grid_spec=pltpu.PrefetchScalarGridSpec(
                 num_scalar_prefetch=1,
-                grid=(count,),
+                grid=(len(steps),),
                 in_specs=[in_vmem] * len(values) + [anywhere] * len(held),
-                out_specs=pl.BlockSpec(
-                    (1, size, half, rows, width), lambda i, t: (t[i], t[count + i], 0, 0, 0)
-                ),
+                out_specs=pl.BlockSpec((1, size, half, rows, width), where),
             ),
             input_output_aliases={len(values) + 1: 0} if held else {},
             compiler_params=params,
             name=name,
-        )(table, *values, *held)
+        )(r[None], *values, *held)
 
     singles = [(0,), (1,), (2,), (3,)]
-    update = place(
-        "place_first", [(0, 0), (0, 1), (3, 0), (1, 1)], singles, [mine_a, mine_b, left_a, right_b]
-    )
-    update = place("place_second", [(3, 1), (1, 0)], singles[:2], [left_b, right_a], update)
-    update = place("place_far", [(2, 0)], [(0, 1)], [far_a, far_b], update)
+    update = place("place_first", [0, 0, 3, 1], [0, 1, 0, 1], singles, [mine_a, mine_b, left_a, right_b])
+    update = place("place_second", [3, 1], [1, 0], singles[:2], [left_b, right_a], update)
+    update = place("place_far", [2], [0], [(0, 1)], [far_a, far_b], update)
     return (update.reshape(reps * per_row, rows, width), new_left[None, None], new_right[None, None])
 
 

time: 131 us -> 131 us (level)
  waiting for transfers between devices: 17.9 us -> 20.4 us
  Pallas kernels: 17.1 us -> 14.9 us
    pallas_call x3, Pallas kernels: 4.88 us -> 3.2 us  [place(): pl.pallas_call(functools.partial(place_kernel, steps), out_shape=update_s...]
  transfers between devices with their start and end apart: 12 -> 12, of which waited for: 6 -> 8; matrix products, arithmetic and copies ran while one was open for 0% -> 0% of each run, Pallas kernels for 3% -> 2%
where the time goes in v7:
time: 131 us; the launch traced here: 130 us
  blocking collectives  73.6 us (56%)
  waiting for transfers between devices  20.4 us (16%)
  starting transfers between devices  17.8 us (14%)
  Pallas kernels  14.9 us (11%)
  local copies, waits for them, and re-layouts  2.68 us (2%)
    all_to_all x1, blocking collectives, shards(): lax.all_to_all(outgoing, 'fsdp', split_axis=0, concat_axis=0, tiled=True)  39.3 us
    all_to_all x1, blocking collectives, shards(): lax.all_to_all(slot_update, 'fsdp', split_axis=0, concat_axis=0, tiled=True)  34.2 us
    pallas_call x1, Pallas kernels, shards(): pl.pallas_call(owner_kernel, in_specs=[in_vmem, in_vmem, in_vmem], out_sp...  9.92 us
    ppermute x1, waiting for transfers between devices, shards(): left_a = lax.ppermute(mine_a, 'rep', plus)  5.08 us
    ppermute x1, waiting for transfers between devices, shards(): far_a = lax.ppermute(left_a, 'rep', plus)  4.13 us
    ppermute x1, waiting for transfers between devices, shards(): second_a = lax.ppermute(relay(kept_a, relayed_a), 'rep', swap3)  4.09 us
    ppermute x1, starting transfers between devices, shards(): second_a = lax.ppermute(relay(kept_a, relayed_a), 'rep', swap3)  3.75 us
    ppermute x1, starting transfers between devices, shards(): far_b = lax.ppermute(right_b, 'rep', minus)  3.27 us
  transfers between devices with their start and end apart: 12, of which 8 were waited for; matrix products, arithmetic and copies ran while one was open for 0% of the time, Pallas kernels for 2%

profile of v7, /device:TPU:32, one launch (start us, length us, event | category | flops | bytes accessed | tf_op | source)
XLA Modules:
  0.0 130.3 jit_solution(1935202425299363599)
XLA Ops:
  0.6 0.0 copy-start.3
  0.6 1.1 dynamic-slice_bitcast_fusion
  1.7 1.7 %collective-permute-start.2 = (bf16[32,8,512]{2,1,0:T(8,128)(2,1)S(1)}, bf16[32,8,512]{2,1,0:T(8,128)(2,1)S(1)}, u32[]{:S(2)}, u32[]{:S(2)}) collective-permute-start(bf16[32,8,512]{2,1,0:T(8,128)(2,1)S(1)} %get-tuple-element.24), channel_id=1, source_target_pairs={{0,64},{64,0},{128,192},{192,128},{1,65},{65,1},{129,193},{193,129... | collective-permute-start | bytes 786440 | tf_op jit(solution)/shard_map/ppermute | solution.py:169
  3.4 2.2 %collective-permute-start.4 = (bf16[32,8,512]{2,1,0:T(8,128)(2,1)S(1)}, bf16[32,8,512]{2,1,0:T(8,128)(2,1)S(1)}, u32[]{:S(2)}, u32[]{:S(2)}) collective-permute-start(bf16[32,8,512]{2,1,0:T(8,128)(2,1)S(1)} %get-tuple-element.23), channel_id=1, source_target_pairs={{0,192},{64,128},{128,64},{192,0},{1,193},{65,129},{129,65},{193,1... | collective-permute-start | bytes 786440 | tf_op jit(solution)/shard_map/ppermute | solution.py:170
  5.6 0.0 copy-start
  5.6 1.6 %copy-done = bf16[1,256,8,512]{3,2,1,0:T(8,128)(2,1)S(1)} copy-done((bf16[1,256,8,512]{3,2,1,0:T(8,128)(2,1)S(1)}, bf16[1,256,8,512]{3,2,1,0:T(8,128)(2,1)}, u32[]{:S(2)}) %copy-start) | copy-done | bytes 2097176
  7.2 0.2 pick.1
  7.3 0.8 collective-permute-start
  8.1 0.6 collective-permute-start.1
  8.7 0.0 copy-done.3
  8.7 1.6 %collective-permute-done.2.relayed = bf16[32,8,512]{2,1,0:T(8,128)(2,1)S(1)} collective-permute-done((bf16[32,8,512]{2,1,0:T(8,128)(2,1)S(1)}, bf16[32,8,512]{2,1,0:T(8,128)(2,1)S(1)}, u32[]{:S(2)}, u32[]{:S(2)}) %collective-permute-start.2) | collective-permute-done | bytes 262176 | tf_op jit(solution)/shard_map/ppermute | solution.py:169
  10.3 0.1 relay.2
  10.4 3.8 %collective-permute-start.3 = (bf16[32,8,512]{2,1,0:T(8,128)(2,1)S(1)}, bf16[32,8,512]{2,1,0:T(8,128)(2,1)S(1)}, u32[]{:S(2)}, u32[]{:S(2)}) collective-permute-start(bf16[32,8,512]{2,1,0:T(8,128)(2,1)S(1)} %relay.2), channel_id=1, source_target_pairs={{0,192},{64,128},{128,64},{192,0},{1,193},{65,129},{129,65},{193,1... | collective-permute-start | bytes 786440 | tf_op jit(solution)/shard_map/ppermute | solution.py:187
  14.2 0.0 collective-permute-done.4.relayed
  14.2 0.1 relay.3
  14.2 0.2 collective-permute-start.5
  14.5 0.2 convert_reduce_fusion
  14.7 1.8 %collective-permute-done.direct_a = bf16[1,32,8,512]{3,2,1,0:T(8,128)(2,1)S(1)} collective-permute-done((bf16[1,32,8,512]{3,2,1,0:T(8,128)(2,1)S(1)}, bf16[1,32,8,512]{3,2,1,0:T(8,128)(2,1)S(1)}, u32[]{:S(2)}, u32[]{:S(2)}) %collective-permute-start) | collective-permute-done | bytes 262176 | tf_op jit(solution)/shard_map/ppermute | solution.py:174
  16.4 3.0 %collective-permute-done.1.direct_b = bf16[1,32,8,512]{3,2,1,0:T(8,128)(2,1)S(1)} collective-permute-done((bf16[1,32,8,512]{3,2,1,0:T(8,128)(2,1)S(1)}, bf16[1,32,8,512]{3,2,1,0:T(8,128)(2,1)S(1)}, u32[]{:S(2)}, u32[]{:S(2)}) %collective-permute-start.1) | collective-permute-done | bytes 262176 | tf_op jit(solution)/shard_map/ppermute | solution.py:175
  19.4 0.1 presum.1
  19.5 0.0 copy-start.1
  19.5 0.0 copy-start.2
  19.5 4.1 %collective-permute-done.3.second_a = bf16[32,8,512]{2,1,0:T(8,128)(2,1)S(1)} collective-permute-done((bf16[32,8,512]{2,1,0:T(8,128)(2,1)S(1)}, bf16[32,8,512]{2,1,0:T(8,128)(2,1)S(1)}, u32[]{:S(2)}, u32[]{:S(2)}) %collective-permute-start.3) | collective-permute-done | bytes 262176 | tf_op jit(solution)/shard_map/ppermute | solution.py:187
  23.6 0.0 collective-permute-done.5.second_b
  23.6 0.8 pack.1
  24.4 39.3 %all_to_all.10.arrived = bf16[64,2,8,512]{3,2,1,0:T(8,128)(2,1)S(1)} all-to-all(bf16[64,2,8,512]{3,2,1,0:T(8,128)(2,1)S(1)} %bitcast.18), channel_id=1, replica_groups=mesh['rep'=4,'fsdp'=64] {'fsdp'}, dimensions={0} | all-to-all | bytes 2097152 | tf_op jit(solution)/shard_map/all_to_all | solution.py:208
  63.7 0.0 copy-done.1
  63.7 0.0 copy-done.2
  63.7 9.9 %owner.1 = (f32[2,512,512]{2,1,0:T(8,128)}, f32[2,512,512]{2,1,0:T(8,128)}, bf16[64,2,8,512]{3,2,1,0:T(8,128)(2,1)S(1)}) custom-call(bf16[64,2,8,512]{3,2,1,0:T(8,128)(2,1)S(1)} %all_to_all.10.arrived, f32[2,512,512]{2,1,0:T(8,128)S(1)} %bitcast.21, f32[2,512,512]{2,1,0:T(8,128)S(1)} %bitcast.22), custom_call_target="tpu_custom_call" | custom-call | tf_op jit(solution)/shard_map/owner/pallas_call | solution.py:212
  73.6 34.2 %all_to_all.11 = bf16[64,2,8,512]{3,2,1,0:T(8,128)(2,1)S(1)} all-to-all(bf16[64,2,8,512]{3,2,1,0:T(8,128)(2,1)S(1)} %get-tuple-element.18), channel_id=1, replica_groups=mesh['rep'=4,'fsdp'=64] {'fsdp'}, dimensions={0} | all-to-all | bytes 2097152 | tf_op jit(solution)/shard_map/all_to_all | solution.py:226
  107.9 0.6 unpack.1
  108.5 0.1 collective-permute-start.6
  108.6 3.2 %collective-permute-start.8 = (bf16[32,8,512]{2,1,0:T(8,128)(2,1)S(1)}, bf16[32,8,512]{2,1,0:T(8,128)(2,1)S(1)}, u32[]{:S(2)}, u32[]{:S(2)}) collective-permute-start(bf16[32,8,512]{2,1,0:T(8,128)(2,1)S(1)} %get-tuple-element.20.refs_1_), channel_id=1, source_target_pairs={{0,192},{64,0},{128,64},{192,128},{1,193},{65,1},{129,65},{193,129... | collective-permute-start | bytes 786440 | tf_op jit(solution)/shard_map/ppermute | solution.py:244
  111.8 1.0 collective-permute-start.11
  112.8 1.1 collective-permute-start.10
  113.9 5.1 %collective-permute-done.6.refs_2_ = bf16[32,8,512]{2,1,0:T(8,128)(2,1)S(1)} collective-permute-done((bf16[32,8,512]{2,1,0:T(8,128)(2,1)S(1)}, bf16[32,8,512]{2,1,0:T(8,128)(2,1)S(1)}, u32[]{:S(2)}, u32[]{:S(2)}) %collective-permute-start.6) | collective-permute-done | bytes 262176 | tf_op jit(solution)/shard_map/ppermute | solution.py:243
  118.9 0.0 collective-permute-start.7
  118.9 0.0 collective-permute-done.8.refs_3_
  119.0 3.3 %collective-permute-start.9 = (bf16[32,8,512]{2,1,0:T(8,128)(2,1)S(1)}, bf16[32,8,512]{2,1,0:T(8,128)(2,1)S(1)}, u32[]{:S(2)}, u32[]{:S(2)}) collective-permute-start(bf16[32,8,512]{2,1,0:T(8,128)(2,1)S(1)} %collective-permute-done.8.refs_3_), channel_id=1, source_target_pairs={{0,192},{64,0},{128,64},{192,128},{1,193},{65,1},{129,65},{193,129... | collective-permute-start | bytes 786440 | tf_op jit(solution)/shard_map/ppermute | solution.py:248
  122.2 1.6 %place_first.1.refs_2_ = bf16[4,2,32,8,512]{4,3,2,1,0:T(8,128)(2,1)} custom-call(s32[1]{0:T(128)} %bitcast.table, bf16[32,8,512]{2,1,0:T(8,128)(2,1)S(1)} %get-tuple-element.19.refs_0_, bf16[32,8,512]{2,1,0:T(8,128)(2,1)S(1)} %get-tuple-element.20.refs_1_, bf16[32,8,512]{2,1,0:T(8,128)(2,1)S(1)} %collective-permute-done.6.refs_2_, ...), custom_call_target="tpu_custom_call" | custom-call | tf_op jit(solution)/shard_map/place_first/pallas_call | solution.py:261
  123.8 0.4 collective-permute-done.11.refs_1_
  124.2 0.4 collective-permute-done.10.refs_0_
  124.6 0.8 place_second.1.refs_2_
  125.4 4.1 %collective-permute-done.7.refs_0_ = bf16[32,8,512]{2,1,0:T(8,128)(2,1)S(1)} collective-permute-done((bf16[32,8,512]{2,1,0:T(8,128)(2,1)S(1)}, bf16[32,8,512]{2,1,0:T(8,128)(2,1)S(1)}, u32[]{:S(2)}, u32[]{:S(2)}) %collective-permute-start.7) | collective-permute-done | bytes 262176 | tf_op jit(solution)/shard_map/ppermute | solution.py:247
  129.5 0.0 collective-permute-done.9.refs_1_
  129.5 0.8 place_far.1
  (2 shorter events, 0.0 us)
Async XLA Ops:
  0.6 8.1 %copy-start.3 = (s32[4,64,1]{1,2,0:T(1,128)S(1)}, s32[4,64,1]{1,2,0:T(1,128)}, u32[]{:S(2)}) copy-start(s32[4,64,1]{1,2,0:T(1,128)} %param.7) | copy-start | bytes 3076
  1.7 8.6 %collective-permute-start.2 = (bf16[32,8,512]{2,1,0:T(8,128)(2,1)S(1)}, bf16[32,8,512]{2,1,0:T(8,128)(2,1)S(1)}, u32[]{:S(2)}, u32[]{:S(2)}) collective-permute-start(bf16[32,8,512]{2,1,0:T(8,128)(2,1)S(1)} %get-tuple-element.24), channel_id=1, source_target_pairs={{0,64},{64,0},{128,192},{192,128},{1,65},{65,1},{129,193},{193,129... | collective-permute-start | bytes 786440 | tf_op jit(solution)/shard_map/ppermute | solution.py:169
  3.4 10.8 %collective-permute-start.4 = (bf16[32,8,512]{2,1,0:T(8,128)(2,1)S(1)}, bf16[32,8,512]{2,1,0:T(8,128)(2,1)S(1)}, u32[]{:S(2)}, u32[]{:S(2)}) collective-permute-start(bf16[32,8,512]{2,1,0:T(8,128)(2,1)S(1)} %get-tuple-element.23), channel_id=1, source_target_pairs={{0,192},{64,128},{128,64},{192,0},{1,193},{65,129},{129,65},{193,1... | collective-permute-start | bytes 786440 | tf_op jit(solution)/shard_map/ppermute | solution.py:170
  5.6 1.6 %copy-start = (bf16[1,256,8,512]{3,2,1,0:T(8,128)(2,1)S(1)}, bf16[1,256,8,512]{3,2,1,0:T(8,128)(2,1)}, u32[]{:S(2)}) copy-start(bf16[1,256,8,512]{3,2,1,0:T(8,128)(2,1)} %param.4) | copy-start | bytes 6291460
  7.3 9.1 %collective-permute-start = (bf16[1,32,8,512]{3,2,1,0:T(8,128)(2,1)S(1)}, bf16[1,32,8,512]{3,2,1,0:T(8,128)(2,1)S(1)}, u32[]{:S(2)}, u32[]{:S(2)}) collective-permute-start(bf16[1,32,8,512]{3,2,1,0:T(8,128)(2,1)S(1)} %get-tuple-element.14), channel_id=1, source_target_pairs={{0,64},{64,0},{128,192},{192,128},{1,65},{65,1},{129,193},{193,129... | collective-permute-start | bytes 786440 | tf_op jit(solution)/shard_map/ppermute | solution.py:174
  8.1 11.3 %collective-permute-start.1 = (bf16[1,32,8,512]{3,2,1,0:T(8,128)(2,1)S(1)}, bf16[1,32,8,512]{3,2,1,0:T(8,128)(2,1)S(1)}, u32[]{:S(2)}, u32[]{:S(2)}) collective-permute-start(bf16[1,32,8,512]{3,2,1,0:T(8,128)(2,1)S(1)} %get-tuple-element.15), channel_id=1, source_target_pairs={{0,192},{64,128},{128,64},{192,0},{1,193},{65,129},{129,65},{193,1... | collective-permute-start | bytes 786440 | tf_op jit(solution)/shard_map/ppermute | solution.py:175
  10.4 13.2 %collective-permute-start.3 = (bf16[32,8,512]{2,1,0:T(8,128)(2,1)S(1)}, bf16[32,8,512]{2,1,0:T(8,128)(2,1)S(1)}, u32[]{:S(2)}, u32[]{:S(2)}) collective-permute-start(bf16[32,8,512]{2,1,0:T(8,128)(2,1)S(1)} %relay.2), channel_id=1, source_target_pairs={{0,192},{64,128},{128,64},{192,0},{1,193},{65,129},{129,65},{193,1... | collective-permute-start | bytes 786440 | tf_op jit(solution)/shard_map/ppermute | solution.py:187
  14.2 9.4 %collective-permute-start.5 = (bf16[32,8,512]{2,1,0:T(8,128)(2,1)S(1)}, bf16[32,8,512]{2,1,0:T(8,128)(2,1)S(1)}, u32[]{:S(2)}, u32[]{:S(2)}) collective-permute-start(bf16[32,8,512]{2,1,0:T(8,128)(2,1)S(1)} %relay.3), channel_id=1, source_target_pairs={{0,64},{64,0},{128,192},{192,128},{1,65},{65,1},{129,193},{193,129... | collective-permute-start | bytes 786440 | tf_op jit(solution)/shard_map/ppermute | solution.py:188
  19.5 44.2 %copy-start.1 = (f32[1,1,2,512,512]{4,3,2,1,0:T(8,128)S(1)}, f32[1,1,2,512,512]{4,3,2,1,0:T(8,128)}, u32[]{:S(2)}) copy-start(f32[1,1,2,512,512]{4,3,2,1,0:T(8,128)} %param.5) | copy-start | bytes 6291460
  19.5 44.2 %copy-start.2 = (f32[1,1,2,512,512]{4,3,2,1,0:T(8,128)S(1)}, f32[1,1,2,512,512]{4,3,2,1,0:T(8,128)}, u32[]{:S(2)}) copy-start(f32[1,1,2,512,512]{4,3,2,1,0:T(8,128)} %param.6) | copy-start | bytes 6291460
  108.5 10.4 %collective-permute-start.6 = (bf16[32,8,512]{2,1,0:T(8,128)(2,1)S(1)}, bf16[32,8,512]{2,1,0:T(8,128)(2,1)S(1)}, u32[]{:S(2)}, u32[]{:S(2)}) collective-permute-start(bf16[32,8,512]{2,1,0:T(8,128)(2,1)S(1)} %get-tuple-element.19.refs_0_), channel_id=1, source_target_pairs={{0,64},{64,128},{128,192},{192,0},{1,65},{65,129},{129,193},{193,1... | collective-permute-start | bytes 786440 | tf_op jit(solution)/shard_map/ppermute | solution.py:243
  108.6 10.3 %collective-permute-start.8 = (bf16[32,8,512]{2,1,0:T(8,128)(2,1)S(1)}, bf16[32,8,512]{2,1,0:T(8,128)(2,1)S(1)}, u32[]{:S(2)}, u32[]{:S(2)}) collective-permute-start(bf16[32,8,512]{2,1,0:T(8,128)(2,1)S(1)} %get-tuple-element.20.refs_1_), channel_id=1, source_target_pairs={{0,192},{64,0},{128,64},{192,128},{1,193},{65,1},{129,65},{193,129... | collective-permute-start | bytes 786440 | tf_op jit(solution)/shard_map/ppermute | solution.py:244
  111.8 12.3 %collective-permute-start.11 = (bf16[32,8,512]{2,1,0:T(8,128)(2,1)S(1)}, bf16[32,8,512]{2,1,0:T(8,128)(2,1)S(1)}, u32[]{:S(2)}, u32[]{:S(2)}) collective-permute-start(bf16[32,8,512]{2,1,0:T(8,128)(2,1)S(1)} %get-tuple-element.19.refs_0_), channel_id=1, source_target_pairs={{0,192},{64,0},{128,64},{192,128},{1,193},{65,1},{129,65},{193,129... | collective-permute-start | bytes 786440 | tf_op jit(solution)/shard_map/ppermute | solution.py:246
  112.8 11.8 %collective-permute-start.10 = (bf16[32,8,512]{2,1,0:T(8,128)(2,1)S(1)}, bf16[32,8,512]{2,1,0:T(8,128)(2,1)S(1)}, u32[]{:S(2)}, u32[]{:S(2)}) collective-permute-start(bf16[32,8,512]{2,1,0:T(8,128)(2,1)S(1)} %get-tuple-element.20.refs_1_), channel_id=1, source_target_pairs={{0,64},{64,128},{128,192},{192,0},{1,65},{65,129},{129,193},{193,1... | collective-permute-start | bytes 786440 | tf_op jit(solution)/shard_map/ppermute | solution.py:245
  118.9 10.6 %collective-permute-start.7 = (bf16[32,8,512]{2,1,0:T(8,128)(2,1)S(1)}, bf16[32,8,512]{2,1,0:T(8,128)(2,1)S(1)}, u32[]{:S(2)}, u32[]{:S(2)}) collective-permute-start(bf16[32,8,512]{2,1,0:T(8,128)(2,1)S(1)} %collective-permute-done.6.refs_2_), channel_id=1, source_target_pairs={{0,64},{64,128},{128,192},{192,0},{1,65},{65,129},{129,193},{193,1... | collective-permute-start | bytes 786440 | tf_op jit(solution)/shard_map/ppermute | solution.py:247
  119.0 10.6 %collective-permute-start.9 = (bf16[32,8,512]{2,1,0:T(8,128)(2,1)S(1)}, bf16[32,8,512]{2,1,0:T(8,128)(2,1)S(1)}, u32[]{:S(2)}, u32[]{:S(2)}) collective-permute-start(bf16[32,8,512]{2,1,0:T(8,128)(2,1)S(1)} %collective-permute-done.8.refs_3_), channel_id=1, source_target_pairs={{0,192},{64,0},{128,64},{192,128},{1,193},{65,1},{129,65},{193,129... | collective-permute-start | bytes 786440 | tf_op jit(solution)/shard_map/ppermute | solution.py:248

commit v8 on v7

--- a/solution.py
+++ b/solution.py
@@ -23,35 +23,36 @@
 def pick_kernel(places, table, parts, *refs):
     outs, sems = refs[:-1], refs[-1]
     copies = []
-    for i, (k, h, target, row) in enumerate(places):
-        copies.append(pltpu.make_async_copy(parts.at[table[0] ^ k, h], outs[target].at[row], sems.at[i]))
+    for i, (k, first, count) in enumerate(places):
+        source = parts.at[table[0] ^ k, pl.ds(first, count)]
+        copies.append(pltpu.make_async_copy(source, outs[i], sems.at[i]))
     for copy in copies:
         copy.start()
     for copy in copies:
         copy.wait()
 
 
-def relay_kernel(kept, relayed, out):
-    out[...] = (kept[0].astype(F32) + relayed[...].astype(F32)).astype(BF16)
+def relay_kernel(kept, relayed, *refs):
+    out = refs[-1]
+    out[...] = (kept[...].astype(F32) + relayed[...].astype(F32)).astype(BF16)
 
 
 def presum_kernel(own, direct_a, direct_b, out):
-    half = direct_a.shape[1]
-    for k, direct in enumerate((direct_a, direct_b)):
-        out[k * half : (k + 1) * half] = own[k].astype(F32) + direct[0].astype(F32)
+    count = direct_a.shape[0]
+    out[:count] = own[:count].astype(F32) + direct_a[...].astype(F32)
+    out[count:] = own[count:].astype(F32) + direct_b[...].astype(F32)
 
 
 def pack_kernel(table, presum, second_a, second_b, out):
-    half = second_a.shape[0]
     out[...] = jnp.zeros(out.shape, out.dtype)
-    for k, second in enumerate((second_a, second_b)):
-
-        def move(j, carry, k=k, second=second):
-            total = presum[k * half + j] + second[j].astype(F32)
-            out[table[k * half + j]] = total.astype(BF16)
+    for first, second in ((0, second_a), (second_a.shape[0], second_b)):
+
+        def move(j, carry, first=first, second=second):
+            total = presum[first + j] + second[j].astype(F32)
+            out[table[first + j]] = total.astype(BF16)
             return carry
 
-        lax.fori_loop(0, half, move, 0, unroll=8)
+        lax.fori_loop(0, second.shape[0], move, 0, unroll=4)
 
 
 def dot(a, b, ca=1, cb=0):
@@ -140,52 +141,54 @@
 
     swap1 = [(i, i ^ 1) for i in range(reps)]
     swap3 = [(i, i ^ 3) for i in range(reps)]
-    parts = grads.reshape(reps, 2, half, rows, width)
+    parts = grads.reshape(reps, per_row, rows, width)
+    count_a = per_row * 9 // 16
+    count_b = per_row - count_a
     params = pltpu.CompilerParams(vmem_limit_bytes=VMEM_BYTES)
-    half_shape = jax.ShapeDtypeStruct((half, rows, width), BF16)
 
     in_vmem = pl.BlockSpec(memory_space=pltpu.VMEM)
     in_hbm = pl.BlockSpec(memory_space=pltpu.HBM)
-
-    def pick(name, *groups):
-        places = [(k, h, o, i) for o, group in enumerate(groups) for i, (k, h) in enumerate(group)]
-        return pl.pallas_call(
-            functools.partial(pick_kernel, places),
-            out_shape=[jax.ShapeDtypeStruct((len(group), half, rows, width), BF16) for group in groups],
-            grid_spec=pltpu.PrefetchScalarGridSpec(
-                num_scalar_prefetch=1,
-                grid=(1,),
-                in_specs=[in_hbm],
-                out_specs=[in_vmem] * len(groups),
-                scratch_shapes=[pltpu.SemaphoreType.DMA((len(places),))],
-            ),
-            compiler_params=params,
-            name=name,
-        )(r[None], parts)
-
-    def opposite(h):
-        return lax.dynamic_slice(parts, (r ^ 2, h, 0, 0, 0), (1, 1, half, rows, width))[0, 0]
-
-    relayed_a = lax.ppermute(opposite(0), "rep", swap1)
-    relayed_b = lax.ppermute(opposite(1), "rep", swap3)
-    send_a, send_b, kept_a, kept_b, own = pick(
-        "pick", [(1, 0)], [(3, 1)], [(3, 0)], [(1, 1)], [(0, 0), (0, 1)]
-    )
+    anywhere = pl.BlockSpec(memory_space=pl.ANY)
+
+    def rows_of(count):
+        return jax.ShapeDtypeStruct((count, rows, width), BF16)
+
+    def opposite(first, count):
+        return lax.dynamic_slice(parts, (r ^ 2, first, 0, 0), (1, count, rows, width))[0]
+
+    relayed_a = lax.ppermute(opposite(0, count_a), "rep", swap1)
+    relayed_b = lax.ppermute(opposite(count_a, count_b), "rep", swap3)
+    places = [(1, 0, count_a), (3, count_a, count_b), (3, 0, count_a), (1, count_a, count_b), (0, 0, per_row)]
+    send_a, send_b, kept_a, kept_b, own = pl.pallas_call(
+        functools.partial(pick_kernel, places),
+        out_shape=[rows_of(count) for _, _, count in places],
+        grid_spec=pltpu.PrefetchScalarGridSpec(
+            num_scalar_prefetch=1,
+            grid=(1,),
+            in_specs=[in_hbm],
+            out_specs=[in_vmem] * len(places),
+            scratch_shapes=[pltpu.SemaphoreType.DMA((len(places),))],
+        ),
+        compiler_params=params,
+        name="pick",
+    )(r[None], parts)
     direct_a = lax.ppermute(send_a, "rep", swap1)
     direct_b = lax.ppermute(send_b, "rep", swap3)
 
-    def relay(kept, relayed):
+    def relay(kept, relayed, *after):
         return pl.pallas_call(
             relay_kernel,
-            in_specs=[in_vmem] * 2,
+            in_specs=[in_vmem] * 2 + [anywhere] * len(after),
             out_specs=in_vmem,
-            out_shape=half_shape,
+            out_shape=rows_of(kept.shape[0]),
             compiler_params=params,
             name="relay",
-        )(kept, relayed)
-
-    second_a = lax.ppermute(relay(kept_a, relayed_a), "rep", swap3)
-    second_b = lax.ppermute(relay(kept_b, relayed_b), "rep", swap1)
+        )(kept, relayed, *after)
+
+    sum_a = relay(kept_a, relayed_a)
+    sum_b = relay(kept_b, relayed_b, sum_a)
+    second_a = lax.ppermute(sum_a, "rep", swap3)
+    second_b = lax.ppermute(sum_b, "rep", swap1)
     presum = pl.pallas_call(
         presum_kernel,
         in_specs=[in_vmem] * 3,
@@ -207,7 +210,6 @@
 
     arrived = lax.all_to_all(outgoing, "fsdp", split_axis=0, concat_axis=0, tiled=True)
 
-    anywhere = pl.BlockSpec(memory_space=pl.ANY)
     factors = jax.ShapeDtypeStruct((capacity, order, order), F32)
     new_left, new_right, slot_update = pl.pallas_call(
         owner_kernel,
@@ -227,7 +229,7 @@
 
     mine_a, mine_b = pl.pallas_call(
         unpack_kernel,
-        out_shape=[half_shape] * 2,
+        out_shape=[rows_of(half)] * 2,
         grid_spec=pltpu.PrefetchScalarGridSpec(
             num_scalar_prefetch=1,
             grid=(1,),

time: 131 us -> 131 us (level)
    ppermute x1, waiting for transfers between devices: 2.95 us -> 4.58 us  [shards(): direct_b = lax.ppermute(send_b, 'rep', swap3)]
    ppermute x4, waiting for transfers between devices: 5.73 us -> 4.11 us  [the longest x1 2.74 us: shards(): second_b = lax.ppermute(sum_b, 'rep', swap1)]
  transfers between devices with their start and end apart: 12 -> 12, of which waited for: 8 -> 9; matrix products, arithmetic and copies ran while one was open for 0% -> 1% of each run, Pallas kernels for 2% -> 3%
where the time goes in v8:
time: 131 us
  blocking collectives  73.6 us (56%)
  waiting for transfers between devices  19.9 us (15%)
  starting transfers between devices  17.1 us (13%)
  Pallas kernels  15.6 us (12%)
  local copies, waits for them, and re-layouts  3.55 us (3%)
    all_to_all x1, blocking collectives, shards(): lax.all_to_all(outgoing, 'fsdp', split_axis=0, concat_axis=0, tiled=True)  39.3 us
    all_to_all x1, blocking collectives, shards(): lax.all_to_all(slot_update, 'fsdp', split_axis=0, concat_axis=0, tiled=True)  34.2 us
    pallas_call x1, Pallas kernels, shards(): pl.pallas_call(owner_kernel, in_specs=[in_vmem, in_vmem, in_vmem], out_sp...  9.92 us
    ppermute x1, waiting for transfers between devices, shards(): left_a = lax.ppermute(mine_a, 'rep', plus)  5.08 us
    ppermute x1, waiting for transfers between devices, shards(): direct_b = lax.ppermute(send_b, 'rep', swap3)  4.58 us
    ppermute x1, waiting for transfers between devices, shards(): far_a = lax.ppermute(left_a, 'rep', plus)  4.13 us
    ppermute x1, starting transfers between devices, shards(): far_b = lax.ppermute(right_b, 'rep', minus)  3.27 us
    ppermute x1, starting transfers between devices, shards(): right_b = lax.ppermute(mine_b, 'rep', minus)  3.22 us
  transfers between devices with their start and end apart: 12, of which 9 were waited for; matrix products, arithmetic and copies ran while one was open for 1% of the time, Pallas kernels for 3%

profile of v8, /device:TPU:32, one launch (start us, length us, event | category | flops | bytes accessed | tf_op | source)
XLA Modules:
  0.0 130.6 jit_solution(2357513473307778526)
XLA Ops:
  0.6 0.0 copy-start.3
  0.7 1.0 dynamic-slice_bitcast_fusion
  1.6 1.7 %collective-permute-start.2 = (bf16[36,8,512]{2,1,0:T(8,128)(2,1)S(1)}, bf16[36,8,512]{2,1,0:T(8,128)(2,1)S(1)}, u32[]{:S(2)}, u32[]{:S(2)}) collective-permute-start(bf16[36,8,512]{2,1,0:T(8,128)(2,1)S(1)} %dynamic-slice_bitcast_fusion), channel_id=1, source_target_pairs={{0,64},{64,0},{128,192},{192,128},{1,65},{65,1},{129,193},{193,129... | collective-permute-start | bytes 884744 | tf_op jit(solution)/shard_map/ppermute | solution.py:159
  3.3 1.0 dynamic-slice_bitcast_fusion.1
  4.3 2.3 %collective-permute-start.4 = (bf16[28,8,512]{2,1,0:T(8,128)(2,1)S(1)}, bf16[28,8,512]{2,1,0:T(8,128)(2,1)S(1)}, u32[]{:S(2)}, u32[]{:S(2)}) collective-permute-start(bf16[28,8,512]{2,1,0:T(8,128)(2,1)S(1)} %dynamic-slice_bitcast_fusion.1), channel_id=1, source_target_pairs={{0,192},{64,128},{128,64},{192,0},{1,193},{65,129},{129,65},{193,1... | collective-permute-start | bytes 688136 | tf_op jit(solution)/shard_map/ppermute | solution.py:160
  6.5 0.0 copy-start
  6.5 1.6 %copy-done = bf16[1,256,8,512]{3,2,1,0:T(8,128)(2,1)S(1)} copy-done((bf16[1,256,8,512]{3,2,1,0:T(8,128)(2,1)S(1)}, bf16[1,256,8,512]{3,2,1,0:T(8,128)(2,1)}, u32[]{:S(2)}) %copy-start) | copy-done | bytes 2097176
  8.1 0.8 pick.1
  8.9 1.1 collective-permute-start.1
  10.1 0.0 collective-permute-start
  10.1 0.0 copy-done.3
  10.1 0.4 collective-permute-done.2.relayed
  10.5 0.1 relay.2.refs_0_
  10.5 3.1 %collective-permute-start.3 = (bf16[36,8,512]{2,1,0:T(8,128)(2,1)S(1)}, bf16[36,8,512]{2,1,0:T(8,128)(2,1)S(1)}, u32[]{:S(2)}, u32[]{:S(2)}) collective-permute-start(bf16[36,8,512]{2,1,0:T(8,128)(2,1)S(1)} %relay.2.refs_0_), channel_id=1, source_target_pairs={{0,192},{64,128},{128,64},{192,0},{1,193},{65,129},{129,65},{193,1... | collective-permute-start | bytes 884744 | tf_op jit(solution)/shard_map/ppermute | solution.py:190
  13.6 0.0 collective-permute-done.4.relayed
  13.7 0.1 relay.3
  13.7 0.3 collective-permute-start.5
  14.0 0.2 convert_reduce_fusion
  14.2 4.6 %collective-permute-done.1.direct_b = bf16[28,8,512]{2,1,0:T(8,128)(2,1)S(1)} collective-permute-done((bf16[28,8,512]{2,1,0:T(8,128)(2,1)S(1)}, bf16[28,8,512]{2,1,0:T(8,128)(2,1)S(1)}, u32[]{:S(2)}, u32[]{:S(2)}) %collective-permute-start.1) | collective-permute-done | bytes 229408 | tf_op jit(solution)/shard_map/ppermute | solution.py:176
  18.8 1.3 collective-permute-done.direct_a
  20.0 0.1 presum.1
  20.1 0.0 copy-start.1
  20.1 0.0 copy-start.2
  20.1 2.7 %collective-permute-done.5.second_b = bf16[28,8,512]{2,1,0:T(8,128)(2,1)S(1)} collective-permute-done((bf16[28,8,512]{2,1,0:T(8,128)(2,1)S(1)}, bf16[28,8,512]{2,1,0:T(8,128)(2,1)S(1)}, u32[]{:S(2)}, u32[]{:S(2)}) %collective-permute-start.5) | collective-permute-done | bytes 229408 | tf_op jit(solution)/shard_map/ppermute | solution.py:191
  22.9 1.0 collective-permute-done.3.second_a
  23.9 0.8 pack.1
  24.6 39.3 %all_to_all.10.arrived = bf16[64,2,8,512]{3,2,1,0:T(8,128)(2,1)S(1)} all-to-all(bf16[64,2,8,512]{3,2,1,0:T(8,128)(2,1)S(1)} %bitcast.18), channel_id=1, replica_groups=mesh['rep'=4,'fsdp'=64] {'fsdp'}, dimensions={0} | all-to-all | bytes 2097152 | tf_op jit(solution)/shard_map/all_to_all | solution.py:211
  64.0 0.0 copy-done.1
  64.0 0.0 copy-done.2
  64.0 9.9 %owner.1 = (f32[2,512,512]{2,1,0:T(8,128)}, f32[2,512,512]{2,1,0:T(8,128)}, bf16[64,2,8,512]{3,2,1,0:T(8,128)(2,1)S(1)}) custom-call(bf16[64,2,8,512]{3,2,1,0:T(8,128)(2,1)S(1)} %all_to_all.10.arrived, f32[2,512,512]{2,1,0:T(8,128)S(1)} %bitcast.22, f32[2,512,512]{2,1,0:T(8,128)S(1)} %bitcast.23), custom_call_target="tpu_custom_call" | custom-call | tf_op jit(solution)/shard_map/owner/pallas_call | solution.py:214
  73.9 34.2 %all_to_all.11 = bf16[64,2,8,512]{3,2,1,0:T(8,128)(2,1)S(1)} all-to-all(bf16[64,2,8,512]{3,2,1,0:T(8,128)(2,1)S(1)} %get-tuple-element.18), channel_id=1, replica_groups=mesh['rep'=4,'fsdp'=64] {'fsdp'}, dimensions={0} | all-to-all | bytes 2097152 | tf_op jit(solution)/shard_map/all_to_all | solution.py:228
  108.2 0.6 unpack.1
  108.8 0.1 collective-permute-start.6
  108.9 3.2 %collective-permute-start.8 = (bf16[32,8,512]{2,1,0:T(8,128)(2,1)S(1)}, bf16[32,8,512]{2,1,0:T(8,128)(2,1)S(1)}, u32[]{:S(2)}, u32[]{:S(2)}) collective-permute-start(bf16[32,8,512]{2,1,0:T(8,128)(2,1)S(1)} %get-tuple-element.20.refs_1_), channel_id=1, source_target_pairs={{0,192},{64,0},{128,64},{192,128},{1,193},{65,1},{129,65},{193,129... | collective-permute-start | bytes 786440 | tf_op jit(solution)/shard_map/ppermute | solution.py:246
  112.1 1.0 collective-permute-start.11
  113.1 1.1 collective-permute-start.10
  114.2 5.1 %collective-permute-done.6.refs_2_ = bf16[32,8,512]{2,1,0:T(8,128)(2,1)S(1)} collective-permute-done((bf16[32,8,512]{2,1,0:T(8,128)(2,1)S(1)}, bf16[32,8,512]{2,1,0:T(8,128)(2,1)S(1)}, u32[]{:S(2)}, u32[]{:S(2)}) %collective-permute-start.6) | collective-permute-done | bytes 262176 | tf_op jit(solution)/shard_map/ppermute | solution.py:245
  119.2 0.0 collective-permute-start.7
  119.2 0.0 collective-permute-done.8.refs_3_
  119.2 3.3 %collective-permute-start.9 = (bf16[32,8,512]{2,1,0:T(8,128)(2,1)S(1)}, bf16[32,8,512]{2,1,0:T(8,128)(2,1)S(1)}, u32[]{:S(2)}, u32[]{:S(2)}) collective-permute-start(bf16[32,8,512]{2,1,0:T(8,128)(2,1)S(1)} %collective-permute-done.8.refs_3_), channel_id=1, source_target_pairs={{0,192},{64,0},{128,64},{192,128},{1,193},{65,1},{129,65},{193,129... | collective-permute-start | bytes 786440 | tf_op jit(solution)/shard_map/ppermute | solution.py:250
  122.5 1.6 %place_first.1.refs_2_ = bf16[4,2,32,8,512]{4,3,2,1,0:T(8,128)(2,1)} custom-call(s32[1]{0:T(128)} %bitcast.table, bf16[32,8,512]{2,1,0:T(8,128)(2,1)S(1)} %get-tuple-element.19.refs_0_, bf16[32,8,512]{2,1,0:T(8,128)(2,1)S(1)} %get-tuple-element.20.refs_1_, bf16[32,8,512]{2,1,0:T(8,128)(2,1)S(1)} %collective-permute-done.6.refs_2_, ...), custom_call_target="tpu_custom_call" | custom-call | tf_op jit(solution)/shard_map/place_first/pallas_call | solution.py:263
  124.1 0.4 collective-permute-done.11.refs_1_
  124.4 0.4 collective-permute-done.10.refs_0_
  124.8 0.8 place_second.1.refs_2_
  125.7 4.1 %collective-permute-done.7.refs_0_ = bf16[32,8,512]{2,1,0:T(8,128)(2,1)S(1)} collective-permute-done((bf16[32,8,512]{2,1,0:T(8,128)(2,1)S(1)}, bf16[32,8,512]{2,1,0:T(8,128)(2,1)S(1)}, u32[]{:S(2)}, u32[]{:S(2)}) %collective-permute-start.7) | collective-permute-done | bytes 262176 | tf_op jit(solution)/shard_map/ppermute | solution.py:249
  129.8 0.0 collective-permute-done.9.refs_1_
  129.8 0.8 place_far.1
  (2 shorter events, 0.0 us)
Async XLA Ops:
  0.6 9.4 %copy-start.3 = (s32[4,64,1]{1,2,0:T(1,128)S(1)}, s32[4,64,1]{1,2,0:T(1,128)}, u32[]{:S(2)}) copy-start(s32[4,64,1]{1,2,0:T(1,128)} %param.7) | copy-start | bytes 3076
  1.6 8.8 %collective-permute-start.2 = (bf16[36,8,512]{2,1,0:T(8,128)(2,1)S(1)}, bf16[36,8,512]{2,1,0:T(8,128)(2,1)S(1)}, u32[]{:S(2)}, u32[]{:S(2)}) collective-permute-start(bf16[36,8,512]{2,1,0:T(8,128)(2,1)S(1)} %dynamic-slice_bitcast_fusion), channel_id=1, source_target_pairs={{0,64},{64,0},{128,192},{192,128},{1,65},{65,1},{129,193},{193,129... | collective-permute-start | bytes 884744 | tf_op jit(solution)/shard_map/ppermute | solution.py:159
  4.3 9.4 %collective-permute-start.4 = (bf16[28,8,512]{2,1,0:T(8,128)(2,1)S(1)}, bf16[28,8,512]{2,1,0:T(8,128)(2,1)S(1)}, u32[]{:S(2)}, u32[]{:S(2)}) collective-permute-start(bf16[28,8,512]{2,1,0:T(8,128)(2,1)S(1)} %dynamic-slice_bitcast_fusion.1), channel_id=1, source_target_pairs={{0,192},{64,128},{128,64},{192,0},{1,193},{65,129},{129,65},{193,1... | collective-permute-start | bytes 688136 | tf_op jit(solution)/shard_map/ppermute | solution.py:160
  6.5 1.6 %copy-start = (bf16[1,256,8,512]{3,2,1,0:T(8,128)(2,1)S(1)}, bf16[1,256,8,512]{3,2,1,0:T(8,128)(2,1)}, u32[]{:S(2)}) copy-start(bf16[1,256,8,512]{3,2,1,0:T(8,128)(2,1)} %param.4) | copy-start | bytes 6291460
  8.9 9.8 %collective-permute-start.1 = (bf16[28,8,512]{2,1,0:T(8,128)(2,1)S(1)}, bf16[28,8,512]{2,1,0:T(8,128)(2,1)S(1)}, u32[]{:S(2)}, u32[]{:S(2)}) collective-permute-start(bf16[28,8,512]{2,1,0:T(8,128)(2,1)S(1)} %get-tuple-element.15), channel_id=1, source_target_pairs={{0,192},{64,128},{128,64},{192,0},{1,193},{65,129},{129,65},{193,1... | collective-permute-start | bytes 688136 | tf_op jit(solution)/shard_map/ppermute | solution.py:176
  10.1 9.9 %collective-permute-start = (bf16[36,8,512]{2,1,0:T(8,128)(2,1)S(1)}, bf16[36,8,512]{2,1,0:T(8,128)(2,1)S(1)}, u32[]{:S(2)}, u32[]{:S(2)}) collective-permute-start(bf16[36,8,512]{2,1,0:T(8,128)(2,1)S(1)} %get-tuple-element.14), channel_id=1, source_target_pairs={{0,64},{64,0},{128,192},{192,128},{1,65},{65,1},{129,193},{193,129... | collective-permute-start | bytes 884744 | tf_op jit(solution)/shard_map/ppermute | solution.py:175
  10.5 13.3 %collective-permute-start.3 = (bf16[36,8,512]{2,1,0:T(8,128)(2,1)S(1)}, bf16[36,8,512]{2,1,0:T(8,128)(2,1)S(1)}, u32[]{:S(2)}, u32[]{:S(2)}) collective-permute-start(bf16[36,8,512]{2,1,0:T(8,128)(2,1)S(1)} %relay.2.refs_0_), channel_id=1, source_target_pairs={{0,192},{64,128},{128,64},{192,0},{1,193},{65,129},{129,65},{193,1... | collective-permute-start | bytes 884744 | tf_op jit(solution)/shard_map/ppermute | solution.py:190
  13.7 9.2 %collective-permute-start.5 = (bf16[28,8,512]{2,1,0:T(8,128)(2,1)S(1)}, bf16[28,8,512]{2,1,0:T(8,128)(2,1)S(1)}, u32[]{:S(2)}, u32[]{:S(2)}) collective-permute-start(bf16[28,8,512]{2,1,0:T(8,128)(2,1)S(1)} %relay.3), channel_id=1, source_target_pairs={{0,64},{64,0},{128,192},{192,128},{1,65},{65,1},{129,193},{193,129... | collective-permute-start | bytes 688136 | tf_op jit(solution)/shard_map/ppermute | solution.py:191
  20.1 43.9 %copy-start.1 = (f32[1,1,2,512,512]{4,3,2,1,0:T(8,128)S(1)}, f32[1,1,2,512,512]{4,3,2,1,0:T(8,128)}, u32[]{:S(2)}) copy-start(f32[1,1,2,512,512]{4,3,2,1,0:T(8,128)} %param.5) | copy-start | bytes 6291460
  20.1 43.8 %copy-start.2 = (f32[1,1,2,512,512]{4,3,2,1,0:T(8,128)S(1)}, f32[1,1,2,512,512]{4,3,2,1,0:T(8,128)}, u32[]{:S(2)}) copy-start(f32[1,1,2,512,512]{4,3,2,1,0:T(8,128)} %param.6) | copy-start | bytes 6291460
  108.8 10.4 %collective-permute-start.6 = (bf16[32,8,512]{2,1,0:T(8,128)(2,1)S(1)}, bf16[32,8,512]{2,1,0:T(8,128)(2,1)S(1)}, u32[]{:S(2)}, u32[]{:S(2)}) collective-permute-start(bf16[32,8,512]{2,1,0:T(8,128)(2,1)S(1)} %get-tuple-element.19.refs_0_), channel_id=1, source_target_pairs={{0,64},{64,128},{128,192},{192,0},{1,65},{65,129},{129,193},{193,1... | collective-permute-start | bytes 786440 | tf_op jit(solution)/shard_map/ppermute | solution.py:245
  108.9 10.3 %collective-permute-start.8 = (bf16[32,8,512]{2,1,0:T(8,128)(2,1)S(1)}, bf16[32,8,512]{2,1,0:T(8,128)(2,1)S(1)}, u32[]{:S(2)}, u32[]{:S(2)}) collective-permute-start(bf16[32,8,512]{2,1,0:T(8,128)(2,1)S(1)} %get-tuple-element.20.refs_1_), channel_id=1, source_target_pairs={{0,192},{64,0},{128,64},{192,128},{1,193},{65,1},{129,65},{193,129... | collective-permute-start | bytes 786440 | tf_op jit(solution)/shard_map/ppermute | solution.py:246
  112.1 12.3 %collective-permute-start.11 = (bf16[32,8,512]{2,1,0:T(8,128)(2,1)S(1)}, bf16[32,8,512]{2,1,0:T(8,128)(2,1)S(1)}, u32[]{:S(2)}, u32[]{:S(2)}) collective-permute-start(bf16[32,8,512]{2,1,0:T(8,128)(2,1)S(1)} %get-tuple-element.19.refs_0_), channel_id=1, source_target_pairs={{0,192},{64,0},{128,64},{192,128},{1,193},{65,1},{129,65},{193,129... | collective-permute-start | bytes 786440 | tf_op jit(solution)/shard_map/ppermute | solution.py:248
  113.1 11.8 %collective-permute-start.10 = (bf16[32,8,512]{2,1,0:T(8,128)(2,1)S(1)}, bf16[32,8,512]{2,1,0:T(8,128)(2,1)S(1)}, u32[]{:S(2)}, u32[]{:S(2)}) collective-permute-start(bf16[32,8,512]{2,1,0:T(8,128)(2,1)S(1)} %get-tuple-element.20.refs_1_), channel_id=1, source_target_pairs={{0,64},{64,128},{128,192},{192,0},{1,65},{65,129},{129,193},{193,1... | collective-permute-start | bytes 786440 | tf_op jit(solution)/shard_map/ppermute | solution.py:247
  119.2 10.6 %collective-permute-start.7 = (bf16[32,8,512]{2,1,0:T(8,128)(2,1)S(1)}, bf16[32,8,512]{2,1,0:T(8,128)(2,1)S(1)}, u32[]{:S(2)}, u32[]{:S(2)}) collective-permute-start(bf16[32,8,512]{2,1,0:T(8,128)(2,1)S(1)} %collective-permute-done.6.refs_2_), channel_id=1, source_target_pairs={{0,64},{64,128},{128,192},{192,0},{1,65},{65,129},{129,193},{193,1... | collective-permute-start | bytes 786440 | tf_op jit(solution)/shard_map/ppermute | solution.py:249
  119.2 10.6 %collective-permute-start.9 = (bf16[32,8,512]{2,1,0:T(8,128)(2,1)S(1)}, bf16[32,8,512]{2,1,0:T(8,128)(2,1)S(1)}, u32[]{:S(2)}, u32[]{:S(2)}) collective-permute-start(bf16[32,8,512]{2,1,0:T(8,128)(2,1)S(1)} %collective-permute-done.8.refs_3_), channel_id=1, source_target_pairs={{0,192},{64,0},{128,64},{192,128},{1,193},{65,1},{129,65},{193,129... | collective-permute-start | bytes 786440 | tf_op jit(solution)/shard_map/ppermute | solution.py:250

commit v9 on v7

--- a/solution.py
+++ b/solution.py
@@ -66,11 +66,11 @@
     sbs = [s.astype(BF16) for s in ss]
     s2s = [dot(s, s) for s in sbs]
     qs = [
-        -2.4375 * s + 1.6875 * s2 + dot(s2.astype(BF16), (0.0625 * s2 - 0.5625 * s).astype(BF16))
+        -2.4375 * s + 1.6875 * s2 + dot((0.0625 * s2 - 0.5625 * s).astype(BF16), s2.astype(BF16))
         for s, s2 in zip(ss, s2s)
     ]
     zs = [
-        3.375 * identity + 1.5 * q - 1.125 * y - 0.5 * dot(b, q.astype(BF16)) for q, y, b in zip(qs, ys, ybs)
+        3.375 * identity + 1.5 * q - 1.125 * y - 0.5 * dot(q.astype(BF16), b) for q, y, b in zip(qs, ys, ybs)
     ]
     return [z.astype(BF16) for z in zs]
 
@@ -96,10 +96,10 @@
         grads.append(grad)
         norms.append(jnp.sum(wide * wide))
         factors.append(new)
-    for s in range(capacity):
-        root_left, root_right = inverse_roots(factors[s], identity)
-        half = dot(root_left, grads[s]).astype(BF16)
-        raw = dot(half, root_right)
+    roots = inverse_roots([m for pair in factors for m in pair], identity)
+    halves = [dot(left_root, grad).astype(BF16) for left_root, grad in zip(roots[::2], grads)]
+    raws = [dot(half, right_root) for half, right_root in zip(halves, roots[1::2])]
+    for s, raw in enumerate(raws):
         factor = jnp.sqrt(norms[s]) * lax.rsqrt(jnp.sum(raw * raw) + 1e-06)
         out[:, s] = (raw * factor).reshape(out.shape[0], out.shape[2], out.shape[3]).astype(BF16)
     for copy in copies:

time: 131 us -> 130 us (level)
  no operation moved by 1% of the time
where the time goes in v9:
time: 130 us; the launch traced here: 129 us
  blocking collectives  73.6 us (57%)
  waiting for transfers between devices  20.4 us (16%)
  starting transfers between devices  17.8 us (14%)
  Pallas kernels  13.9 us (11%)
  local copies, waits for them, and re-layouts  2.68 us (2%)
    all_to_all x1, blocking collectives, shards(): lax.all_to_all(outgoing, 'fsdp', split_axis=0, concat_axis=0, tiled=True)  39.3 us
    all_to_all x1, blocking collectives, shards(): lax.all_to_all(slot_update, 'fsdp', split_axis=0, concat_axis=0, tiled=True)  34.2 us
    pallas_call x1, Pallas kernels, shards(): pl.pallas_call(owner_kernel, in_specs=[in_vmem, in_vmem, in_vmem], out_sp...  8.94 us
    ppermute x1, waiting for transfers between devices, shards(): left_a = lax.ppermute(mine_a, 'rep', plus)  5.08 us
    ppermute x1, waiting for transfers between devices, shards(): far_a = lax.ppermute(left_a, 'rep', plus)  4.13 us
    ppermute x1, waiting for transfers between devices, shards(): second_a = lax.ppermute(relay(kept_a, relayed_a), 'rep', swap3)  4.09 us
    ppermute x1, starting transfers between devices, shards(): second_a = lax.ppermute(relay(kept_a, relayed_a), 'rep', swap3)  3.75 us
    ppermute x1, starting transfers between devices, shards(): far_b = lax.ppermute(right_b, 'rep', minus)  3.27 us
  transfers between devices with their start and end apart: 12, of which 8 were waited for; matrix products, arithmetic and copies ran while one was open for 0% of the time, Pallas kernels for 2%

profile of v9, /device:TPU:32, one launch (start us, length us, event | category | flops | bytes accessed | tf_op | source)
XLA Modules:
  0.0 129.4 jit_solution(1422551641247001383)
XLA Ops:
  0.6 0.0 copy-start.3
  0.6 1.1 dynamic-slice_bitcast_fusion
  1.7 1.7 %collective-permute-start.2 = (bf16[32,8,512]{2,1,0:T(8,128)(2,1)S(1)}, bf16[32,8,512]{2,1,0:T(8,128)(2,1)S(1)}, u32[]{:S(2)}, u32[]{:S(2)}) collective-permute-start(bf16[32,8,512]{2,1,0:T(8,128)(2,1)S(1)} %get-tuple-element.24), channel_id=1, source_target_pairs={{0,64},{64,0},{128,192},{192,128},{1,65},{65,1},{129,193},{193,129... | collective-permute-start | bytes 786440 | tf_op jit(solution)/shard_map/ppermute | solution.py:169
  3.4 2.2 %collective-permute-start.4 = (bf16[32,8,512]{2,1,0:T(8,128)(2,1)S(1)}, bf16[32,8,512]{2,1,0:T(8,128)(2,1)S(1)}, u32[]{:S(2)}, u32[]{:S(2)}) collective-permute-start(bf16[32,8,512]{2,1,0:T(8,128)(2,1)S(1)} %get-tuple-element.23), channel_id=1, source_target_pairs={{0,192},{64,128},{128,64},{192,0},{1,193},{65,129},{129,65},{193,1... | collective-permute-start | bytes 786440 | tf_op jit(solution)/shard_map/ppermute | solution.py:170
  5.6 0.0 copy-start
  5.6 1.6 %copy-done = bf16[1,256,8,512]{3,2,1,0:T(8,128)(2,1)S(1)} copy-done((bf16[1,256,8,512]{3,2,1,0:T(8,128)(2,1)S(1)}, bf16[1,256,8,512]{3,2,1,0:T(8,128)(2,1)}, u32[]{:S(2)}) %copy-start) | copy-done | bytes 2097176
  7.2 0.2 pick.1
  7.3 0.8 collective-permute-start
  8.1 0.6 collective-permute-start.1
  8.7 0.0 copy-done.3
  8.7 1.6 %collective-permute-done.2.relayed = bf16[32,8,512]{2,1,0:T(8,128)(2,1)S(1)} collective-permute-done((bf16[32,8,512]{2,1,0:T(8,128)(2,1)S(1)}, bf16[32,8,512]{2,1,0:T(8,128)(2,1)S(1)}, u32[]{:S(2)}, u32[]{:S(2)}) %collective-permute-start.2) | collective-permute-done | bytes 262176 | tf_op jit(solution)/shard_map/ppermute | solution.py:169
  10.3 0.1 relay.2
  10.4 3.8 %collective-permute-start.3 = (bf16[32,8,512]{2,1,0:T(8,128)(2,1)S(1)}, bf16[32,8,512]{2,1,0:T(8,128)(2,1)S(1)}, u32[]{:S(2)}, u32[]{:S(2)}) collective-permute-start(bf16[32,8,512]{2,1,0:T(8,128)(2,1)S(1)} %relay.2), channel_id=1, source_target_pairs={{0,192},{64,128},{128,64},{192,0},{1,193},{65,129},{129,65},{193,1... | collective-permute-start | bytes 786440 | tf_op jit(solution)/shard_map/ppermute | solution.py:187
  14.2 0.0 collective-permute-done.4.relayed
  14.2 0.1 relay.3
  14.2 0.2 collective-permute-start.5
  14.5 0.2 convert_reduce_fusion
  14.7 1.8 %collective-permute-done.direct_a = bf16[1,32,8,512]{3,2,1,0:T(8,128)(2,1)S(1)} collective-permute-done((bf16[1,32,8,512]{3,2,1,0:T(8,128)(2,1)S(1)}, bf16[1,32,8,512]{3,2,1,0:T(8,128)(2,1)S(1)}, u32[]{:S(2)}, u32[]{:S(2)}) %collective-permute-start) | collective-permute-done | bytes 262176 | tf_op jit(solution)/shard_map/ppermute | solution.py:174
  16.4 3.0 %collective-permute-done.1.direct_b = bf16[1,32,8,512]{3,2,1,0:T(8,128)(2,1)S(1)} collective-permute-done((bf16[1,32,8,512]{3,2,1,0:T(8,128)(2,1)S(1)}, bf16[1,32,8,512]{3,2,1,0:T(8,128)(2,1)S(1)}, u32[]{:S(2)}, u32[]{:S(2)}) %collective-permute-start.1) | collective-permute-done | bytes 262176 | tf_op jit(solution)/shard_map/ppermute | solution.py:175
  19.4 0.1 presum.1
  19.5 0.0 copy-start.1
  19.5 0.0 copy-start.2
  19.5 4.1 %collective-permute-done.3.second_a = bf16[32,8,512]{2,1,0:T(8,128)(2,1)S(1)} collective-permute-done((bf16[32,8,512]{2,1,0:T(8,128)(2,1)S(1)}, bf16[32,8,512]{2,1,0:T(8,128)(2,1)S(1)}, u32[]{:S(2)}, u32[]{:S(2)}) %collective-permute-start.3) | collective-permute-done | bytes 262176 | tf_op jit(solution)/shard_map/ppermute | solution.py:187
  23.6 0.0 collective-permute-done.5.second_b
  23.6 0.8 pack.1
  24.4 39.3 %all_to_all.10.arrived = bf16[64,2,8,512]{3,2,1,0:T(8,128)(2,1)S(1)} all-to-all(bf16[64,2,8,512]{3,2,1,0:T(8,128)(2,1)S(1)} %bitcast.18), channel_id=1, replica_groups=mesh['rep'=4,'fsdp'=64] {'fsdp'}, dimensions={0} | all-to-all | bytes 2097152 | tf_op jit(solution)/shard_map/all_to_all | solution.py:208
  63.7 0.0 copy-done.1
  63.7 0.0 copy-done.2
  63.7 8.9 %owner.1 = (f32[2,512,512]{2,1,0:T(8,128)}, f32[2,512,512]{2,1,0:T(8,128)}, bf16[64,2,8,512]{3,2,1,0:T(8,128)(2,1)S(1)}) custom-call(bf16[64,2,8,512]{3,2,1,0:T(8,128)(2,1)S(1)} %all_to_all.10.arrived, f32[2,512,512]{2,1,0:T(8,128)S(1)} %bitcast.21, f32[2,512,512]{2,1,0:T(8,128)S(1)} %bitcast.22), custom_call_target="tpu_custom_call" | custom-call | tf_op jit(solution)/shard_map/owner/pallas_call | solution.py:212
  72.6 34.2 %all_to_all.11 = bf16[64,2,8,512]{3,2,1,0:T(8,128)(2,1)S(1)} all-to-all(bf16[64,2,8,512]{3,2,1,0:T(8,128)(2,1)S(1)} %get-tuple-element.18), channel_id=1, replica_groups=mesh['rep'=4,'fsdp'=64] {'fsdp'}, dimensions={0} | all-to-all | bytes 2097152 | tf_op jit(solution)/shard_map/all_to_all | solution.py:226
  106.9 0.6 unpack.1
  107.5 0.1 collective-permute-start.6
  107.6 3.2 %collective-permute-start.8 = (bf16[32,8,512]{2,1,0:T(8,128)(2,1)S(1)}, bf16[32,8,512]{2,1,0:T(8,128)(2,1)S(1)}, u32[]{:S(2)}, u32[]{:S(2)}) collective-permute-start(bf16[32,8,512]{2,1,0:T(8,128)(2,1)S(1)} %get-tuple-element.20.refs_1_), channel_id=1, source_target_pairs={{0,192},{64,0},{128,64},{192,128},{1,193},{65,1},{129,65},{193,129... | collective-permute-start | bytes 786440 | tf_op jit(solution)/shard_map/ppermute | solution.py:244
  110.8 1.0 collective-permute-start.11
  111.8 1.1 collective-permute-start.10
  112.9 5.1 %collective-permute-done.6.refs_2_ = bf16[32,8,512]{2,1,0:T(8,128)(2,1)S(1)} collective-permute-done((bf16[32,8,512]{2,1,0:T(8,128)(2,1)S(1)}, bf16[32,8,512]{2,1,0:T(8,128)(2,1)S(1)}, u32[]{:S(2)}, u32[]{:S(2)}) %collective-permute-start.6) | collective-permute-done | bytes 262176 | tf_op jit(solution)/shard_map/ppermute | solution.py:243
  118.0 0.0 collective-permute-start.7
  118.0 0.0 collective-permute-done.8.refs_3_
  118.0 3.3 %collective-permute-start.9 = (bf16[32,8,512]{2,1,0:T(8,128)(2,1)S(1)}, bf16[32,8,512]{2,1,0:T(8,128)(2,1)S(1)}, u32[]{:S(2)}, u32[]{:S(2)}) collective-permute-start(bf16[32,8,512]{2,1,0:T(8,128)(2,1)S(1)} %collective-permute-done.8.refs_3_), channel_id=1, source_target_pairs={{0,192},{64,0},{128,64},{192,128},{1,193},{65,1},{129,65},{193,129... | collective-permute-start | bytes 786440 | tf_op jit(solution)/shard_map/ppermute | solution.py:248
  121.2 1.6 %place_first.1.refs_2_ = bf16[4,2,32,8,512]{4,3,2,1,0:T(8,128)(2,1)} custom-call(s32[1]{0:T(128)} %bitcast.table, bf16[32,8,512]{2,1,0:T(8,128)(2,1)S(1)} %get-tuple-element.19.refs_0_, bf16[32,8,512]{2,1,0:T(8,128)(2,1)S(1)} %get-tuple-element.20.refs_1_, bf16[32,8,512]{2,1,0:T(8,128)(2,1)S(1)} %collective-permute-done.6.refs_2_, ...), custom_call_target="tpu_custom_call" | custom-call | tf_op jit(solution)/shard_map/place_first/pallas_call | solution.py:261
  122.8 0.4 collective-permute-done.11.refs_1_
  123.2 0.4 collective-permute-done.10.refs_0_
  123.6 0.8 place_second.1.refs_2_
  124.4 4.1 %collective-permute-done.7.refs_0_ = bf16[32,8,512]{2,1,0:T(8,128)(2,1)S(1)} collective-permute-done((bf16[32,8,512]{2,1,0:T(8,128)(2,1)S(1)}, bf16[32,8,512]{2,1,0:T(8,128)(2,1)S(1)}, u32[]{:S(2)}, u32[]{:S(2)}) %collective-permute-start.7) | collective-permute-done | bytes 262176 | tf_op jit(solution)/shard_map/ppermute | solution.py:247
  128.5 0.0 collective-permute-done.9.refs_1_
  128.5 0.8 place_far.1
  (2 shorter events, 0.0 us)
Async XLA Ops:
  0.6 8.1 %copy-start.3 = (s32[4,64,1]{1,2,0:T(1,128)S(1)}, s32[4,64,1]{1,2,0:T(1,128)}, u32[]{:S(2)}) copy-start(s32[4,64,1]{1,2,0:T(1,128)} %param.7) | copy-start | bytes 3076
  1.7 8.6 %collective-permute-start.2 = (bf16[32,8,512]{2,1,0:T(8,128)(2,1)S(1)}, bf16[32,8,512]{2,1,0:T(8,128)(2,1)S(1)}, u32[]{:S(2)}, u32[]{:S(2)}) collective-permute-start(bf16[32,8,512]{2,1,0:T(8,128)(2,1)S(1)} %get-tuple-element.24), channel_id=1, source_target_pairs={{0,64},{64,0},{128,192},{192,128},{1,65},{65,1},{129,193},{193,129... | collective-permute-start | bytes 786440 | tf_op jit(solution)/shard_map/ppermute | solution.py:169
  3.4 10.8 %collective-permute-start.4 = (bf16[32,8,512]{2,1,0:T(8,128)(2,1)S(1)}, bf16[32,8,512]{2,1,0:T(8,128)(2,1)S(1)}, u32[]{:S(2)}, u32[]{:S(2)}) collective-permute-start(bf16[32,8,512]{2,1,0:T(8,128)(2,1)S(1)} %get-tuple-element.23), channel_id=1, source_target_pairs={{0,192},{64,128},{128,64},{192,0},{1,193},{65,129},{129,65},{193,1... | collective-permute-start | bytes 786440 | tf_op jit(solution)/shard_map/ppermute | solution.py:170
  5.6 1.6 %copy-start = (bf16[1,256,8,512]{3,2,1,0:T(8,128)(2,1)S(1)}, bf16[1,256,8,512]{3,2,1,0:T(8,128)(2,1)}, u32[]{:S(2)}) copy-start(bf16[1,256,8,512]{3,2,1,0:T(8,128)(2,1)} %param.4) | copy-start | bytes 6291460
  7.3 9.1 %collective-permute-start = (bf16[1,32,8,512]{3,2,1,0:T(8,128)(2,1)S(1)}, bf16[1,32,8,512]{3,2,1,0:T(8,128)(2,1)S(1)}, u32[]{:S(2)}, u32[]{:S(2)}) collective-permute-start(bf16[1,32,8,512]{3,2,1,0:T(8,128)(2,1)S(1)} %get-tuple-element.14), channel_id=1, source_target_pairs={{0,64},{64,0},{128,192},{192,128},{1,65},{65,1},{129,193},{193,129... | collective-permute-start | bytes 786440 | tf_op jit(solution)/shard_map/ppermute | solution.py:174
  8.1 11.3 %collective-permute-start.1 = (bf16[1,32,8,512]{3,2,1,0:T(8,128)(2,1)S(1)}, bf16[1,32,8,512]{3,2,1,0:T(8,128)(2,1)S(1)}, u32[]{:S(2)}, u32[]{:S(2)}) collective-permute-start(bf16[1,32,8,512]{3,2,1,0:T(8,128)(2,1)S(1)} %get-tuple-element.15), channel_id=1, source_target_pairs={{0,192},{64,128},{128,64},{192,0},{1,193},{65,129},{129,65},{193,1... | collective-permute-start | bytes 786440 | tf_op jit(solution)/shard_map/ppermute | solution.py:175
  10.4 13.2 %collective-permute-start.3 = (bf16[32,8,512]{2,1,0:T(8,128)(2,1)S(1)}, bf16[32,8,512]{2,1,0:T(8,128)(2,1)S(1)}, u32[]{:S(2)}, u32[]{:S(2)}) collective-permute-start(bf16[32,8,512]{2,1,0:T(8,128)(2,1)S(1)} %relay.2), channel_id=1, source_target_pairs={{0,192},{64,128},{128,64},{192,0},{1,193},{65,129},{129,65},{193,1... | collective-permute-start | bytes 786440 | tf_op jit(solution)/shard_map/ppermute | solution.py:187
  14.2 9.4 %collective-permute-start.5 = (bf16[32,8,512]{2,1,0:T(8,128)(2,1)S(1)}, bf16[32,8,512]{2,1,0:T(8,128)(2,1)S(1)}, u32[]{:S(2)}, u32[]{:S(2)}) collective-permute-start(bf16[32,8,512]{2,1,0:T(8,128)(2,1)S(1)} %relay.3), channel_id=1, source_target_pairs={{0,64},{64,0},{128,192},{192,128},{1,65},{65,1},{129,193},{193,129... | collective-permute-start | bytes 786440 | tf_op jit(solution)/shard_map/ppermute | solution.py:188
  19.5 44.2 %copy-start.1 = (f32[1,1,2,512,512]{4,3,2,1,0:T(8,128)S(1)}, f32[1,1,2,512,512]{4,3,2,1,0:T(8,128)}, u32[]{:S(2)}) copy-start(f32[1,1,2,512,512]{4,3,2,1,0:T(8,128)} %param.5) | copy-start | bytes 6291460
  19.5 44.2 %copy-start.2 = (f32[1,1,2,512,512]{4,3,2,1,0:T(8,128)S(1)}, f32[1,1,2,512,512]{4,3,2,1,0:T(8,128)}, u32[]{:S(2)}) copy-start(f32[1,1,2,512,512]{4,3,2,1,0:T(8,128)} %param.6) | copy-start | bytes 6291460
  107.5 10.4 %collective-permute-start.6 = (bf16[32,8,512]{2,1,0:T(8,128)(2,1)S(1)}, bf16[32,8,512]{2,1,0:T(8,128)(2,1)S(1)}, u32[]{:S(2)}, u32[]{:S(2)}) collective-permute-start(bf16[32,8,512]{2,1,0:T(8,128)(2,1)S(1)} %get-tuple-element.19.refs_0_), channel_id=1, source_target_pairs={{0,64},{64,128},{128,192},{192,0},{1,65},{65,129},{129,193},{193,1... | collective-permute-start | bytes 786440 | tf_op jit(solution)/shard_map/ppermute | solution.py:243
  107.6 10.3 %collective-permute-start.8 = (bf16[32,8,512]{2,1,0:T(8,128)(2,1)S(1)}, bf16[32,8,512]{2,1,0:T(8,128)(2,1)S(1)}, u32[]{:S(2)}, u32[]{:S(2)}) collective-permute-start(bf16[32,8,512]{2,1,0:T(8,128)(2,1)S(1)} %get-tuple-element.20.refs_1_), channel_id=1, source_target_pairs={{0,192},{64,0},{128,64},{192,128},{1,193},{65,1},{129,65},{193,129... | collective-permute-start | bytes 786440 | tf_op jit(solution)/shard_map/ppermute | solution.py:244
  110.8 12.3 %collective-permute-start.11 = (bf16[32,8,512]{2,1,0:T(8,128)(2,1)S(1)}, bf16[32,8,512]{2,1,0:T(8,128)(2,1)S(1)}, u32[]{:S(2)}, u32[]{:S(2)}) collective-permute-start(bf16[32,8,512]{2,1,0:T(8,128)(2,1)S(1)} %get-tuple-element.19.refs_0_), channel_id=1, source_target_pairs={{0,192},{64,0},{128,64},{192,128},{1,193},{65,1},{129,65},{193,129... | collective-permute-start | bytes 786440 | tf_op jit(solution)/shard_map/ppermute | solution.py:246
  111.8 11.8 %collective-permute-start.10 = (bf16[32,8,512]{2,1,0:T(8,128)(2,1)S(1)}, bf16[32,8,512]{2,1,0:T(8,128)(2,1)S(1)}, u32[]{:S(2)}, u32[]{:S(2)}) collective-permute-start(bf16[32,8,512]{2,1,0:T(8,128)(2,1)S(1)} %get-tuple-element.20.refs_1_), channel_id=1, source_target_pairs={{0,64},{64,128},{128,192},{192,0},{1,65},{65,129},{129,193},{193,1... | collective-permute-start | bytes 786440 | tf_op jit(solution)/shard_map/ppermute | solution.py:245
  118.0 10.6 %collective-permute-start.7 = (bf16[32,8,512]{2,1,0:T(8,128)(2,1)S(1)}, bf16[32,8,512]{2,1,0:T(8,128)(2,1)S(1)}, u32[]{:S(2)}, u32[]{:S(2)}) collective-permute-start(bf16[32,8,512]{2,1,0:T(8,128)(2,1)S(1)} %collective-permute-done.6.refs_2_), channel_id=1, source_target_pairs={{0,64},{64,128},{128,192},{192,0},{1,65},{65,129},{129,193},{193,1... | collective-permute-start | bytes 786440 | tf_op jit(solution)/shard_map/ppermute | solution.py:247
  118.0 10.6 %collective-permute-start.9 = (bf16[32,8,512]{2,1,0:T(8,128)(2,1)S(1)}, bf16[32,8,512]{2,1,0:T(8,128)(2,1)S(1)}, u32[]{:S(2)}, u32[]{:S(2)}) collective-permute-start(bf16[32,8,512]{2,1,0:T(8,128)(2,1)S(1)} %collective-permute-done.8.refs_3_), channel_id=1, source_target_pairs={{0,192},{64,0},{128,64},{192,128},{1,193},{65,1},{129,65},{193,129... | collective-permute-start | bytes 786440 | tf_op jit(solution)/shard_map/ppermute | solution.py:248

commit v10 on v9

--- a/solution.py
+++ b/solution.py
@@ -59,10 +59,13 @@
 
 
 def inverse_roots(matrices, identity):
-    ys = [m * lax.rsqrt(jnp.sum(m * m) + 1e-06) for m in matrices]
-    ybs = [y.astype(BF16) for y in ys]
+    scales = [lax.rsqrt(jnp.sum(m * m) + 1e-06) for m in matrices]
+    ybs = [(m * c).astype(BF16) for m, c in zip(matrices, scales)]
     y2s = [dot(b, b) for b in ybs]
-    ss = [2.25 * y - 1.5 * y2 + 0.25 * dot(y2.astype(BF16), b) for y, y2, b in zip(ys, y2s, ybs)]
+    ss = [
+        (2.25 * c) * m - 1.5 * y2 + 0.25 * dot(y2.astype(BF16), b)
+        for m, c, y2, b in zip(matrices, scales, y2s, ybs)
+    ]
     sbs = [s.astype(BF16) for s in ss]
     s2s = [dot(s, s) for s in sbs]
     qs = [
@@ -70,7 +73,8 @@
         for s, s2 in zip(ss, s2s)
     ]
     zs = [
-        3.375 * identity + 1.5 * q - 1.125 * y - 0.5 * dot(q.astype(BF16), b) for q, y, b in zip(qs, ys, ybs)
+        3.375 * identity + 1.5 * q - (1.125 * c) * m - 0.5 * dot(q.astype(BF16), b)
+        for q, m, c, b in zip(qs, matrices, scales, ybs)
     ]
     return [z.astype(BF16) for z in zs]
 
@@ -80,28 +84,24 @@
     row = lax.broadcasted_iota(jnp.int32, (n, n), 0)
     col = lax.broadcasted_iota(jnp.int32, (n, n), 1)
     identity = (row == col).astype(F32)
-    copies, grads, norms, factors = [], [], [], []
-    for s in range(capacity):
-        wide = arrived[:, s].astype(F32).reshape(n, n)
-        grad = wide.astype(BF16)
-        turned = grad.T
-        new = (
-            0.9 * left[s] + 0.1 * dot(grad, grad, 1, 1),
-            0.9 * right[s] + 0.1 * dot(turned, turned, 1, 1),
-        )
-        for k, (held, target) in enumerate(((held_left, new_left), (held_right, new_right))):
-            held[s] = new[k]
-            copies.append(pltpu.make_async_copy(held.at[s], target.at[s], sems.at[2 * s + k]))
-            copies[-1].start()
-        grads.append(grad)
-        norms.append(jnp.sum(wide * wide))
-        factors.append(new)
-    roots = inverse_roots([m for pair in factors for m in pair], identity)
-    halves = [dot(left_root, grad).astype(BF16) for left_root, grad in zip(roots[::2], grads)]
-    raws = [dot(half, right_root) for half, right_root in zip(halves, roots[1::2])]
+    wides = [arrived[:, s].astype(F32).reshape(n, n) for s in range(capacity)]
+    grads = [wide.astype(BF16) for wide in wides]
+    norms = [jnp.sum(wide * wide) for wide in wides]
+    turned = [grad.T for grad in grads]
+    grams = [dot(g, g, 1, 1) for pair in zip(grads, turned) for g in pair]
+    factors = [0.9 * (left, right)[k % 2][k // 2] + 0.1 * gram for k, gram in enumerate(grams)]
+    copies = []
+    for k, factor in enumerate(factors):
+        held, target = ((held_left, new_left), (held_right, new_right))[k % 2]
+        held[k // 2] = factor
+        copies.append(pltpu.make_async_copy(held.at[k // 2], target.at[k // 2], sems.at[k]))
+        copies[-1].start()
+    roots = inverse_roots(factors, identity)
+    halves = [dot(root_left, grad).astype(BF16) for root_left, grad in zip(roots[::2], grads)]
+    raws = [dot(half, root_right) for half, root_right in zip(halves, roots[1::2])]
     for s, raw in enumerate(raws):
-        factor = jnp.sqrt(norms[s]) * lax.rsqrt(jnp.sum(raw * raw) + 1e-06)
-        out[:, s] = (raw * factor).reshape(out.shape[0], out.shape[2], out.shape[3]).astype(BF16)
+        scale = jnp.sqrt(norms[s]) * lax.rsqrt(jnp.sum(raw * raw) + 1e-06)
+        out[:, s] = (raw * scale).reshape(out.shape[0], out.shape[2], out.shape[3]).astype(BF16)
     for copy in copies:
         copy.wait()
 

time: 130 us -> 130 us (level)
  no operation moved by 1% of the time
where the time goes in v10:
time: 130 us; the launch traced here: 129 us
  blocking collectives  73.6 us (57%)
  waiting for transfers between devices  20.4 us (16%)
  starting transfers between devices  17.8 us (14%)
  Pallas kernels  13.9 us (11%)
  local copies, waits for them, and re-layouts  2.68 us (2%)
    all_to_all x1, blocking collectives, shards(): lax.all_to_all(outgoing, 'fsdp', split_axis=0, concat_axis=0, tiled=True)  39.3 us
    all_to_all x1, blocking collectives, shards(): lax.all_to_all(slot_update, 'fsdp', split_axis=0, concat_axis=0, tiled=True)  34.2 us
    pallas_call x1, Pallas kernels, shards(): pl.pallas_call(owner_kernel, in_specs=[in_vmem, in_vmem, in_vmem], out_sp...  8.88 us
    ppermute x1, waiting for transfers between devices, shards(): left_a = lax.ppermute(mine_a, 'rep', plus)  5.08 us
    ppermute x1, waiting for transfers between devices, shards(): far_a = lax.ppermute(left_a, 'rep', plus)  4.13 us
    ppermute x1, waiting for transfers between devices, shards(): second_a = lax.ppermute(relay(kept_a, relayed_a), 'rep', swap3)  4.09 us
    ppermute x1, starting transfers between devices, shards(): second_a = lax.ppermute(relay(kept_a, relayed_a), 'rep', swap3)  3.75 us
    ppermute x1, starting transfers between devices, shards(): far_b = lax.ppermute(right_b, 'rep', minus)  3.27 us
  transfers between devices with their start and end apart: 12, of which 8 were waited for; matrix products, arithmetic and copies ran while one was open for 0% of the time, Pallas kernels for 2%

profile of v10, /device:TPU:32, one launch (start us, length us, event | category | flops | bytes accessed | tf_op | source)
XLA Modules:
  0.0 129.3 jit_solution(6168067129986426646)
XLA Ops:
  0.6 0.0 copy-start.3
  0.6 1.1 dynamic-slice_bitcast_fusion
  1.7 1.7 %collective-permute-start.2 = (bf16[32,8,512]{2,1,0:T(8,128)(2,1)S(1)}, bf16[32,8,512]{2,1,0:T(8,128)(2,1)S(1)}, u32[]{:S(2)}, u32[]{:S(2)}) collective-permute-start(bf16[32,8,512]{2,1,0:T(8,128)(2,1)S(1)} %get-tuple-element.24), channel_id=1, source_target_pairs={{0,64},{64,0},{128,192},{192,128},{1,65},{65,1},{129,193},{193,129... | collective-permute-start | bytes 786440 | tf_op jit(solution)/shard_map/ppermute | solution.py:169
  3.4 2.2 %collective-permute-start.4 = (bf16[32,8,512]{2,1,0:T(8,128)(2,1)S(1)}, bf16[32,8,512]{2,1,0:T(8,128)(2,1)S(1)}, u32[]{:S(2)}, u32[]{:S(2)}) collective-permute-start(bf16[32,8,512]{2,1,0:T(8,128)(2,1)S(1)} %get-tuple-element.23), channel_id=1, source_target_pairs={{0,192},{64,128},{128,64},{192,0},{1,193},{65,129},{129,65},{193,1... | collective-permute-start | bytes 786440 | tf_op jit(solution)/shard_map/ppermute | solution.py:170
  5.6 0.0 copy-start
  5.6 1.6 %copy-done = bf16[1,256,8,512]{3,2,1,0:T(8,128)(2,1)S(1)} copy-done((bf16[1,256,8,512]{3,2,1,0:T(8,128)(2,1)S(1)}, bf16[1,256,8,512]{3,2,1,0:T(8,128)(2,1)}, u32[]{:S(2)}) %copy-start) | copy-done | bytes 2097176
  7.2 0.2 pick.1
  7.3 0.8 collective-permute-start
  8.1 0.6 collective-permute-start.1
  8.7 0.0 copy-done.3
  8.7 1.6 %collective-permute-done.2.relayed = bf16[32,8,512]{2,1,0:T(8,128)(2,1)S(1)} collective-permute-done((bf16[32,8,512]{2,1,0:T(8,128)(2,1)S(1)}, bf16[32,8,512]{2,1,0:T(8,128)(2,1)S(1)}, u32[]{:S(2)}, u32[]{:S(2)}) %collective-permute-start.2) | collective-permute-done | bytes 262176 | tf_op jit(solution)/shard_map/ppermute | solution.py:169
  10.3 0.1 relay.2
  10.4 3.8 %collective-permute-start.3 = (bf16[32,8,512]{2,1,0:T(8,128)(2,1)S(1)}, bf16[32,8,512]{2,1,0:T(8,128)(2,1)S(1)}, u32[]{:S(2)}, u32[]{:S(2)}) collective-permute-start(bf16[32,8,512]{2,1,0:T(8,128)(2,1)S(1)} %relay.2), channel_id=1, source_target_pairs={{0,192},{64,128},{128,64},{192,0},{1,193},{65,129},{129,65},{193,1... | collective-permute-start | bytes 786440 | tf_op jit(solution)/shard_map/ppermute | solution.py:187
  14.2 0.0 collective-permute-done.4.relayed
  14.2 0.1 relay.3
  14.2 0.2 collective-permute-start.5
  14.5 0.2 convert_reduce_fusion
  14.7 1.8 %collective-permute-done.direct_a = bf16[1,32,8,512]{3,2,1,0:T(8,128)(2,1)S(1)} collective-permute-done((bf16[1,32,8,512]{3,2,1,0:T(8,128)(2,1)S(1)}, bf16[1,32,8,512]{3,2,1,0:T(8,128)(2,1)S(1)}, u32[]{:S(2)}, u32[]{:S(2)}) %collective-permute-start) | collective-permute-done | bytes 262176 | tf_op jit(solution)/shard_map/ppermute | solution.py:174
  16.4 3.0 %collective-permute-done.1.direct_b = bf16[1,32,8,512]{3,2,1,0:T(8,128)(2,1)S(1)} collective-permute-done((bf16[1,32,8,512]{3,2,1,0:T(8,128)(2,1)S(1)}, bf16[1,32,8,512]{3,2,1,0:T(8,128)(2,1)S(1)}, u32[]{:S(2)}, u32[]{:S(2)}) %collective-permute-start.1) | collective-permute-done | bytes 262176 | tf_op jit(solution)/shard_map/ppermute | solution.py:175
  19.4 0.1 presum.1
  19.5 0.0 copy-start.1
  19.5 0.0 copy-start.2
  19.5 4.1 %collective-permute-done.3.second_a = bf16[32,8,512]{2,1,0:T(8,128)(2,1)S(1)} collective-permute-done((bf16[32,8,512]{2,1,0:T(8,128)(2,1)S(1)}, bf16[32,8,512]{2,1,0:T(8,128)(2,1)S(1)}, u32[]{:S(2)}, u32[]{:S(2)}) %collective-permute-start.3) | collective-permute-done | bytes 262176 | tf_op jit(solution)/shard_map/ppermute | solution.py:187
  23.6 0.0 collective-permute-done.5.second_b
  23.6 0.8 pack.1
  24.4 39.3 %all_to_all.10.arrived = bf16[64,2,8,512]{3,2,1,0:T(8,128)(2,1)S(1)} all-to-all(bf16[64,2,8,512]{3,2,1,0:T(8,128)(2,1)S(1)} %bitcast.18), channel_id=1, replica_groups=mesh['rep'=4,'fsdp'=64] {'fsdp'}, dimensions={0} | all-to-all | bytes 2097152 | tf_op jit(solution)/shard_map/all_to_all | solution.py:208
  63.7 0.0 copy-done.1
  63.7 0.0 copy-done.2
  63.7 8.9 %owner.1 = (f32[2,512,512]{2,1,0:T(8,128)}, f32[2,512,512]{2,1,0:T(8,128)}, bf16[64,2,8,512]{3,2,1,0:T(8,128)(2,1)S(1)}) custom-call(bf16[64,2,8,512]{3,2,1,0:T(8,128)(2,1)S(1)} %all_to_all.10.arrived, f32[2,512,512]{2,1,0:T(8,128)S(1)} %bitcast.21, f32[2,512,512]{2,1,0:T(8,128)S(1)} %bitcast.22), custom_call_target="tpu_custom_call" | custom-call | tf_op jit(solution)/shard_map/owner/pallas_call | solution.py:212
  72.6 34.2 %all_to_all.11 = bf16[64,2,8,512]{3,2,1,0:T(8,128)(2,1)S(1)} all-to-all(bf16[64,2,8,512]{3,2,1,0:T(8,128)(2,1)S(1)} %get-tuple-element.18), channel_id=1, replica_groups=mesh['rep'=4,'fsdp'=64] {'fsdp'}, dimensions={0} | all-to-all | bytes 2097152 | tf_op jit(solution)/shard_map/all_to_all | solution.py:226
  106.8 0.6 unpack.1
  107.5 0.1 collective-permute-start.6
  107.6 3.2 %collective-permute-start.8 = (bf16[32,8,512]{2,1,0:T(8,128)(2,1)S(1)}, bf16[32,8,512]{2,1,0:T(8,128)(2,1)S(1)}, u32[]{:S(2)}, u32[]{:S(2)}) collective-permute-start(bf16[32,8,512]{2,1,0:T(8,128)(2,1)S(1)} %get-tuple-element.20.refs_1_), channel_id=1, source_target_pairs={{0,192},{64,0},{128,64},{192,128},{1,193},{65,1},{129,65},{193,129... | collective-permute-start | bytes 786440 | tf_op jit(solution)/shard_map/ppermute | solution.py:244
  110.8 1.0 collective-permute-start.11
  111.8 1.0 collective-permute-start.10
  112.8 5.1 %collective-permute-done.6.refs_2_ = bf16[32,8,512]{2,1,0:T(8,128)(2,1)S(1)} collective-permute-done((bf16[32,8,512]{2,1,0:T(8,128)(2,1)S(1)}, bf16[32,8,512]{2,1,0:T(8,128)(2,1)S(1)}, u32[]{:S(2)}, u32[]{:S(2)}) %collective-permute-start.6) | collective-permute-done | bytes 262176 | tf_op jit(solution)/shard_map/ppermute | solution.py:243
  117.9 0.0 collective-permute-start.7
  117.9 0.0 collective-permute-done.8.refs_3_
  117.9 3.3 %collective-permute-start.9 = (bf16[32,8,512]{2,1,0:T(8,128)(2,1)S(1)}, bf16[32,8,512]{2,1,0:T(8,128)(2,1)S(1)}, u32[]{:S(2)}, u32[]{:S(2)}) collective-permute-start(bf16[32,8,512]{2,1,0:T(8,128)(2,1)S(1)} %collective-permute-done.8.refs_3_), channel_id=1, source_target_pairs={{0,192},{64,0},{128,64},{192,128},{1,193},{65,1},{129,65},{193,129... | collective-permute-start | bytes 786440 | tf_op jit(solution)/shard_map/ppermute | solution.py:248
  121.2 1.6 %place_first.1.refs_2_ = bf16[4,2,32,8,512]{4,3,2,1,0:T(8,128)(2,1)} custom-call(s32[1]{0:T(128)} %bitcast.table, bf16[32,8,512]{2,1,0:T(8,128)(2,1)S(1)} %get-tuple-element.19.refs_0_, bf16[32,8,512]{2,1,0:T(8,128)(2,1)S(1)} %get-tuple-element.20.refs_1_, bf16[32,8,512]{2,1,0:T(8,128)(2,1)S(1)} %collective-permute-done.6.refs_2_, ...), custom_call_target="tpu_custom_call" | custom-call | tf_op jit(solution)/shard_map/place_first/pallas_call | solution.py:261
  122.7 0.4 collective-permute-done.11.refs_1_
  123.1 0.4 collective-permute-done.10.refs_0_
  123.5 0.8 place_second.1.refs_2_
  124.3 4.1 %collective-permute-done.7.refs_0_ = bf16[32,8,512]{2,1,0:T(8,128)(2,1)S(1)} collective-permute-done((bf16[32,8,512]{2,1,0:T(8,128)(2,1)S(1)}, bf16[32,8,512]{2,1,0:T(8,128)(2,1)S(1)}, u32[]{:S(2)}, u32[]{:S(2)}) %collective-permute-start.7) | collective-permute-done | bytes 262176 | tf_op jit(solution)/shard_map/ppermute | solution.py:247
  128.4 0.0 collective-permute-done.9.refs_1_
  128.5 0.8 place_far.1
  (2 shorter events, 0.0 us)
Async XLA Ops:
  0.6 8.1 %copy-start.3 = (s32[4,64,1]{1,2,0:T(1,128)S(1)}, s32[4,64,1]{1,2,0:T(1,128)}, u32[]{:S(2)}) copy-start(s32[4,64,1]{1,2,0:T(1,128)} %param.7) | copy-start | bytes 3076
  1.7 8.6 %collective-permute-start.2 = (bf16[32,8,512]{2,1,0:T(8,128)(2,1)S(1)}, bf16[32,8,512]{2,1,0:T(8,128)(2,1)S(1)}, u32[]{:S(2)}, u32[]{:S(2)}) collective-permute-start(bf16[32,8,512]{2,1,0:T(8,128)(2,1)S(1)} %get-tuple-element.24), channel_id=1, source_target_pairs={{0,64},{64,0},{128,192},{192,128},{1,65},{65,1},{129,193},{193,129... | collective-permute-start | bytes 786440 | tf_op jit(solution)/shard_map/ppermute | solution.py:169
  3.4 10.8 %collective-permute-start.4 = (bf16[32,8,512]{2,1,0:T(8,128)(2,1)S(1)}, bf16[32,8,512]{2,1,0:T(8,128)(2,1)S(1)}, u32[]{:S(2)}, u32[]{:S(2)}) collective-permute-start(bf16[32,8,512]{2,1,0:T(8,128)(2,1)S(1)} %get-tuple-element.23), channel_id=1, source_target_pairs={{0,192},{64,128},{128,64},{192,0},{1,193},{65,129},{129,65},{193,1... | collective-permute-start | bytes 786440 | tf_op jit(solution)/shard_map/ppermute | solution.py:170
  5.6 1.6 %copy-start = (bf16[1,256,8,512]{3,2,1,0:T(8,128)(2,1)S(1)}, bf16[1,256,8,512]{3,2,1,0:T(8,128)(2,1)}, u32[]{:S(2)}) copy-start(bf16[1,256,8,512]{3,2,1,0:T(8,128)(2,1)} %param.4) | copy-start | bytes 6291460
  7.3 9.1 %collective-permute-start = (bf16[1,32,8,512]{3,2,1,0:T(8,128)(2,1)S(1)}, bf16[1,32,8,512]{3,2,1,0:T(8,128)(2,1)S(1)}, u32[]{:S(2)}, u32[]{:S(2)}) collective-permute-start(bf16[1,32,8,512]{3,2,1,0:T(8,128)(2,1)S(1)} %get-tuple-element.14), channel_id=1, source_target_pairs={{0,64},{64,0},{128,192},{192,128},{1,65},{65,1},{129,193},{193,129... | collective-permute-start | bytes 786440 | tf_op jit(solution)/shard_map/ppermute | solution.py:174
  8.1 11.3 %collective-permute-start.1 = (bf16[1,32,8,512]{3,2,1,0:T(8,128)(2,1)S(1)}, bf16[1,32,8,512]{3,2,1,0:T(8,128)(2,1)S(1)}, u32[]{:S(2)}, u32[]{:S(2)}) collective-permute-start(bf16[1,32,8,512]{3,2,1,0:T(8,128)(2,1)S(1)} %get-tuple-element.15), channel_id=1, source_target_pairs={{0,192},{64,128},{128,64},{192,0},{1,193},{65,129},{129,65},{193,1... | collective-permute-start | bytes 786440 | tf_op jit(solution)/shard_map/ppermute | solution.py:175
  10.4 13.2 %collective-permute-start.3 = (bf16[32,8,512]{2,1,0:T(8,128)(2,1)S(1)}, bf16[32,8,512]{2,1,0:T(8,128)(2,1)S(1)}, u32[]{:S(2)}, u32[]{:S(2)}) collective-permute-start(bf16[32,8,512]{2,1,0:T(8,128)(2,1)S(1)} %relay.2), channel_id=1, source_target_pairs={{0,192},{64,128},{128,64},{192,0},{1,193},{65,129},{129,65},{193,1... | collective-permute-start | bytes 786440 | tf_op jit(solution)/shard_map/ppermute | solution.py:187
  14.2 9.4 %collective-permute-start.5 = (bf16[32,8,512]{2,1,0:T(8,128)(2,1)S(1)}, bf16[32,8,512]{2,1,0:T(8,128)(2,1)S(1)}, u32[]{:S(2)}, u32[]{:S(2)}) collective-permute-start(bf16[32,8,512]{2,1,0:T(8,128)(2,1)S(1)} %relay.3), channel_id=1, source_target_pairs={{0,64},{64,0},{128,192},{192,128},{1,65},{65,1},{129,193},{193,129... | collective-permute-start | bytes 786440 | tf_op jit(solution)/shard_map/ppermute | solution.py:188
  19.5 44.2 %copy-start.1 = (f32[1,1,2,512,512]{4,3,2,1,0:T(8,128)S(1)}, f32[1,1,2,512,512]{4,3,2,1,0:T(8,128)}, u32[]{:S(2)}) copy-start(f32[1,1,2,512,512]{4,3,2,1,0:T(8,128)} %param.5) | copy-start | bytes 6291460
  19.5 44.2 %copy-start.2 = (f32[1,1,2,512,512]{4,3,2,1,0:T(8,128)S(1)}, f32[1,1,2,512,512]{4,3,2,1,0:T(8,128)}, u32[]{:S(2)}) copy-start(f32[1,1,2,512,512]{4,3,2,1,0:T(8,128)} %param.6) | copy-start | bytes 6291460
  107.5 10.4 %collective-permute-start.6 = (bf16[32,8,512]{2,1,0:T(8,128)(2,1)S(1)}, bf16[32,8,512]{2,1,0:T(8,128)(2,1)S(1)}, u32[]{:S(2)}, u32[]{:S(2)}) collective-permute-start(bf16[32,8,512]{2,1,0:T(8,128)(2,1)S(1)} %get-tuple-element.19.refs_0_), channel_id=1, source_target_pairs={{0,64},{64,128},{128,192},{192,0},{1,65},{65,129},{129,193},{193,1... | collective-permute-start | bytes 786440 | tf_op jit(solution)/shard_map/ppermute | solution.py:243
  107.6 10.3 %collective-permute-start.8 = (bf16[32,8,512]{2,1,0:T(8,128)(2,1)S(1)}, bf16[32,8,512]{2,1,0:T(8,128)(2,1)S(1)}, u32[]{:S(2)}, u32[]{:S(2)}) collective-permute-start(bf16[32,8,512]{2,1,0:T(8,128)(2,1)S(1)} %get-tuple-element.20.refs_1_), channel_id=1, source_target_pairs={{0,192},{64,0},{128,64},{192,128},{1,193},{65,1},{129,65},{193,129... | collective-permute-start | bytes 786440 | tf_op jit(solution)/shard_map/ppermute | solution.py:244
  110.8 12.3 %collective-permute-start.11 = (bf16[32,8,512]{2,1,0:T(8,128)(2,1)S(1)}, bf16[32,8,512]{2,1,0:T(8,128)(2,1)S(1)}, u32[]{:S(2)}, u32[]{:S(2)}) collective-permute-start(bf16[32,8,512]{2,1,0:T(8,128)(2,1)S(1)} %get-tuple-element.19.refs_0_), channel_id=1, source_target_pairs={{0,192},{64,0},{128,64},{192,128},{1,193},{65,1},{129,65},{193,129... | collective-permute-start | bytes 786440 | tf_op jit(solution)/shard_map/ppermute | solution.py:246
  111.8 11.7 %collective-permute-start.10 = (bf16[32,8,512]{2,1,0:T(8,128)(2,1)S(1)}, bf16[32,8,512]{2,1,0:T(8,128)(2,1)S(1)}, u32[]{:S(2)}, u32[]{:S(2)}) collective-permute-start(bf16[32,8,512]{2,1,0:T(8,128)(2,1)S(1)} %get-tuple-element.20.refs_1_), channel_id=1, source_target_pairs={{0,64},{64,128},{128,192},{192,0},{1,65},{65,129},{129,193},{193,1... | collective-permute-start | bytes 786440 | tf_op jit(solution)/shard_map/ppermute | solution.py:245
  117.9 10.6 %collective-permute-start.7 = (bf16[32,8,512]{2,1,0:T(8,128)(2,1)S(1)}, bf16[32,8,512]{2,1,0:T(8,128)(2,1)S(1)}, u32[]{:S(2)}, u32[]{:S(2)}) collective-permute-start(bf16[32,8,512]{2,1,0:T(8,128)(2,1)S(1)} %collective-permute-done.6.refs_2_), channel_id=1, source_target_pairs={{0,64},{64,128},{128,192},{192,0},{1,65},{65,129},{129,193},{193,1... | collective-permute-start | bytes 786440 | tf_op jit(solution)/shard_map/ppermute | solution.py:247
  117.9 10.6 %collective-permute-start.9 = (bf16[32,8,512]{2,1,0:T(8,128)(2,1)S(1)}, bf16[32,8,512]{2,1,0:T(8,128)(2,1)S(1)}, u32[]{:S(2)}, u32[]{:S(2)}) collective-permute-start(bf16[32,8,512]{2,1,0:T(8,128)(2,1)S(1)} %collective-permute-done.8.refs_3_), channel_id=1, source_target_pairs={{0,192},{64,0},{128,64},{192,128},{1,193},{65,1},{129,65},{193,129... | collective-permute-start | bytes 786440 | tf_op jit(solution)/shard_map/ppermute | solution.py:248

commit v11 on v10

--- a/solution.py
+++ b/solution.py
@@ -238,14 +238,12 @@
         name="unpack",
     )(slot_of, returned.reshape(fsdp * capacity, rows, width))
 
-    plus = [(i, (i + 1) % reps) for i in range(reps)]
-    minus = [(i, (i - 1) % reps) for i in range(reps)]
-    left_a = lax.ppermute(mine_a, "rep", plus)
-    right_b = lax.ppermute(mine_b, "rep", minus)
-    left_b = lax.ppermute(mine_b, "rep", plus)
-    right_a = lax.ppermute(mine_a, "rep", minus)
-    far_a = lax.ppermute(left_a, "rep", plus)
-    far_b = lax.ppermute(right_b, "rep", minus)
+    near1_a = lax.ppermute(mine_a, "rep", swap1)
+    near3_b = lax.ppermute(mine_b, "rep", swap3)
+    near1_b = lax.ppermute(mine_b, "rep", swap1)
+    near3_a = lax.ppermute(mine_a, "rep", swap3)
+    far_b = lax.ppermute(near3_b, "rep", swap1)
+    far_a = lax.ppermute(near1_a, "rep", swap3)
     update_shape = jax.ShapeDtypeStruct((reps, 2, half, rows, width), BF16)
 
     def place(name, turns, halves, steps, values, before=None):
@@ -256,7 +254,7 @@
             turn, first = turns[-1], halves[-1]
             for k in range(len(steps) - 1):
                 turn, first = jnp.where(i == k, turns[k], turn), jnp.where(i == k, halves[k], first)
-            return lax.rem(t[0] + turn, reps), first, 0, 0, 0
+            return t[0] ^ turn, first, 0, 0, 0
 
         return pl.pallas_call(
             functools.partial(place_kernel, steps),
@@ -273,8 +271,8 @@
         )(r[None], *values, *held)
 
     singles = [(0,), (1,), (2,), (3,)]
-    update = place("place_first", [0, 0, 3, 1], [0, 1, 0, 1], singles, [mine_a, mine_b, left_a, right_b])
-    update = place("place_second", [3, 1], [1, 0], singles[:2], [left_b, right_a], update)
+    update = place("place_first", [0, 0, 1, 3], [0, 1, 0, 1], singles, [mine_a, mine_b, near1_a, near3_b])
+    update = place("place_second", [1, 3], [1, 0], singles[:2], [near1_b, near3_a], update)
     update = place("place_far", [2], [0], [(0, 1)], [far_a, far_b], update)
     return (update.reshape(reps * per_row, rows, width), new_left[None, None], new_right[None, None])
 

time: 130 us -> 130 us (level)
  waiting for transfers between devices: 20.4 us -> 22.8 us
  starting transfers between devices: 17.8 us -> 15.5 us
    ppermute x6, waiting for transfers between devices: 9.99 us -> 12.4 us  [the longest x1 5.08 us: shards(): near1_a = lax.ppermute(mine_a, 'rep', swap1)]
    ppermute x6, starting transfers between devices: 8.61 us -> 6.33 us  [the longest x1 2.28 us: shards(): near3_b = lax.ppermute(mine_b, 'rep', swap3)]
  transfers between devices with their start and end apart: 12 -> 12, of which waited for: 8 -> 7; matrix products, arithmetic and copies ran while one was open for 0% -> 0% of each run, Pallas kernels for 2% -> 2%
where the time goes in v11:
time: 130 us; the launch traced here: 129 us
  blocking collectives  73.6 us (57%)
  waiting for transfers between devices  22.8 us (18%)
  starting transfers between devices  15.5 us (12%)
  Pallas kernels  13.9 us (11%)
  local copies, waits for them, and re-layouts  2.68 us (2%)
    all_to_all x1, blocking collectives, shards(): lax.all_to_all(outgoing, 'fsdp', split_axis=0, concat_axis=0, tiled=True)  39.3 us
    all_to_all x1, blocking collectives, shards(): lax.all_to_all(slot_update, 'fsdp', split_axis=0, concat_axis=0, tiled=True)  34.2 us
    pallas_call x1, Pallas kernels, shards(): pl.pallas_call(owner_kernel, in_specs=[in_vmem, in_vmem, in_vmem], out_sp...  8.88 us
    ppermute x1, waiting for transfers between devices, shards(): near1_a = lax.ppermute(mine_a, 'rep', swap1)  5.08 us
    ppermute x1, waiting for transfers between devices, shards(): far_a = lax.ppermute(near1_a, 'rep', swap3)  4.12 us
    ppermute x1, waiting for transfers between devices, shards(): second_a = lax.ppermute(relay(kept_a, relayed_a), 'rep', swap3)  4.09 us
    ppermute x1, starting transfers between devices, shards(): second_a = lax.ppermute(relay(kept_a, relayed_a), 'rep', swap3)  3.75 us
    pallas_call x3, Pallas kernels, place(): pl.pallas_call(functools.partial(place_kernel, steps), out_shape=update_s...  3.19 us
  transfers between devices with their start and end apart: 12, of which 7 were waited for; matrix products, arithmetic and copies ran while one was open for 0% of the time, Pallas kernels for 2%

profile of v11, /device:TPU:32, one launch (start us, length us, event | category | flops | bytes accessed | tf_op | source)
XLA Modules:
  0.0 129.4 jit_solution(11238340321035949224)
XLA Ops:
  0.6 0.0 copy-start.3
  0.6 1.1 dynamic-slice_bitcast_fusion
  1.7 1.7 %collective-permute-start.2 = (bf16[32,8,512]{2,1,0:T(8,128)(2,1)S(1)}, bf16[32,8,512]{2,1,0:T(8,128)(2,1)S(1)}, u32[]{:S(2)}, u32[]{:S(2)}) collective-permute-start(bf16[32,8,512]{2,1,0:T(8,128)(2,1)S(1)} %get-tuple-element.24), channel_id=1, source_target_pairs={{0,64},{64,0},{128,192},{192,128},{1,65},{65,1},{129,193},{193,129... | collective-permute-start | bytes 786440 | tf_op jit(solution)/shard_map/ppermute | solution.py:169
  3.4 2.2 %collective-permute-start.4 = (bf16[32,8,512]{2,1,0:T(8,128)(2,1)S(1)}, bf16[32,8,512]{2,1,0:T(8,128)(2,1)S(1)}, u32[]{:S(2)}, u32[]{:S(2)}) collective-permute-start(bf16[32,8,512]{2,1,0:T(8,128)(2,1)S(1)} %get-tuple-element.23), channel_id=1, source_target_pairs={{0,192},{64,128},{128,64},{192,0},{1,193},{65,129},{129,65},{193,1... | collective-permute-start | bytes 786440 | tf_op jit(solution)/shard_map/ppermute | solution.py:170
  5.6 0.0 copy-start
  5.6 1.6 %copy-done = bf16[1,256,8,512]{3,2,1,0:T(8,128)(2,1)S(1)} copy-done((bf16[1,256,8,512]{3,2,1,0:T(8,128)(2,1)S(1)}, bf16[1,256,8,512]{3,2,1,0:T(8,128)(2,1)}, u32[]{:S(2)}) %copy-start) | copy-done | bytes 2097176
  7.2 0.2 pick.1
  7.3 0.8 collective-permute-start
  8.1 0.6 collective-permute-start.1
  8.7 0.0 copy-done.3
  8.7 1.6 %collective-permute-done.2.relayed = bf16[32,8,512]{2,1,0:T(8,128)(2,1)S(1)} collective-permute-done((bf16[32,8,512]{2,1,0:T(8,128)(2,1)S(1)}, bf16[32,8,512]{2,1,0:T(8,128)(2,1)S(1)}, u32[]{:S(2)}, u32[]{:S(2)}) %collective-permute-start.2) | collective-permute-done | bytes 262176 | tf_op jit(solution)/shard_map/ppermute | solution.py:169
  10.3 0.1 relay.2
  10.4 3.8 %collective-permute-start.3 = (bf16[32,8,512]{2,1,0:T(8,128)(2,1)S(1)}, bf16[32,8,512]{2,1,0:T(8,128)(2,1)S(1)}, u32[]{:S(2)}, u32[]{:S(2)}) collective-permute-start(bf16[32,8,512]{2,1,0:T(8,128)(2,1)S(1)} %relay.2), channel_id=1, source_target_pairs={{0,192},{64,128},{128,64},{192,0},{1,193},{65,129},{129,65},{193,1... | collective-permute-start | bytes 786440 | tf_op jit(solution)/shard_map/ppermute | solution.py:187
  14.2 0.0 collective-permute-done.4.relayed
  14.2 0.1 relay.3
  14.2 0.2 collective-permute-start.5
  14.5 0.2 convert_reduce_fusion
  14.7 1.8 %collective-permute-done.direct_a = bf16[1,32,8,512]{3,2,1,0:T(8,128)(2,1)S(1)} collective-permute-done((bf16[1,32,8,512]{3,2,1,0:T(8,128)(2,1)S(1)}, bf16[1,32,8,512]{3,2,1,0:T(8,128)(2,1)S(1)}, u32[]{:S(2)}, u32[]{:S(2)}) %collective-permute-start) | collective-permute-done | bytes 262176 | tf_op jit(solution)/shard_map/ppermute | solution.py:174
  16.4 3.0 %collective-permute-done.1.direct_b = bf16[1,32,8,512]{3,2,1,0:T(8,128)(2,1)S(1)} collective-permute-done((bf16[1,32,8,512]{3,2,1,0:T(8,128)(2,1)S(1)}, bf16[1,32,8,512]{3,2,1,0:T(8,128)(2,1)S(1)}, u32[]{:S(2)}, u32[]{:S(2)}) %collective-permute-start.1) | collective-permute-done | bytes 262176 | tf_op jit(solution)/shard_map/ppermute | solution.py:175
  19.4 0.1 presum.1
  19.5 0.0 copy-start.1
  19.5 0.0 copy-start.2
  19.5 4.1 %collective-permute-done.3.second_a = bf16[32,8,512]{2,1,0:T(8,128)(2,1)S(1)} collective-permute-done((bf16[32,8,512]{2,1,0:T(8,128)(2,1)S(1)}, bf16[32,8,512]{2,1,0:T(8,128)(2,1)S(1)}, u32[]{:S(2)}, u32[]{:S(2)}) %collective-permute-start.3) | collective-permute-done | bytes 262176 | tf_op jit(solution)/shard_map/ppermute | solution.py:187
  23.6 0.0 collective-permute-done.5.second_b
  23.6 0.8 pack.1
  24.4 39.3 %all_to_all.10.arrived = bf16[64,2,8,512]{3,2,1,0:T(8,128)(2,1)S(1)} all-to-all(bf16[64,2,8,512]{3,2,1,0:T(8,128)(2,1)S(1)} %bitcast.18), channel_id=1, replica_groups=mesh['rep'=4,'fsdp'=64] {'fsdp'}, dimensions={0} | all-to-all | bytes 2097152 | tf_op jit(solution)/shard_map/all_to_all | solution.py:208
  63.7 0.0 copy-done.1
  63.7 0.0 copy-done.2
  63.7 8.9 %owner.1 = (f32[2,512,512]{2,1,0:T(8,128)}, f32[2,512,512]{2,1,0:T(8,128)}, bf16[64,2,8,512]{3,2,1,0:T(8,128)(2,1)S(1)}) custom-call(bf16[64,2,8,512]{3,2,1,0:T(8,128)(2,1)S(1)} %all_to_all.10.arrived, f32[2,512,512]{2,1,0:T(8,128)S(1)} %bitcast.21, f32[2,512,512]{2,1,0:T(8,128)S(1)} %bitcast.22), custom_call_target="tpu_custom_call" | custom-call | tf_op jit(solution)/shard_map/owner/pallas_call | solution.py:212
  72.6 34.2 %all_to_all.11 = bf16[64,2,8,512]{3,2,1,0:T(8,128)(2,1)S(1)} all-to-all(bf16[64,2,8,512]{3,2,1,0:T(8,128)(2,1)S(1)} %get-tuple-element.18), channel_id=1, replica_groups=mesh['rep'=4,'fsdp'=64] {'fsdp'}, dimensions={0} | all-to-all | bytes 2097152 | tf_op jit(solution)/shard_map/all_to_all | solution.py:226
  106.8 0.6 unpack.1
  107.5 0.1 collective-permute-start.6
  107.6 2.3 %collective-permute-start.8 = (bf16[32,8,512]{2,1,0:T(8,128)(2,1)S(1)}, bf16[32,8,512]{2,1,0:T(8,128)(2,1)S(1)}, u32[]{:S(2)}, u32[]{:S(2)}) collective-permute-start(bf16[32,8,512]{2,1,0:T(8,128)(2,1)S(1)} %get-tuple-element.20.refs_1_), channel_id=1, source_target_pairs={{0,192},{64,128},{128,64},{192,0},{1,193},{65,129},{129,65},{193,1... | collective-permute-start | bytes 786440 | tf_op jit(solution)/shard_map/ppermute | solution.py:242
  109.8 1.0 collective-permute-start.11
  110.9 0.7 collective-permute-start.10
  111.6 5.1 %collective-permute-done.6.refs_2_ = bf16[32,8,512]{2,1,0:T(8,128)(2,1)S(1)} collective-permute-done((bf16[32,8,512]{2,1,0:T(8,128)(2,1)S(1)}, bf16[32,8,512]{2,1,0:T(8,128)(2,1)S(1)}, u32[]{:S(2)}, u32[]{:S(2)}) %collective-permute-start.6) | collective-permute-done | bytes 262176 | tf_op jit(solution)/shard_map/ppermute | solution.py:241
  116.7 2.2 %collective-permute-start.7 = (bf16[32,8,512]{2,1,0:T(8,128)(2,1)S(1)}, bf16[32,8,512]{2,1,0:T(8,128)(2,1)S(1)}, u32[]{:S(2)}, u32[]{:S(2)}) collective-permute-start(bf16[32,8,512]{2,1,0:T(8,128)(2,1)S(1)} %collective-permute-done.6.refs_2_), channel_id=1, source_target_pairs={{0,192},{64,128},{128,64},{192,0},{1,193},{65,129},{129,65},{193,1... | collective-permute-start | bytes 786440 | tf_op jit(solution)/shard_map/ppermute | solution.py:246
  118.9 0.0 collective-permute-done.8.refs_3_
  118.9 0.0 collective-permute-start.9
  118.9 1.6 %place_first.1.refs_2_ = bf16[4,2,32,8,512]{4,3,2,1,0:T(8,128)(2,1)} custom-call(s32[1]{0:T(128)} %bitcast.table, bf16[32,8,512]{2,1,0:T(8,128)(2,1)S(1)} %get-tuple-element.19.refs_0_, bf16[32,8,512]{2,1,0:T(8,128)(2,1)S(1)} %get-tuple-element.20.refs_1_, bf16[32,8,512]{2,1,0:T(8,128)(2,1)S(1)} %collective-permute-done.6.refs_2_, ...), custom_call_target="tpu_custom_call" | custom-call | tf_op jit(solution)/shard_map/place_first/pallas_call | solution.py:259
  120.4 3.2 %collective-permute-done.11.refs_1_ = bf16[32,8,512]{2,1,0:T(8,128)(2,1)S(1)} collective-permute-done((bf16[32,8,512]{2,1,0:T(8,128)(2,1)S(1)}, bf16[32,8,512]{2,1,0:T(8,128)(2,1)S(1)}, u32[]{:S(2)}, u32[]{:S(2)}) %collective-permute-start.11) | collective-permute-done | bytes 262176 | tf_op jit(solution)/shard_map/ppermute | solution.py:244
  123.6 0.0 collective-permute-done.10.refs_0_
  123.6 0.8 place_second.1.refs_2_
  124.4 4.1 %collective-permute-done.7.refs_0_ = bf16[32,8,512]{2,1,0:T(8,128)(2,1)S(1)} collective-permute-done((bf16[32,8,512]{2,1,0:T(8,128)(2,1)S(1)}, bf16[32,8,512]{2,1,0:T(8,128)(2,1)S(1)}, u32[]{:S(2)}, u32[]{:S(2)}) %collective-permute-start.7) | collective-permute-done | bytes 262176 | tf_op jit(solution)/shard_map/ppermute | solution.py:246
  128.6 0.0 collective-permute-done.9.refs_1_
  128.6 0.8 place_far.1
  (2 shorter events, 0.0 us)
Async XLA Ops:
  0.6 8.1 %copy-start.3 = (s32[4,64,1]{1,2,0:T(1,128)S(1)}, s32[4,64,1]{1,2,0:T(1,128)}, u32[]{:S(2)}) copy-start(s32[4,64,1]{1,2,0:T(1,128)} %param.7) | copy-start | bytes 3076
  1.7 8.6 %collective-permute-start.2 = (bf16[32,8,512]{2,1,0:T(8,128)(2,1)S(1)}, bf16[32,8,512]{2,1,0:T(8,128)(2,1)S(1)}, u32[]{:S(2)}, u32[]{:S(2)}) collective-permute-start(bf16[32,8,512]{2,1,0:T(8,128)(2,1)S(1)} %get-tuple-element.24), channel_id=1, source_target_pairs={{0,64},{64,0},{128,192},{192,128},{1,65},{65,1},{129,193},{193,129... | collective-permute-start | bytes 786440 | tf_op jit(solution)/shard_map/ppermute | solution.py:169
  3.4 10.8 %collective-permute-start.4 = (bf16[32,8,512]{2,1,0:T(8,128)(2,1)S(1)}, bf16[32,8,512]{2,1,0:T(8,128)(2,1)S(1)}, u32[]{:S(2)}, u32[]{:S(2)}) collective-permute-start(bf16[32,8,512]{2,1,0:T(8,128)(2,1)S(1)} %get-tuple-element.23), channel_id=1, source_target_pairs={{0,192},{64,128},{128,64},{192,0},{1,193},{65,129},{129,65},{193,1... | collective-permute-start | bytes 786440 | tf_op jit(solution)/shard_map/ppermute | solution.py:170
  5.6 1.6 %copy-start = (bf16[1,256,8,512]{3,2,1,0:T(8,128)(2,1)S(1)}, bf16[1,256,8,512]{3,2,1,0:T(8,128)(2,1)}, u32[]{:S(2)}) copy-start(bf16[1,256,8,512]{3,2,1,0:T(8,128)(2,1)} %param.4) | copy-start | bytes 6291460
  7.3 9.1 %collective-permute-start = (bf16[1,32,8,512]{3,2,1,0:T(8,128)(2,1)S(1)}, bf16[1,32,8,512]{3,2,1,0:T(8,128)(2,1)S(1)}, u32[]{:S(2)}, u32[]{:S(2)}) collective-permute-start(bf16[1,32,8,512]{3,2,1,0:T(8,128)(2,1)S(1)} %get-tuple-element.14), channel_id=1, source_target_pairs={{0,64},{64,0},{128,192},{192,128},{1,65},{65,1},{129,193},{193,129... | collective-permute-start | bytes 786440 | tf_op jit(solution)/shard_map/ppermute | solution.py:174
  8.1 11.3 %collective-permute-start.1 = (bf16[1,32,8,512]{3,2,1,0:T(8,128)(2,1)S(1)}, bf16[1,32,8,512]{3,2,1,0:T(8,128)(2,1)S(1)}, u32[]{:S(2)}, u32[]{:S(2)}) collective-permute-start(bf16[1,32,8,512]{3,2,1,0:T(8,128)(2,1)S(1)} %get-tuple-element.15), channel_id=1, source_target_pairs={{0,192},{64,128},{128,64},{192,0},{1,193},{65,129},{129,65},{193,1... | collective-permute-start | bytes 786440 | tf_op jit(solution)/shard_map/ppermute | solution.py:175
  10.4 13.2 %collective-permute-start.3 = (bf16[32,8,512]{2,1,0:T(8,128)(2,1)S(1)}, bf16[32,8,512]{2,1,0:T(8,128)(2,1)S(1)}, u32[]{:S(2)}, u32[]{:S(2)}) collective-permute-start(bf16[32,8,512]{2,1,0:T(8,128)(2,1)S(1)} %relay.2), channel_id=1, source_target_pairs={{0,192},{64,128},{128,64},{192,0},{1,193},{65,129},{129,65},{193,1... | collective-permute-start | bytes 786440 | tf_op jit(solution)/shard_map/ppermute | solution.py:187
  14.2 9.4 %collective-permute-start.5 = (bf16[32,8,512]{2,1,0:T(8,128)(2,1)S(1)}, bf16[32,8,512]{2,1,0:T(8,128)(2,1)S(1)}, u32[]{:S(2)}, u32[]{:S(2)}) collective-permute-start(bf16[32,8,512]{2,1,0:T(8,128)(2,1)S(1)} %relay.3), channel_id=1, source_target_pairs={{0,64},{64,0},{128,192},{192,128},{1,65},{65,1},{129,193},{193,129... | collective-permute-start | bytes 786440 | tf_op jit(solution)/shard_map/ppermute | solution.py:188
  19.5 44.2 %copy-start.1 = (f32[1,1,2,512,512]{4,3,2,1,0:T(8,128)S(1)}, f32[1,1,2,512,512]{4,3,2,1,0:T(8,128)}, u32[]{:S(2)}) copy-start(f32[1,1,2,512,512]{4,3,2,1,0:T(8,128)} %param.5) | copy-start | bytes 6291460
  19.5 44.2 %copy-start.2 = (f32[1,1,2,512,512]{4,3,2,1,0:T(8,128)S(1)}, f32[1,1,2,512,512]{4,3,2,1,0:T(8,128)}, u32[]{:S(2)}) copy-start(f32[1,1,2,512,512]{4,3,2,1,0:T(8,128)} %param.6) | copy-start | bytes 6291460
  107.5 9.2 %collective-permute-start.6 = (bf16[32,8,512]{2,1,0:T(8,128)(2,1)S(1)}, bf16[32,8,512]{2,1,0:T(8,128)(2,1)S(1)}, u32[]{:S(2)}, u32[]{:S(2)}) collective-permute-start(bf16[32,8,512]{2,1,0:T(8,128)(2,1)S(1)} %get-tuple-element.19.refs_0_), channel_id=1, source_target_pairs={{0,64},{64,0},{128,192},{192,128},{1,65},{65,1},{129,193},{193,129... | collective-permute-start | bytes 786440 | tf_op jit(solution)/shard_map/ppermute | solution.py:241
  107.6 11.3 %collective-permute-start.8 = (bf16[32,8,512]{2,1,0:T(8,128)(2,1)S(1)}, bf16[32,8,512]{2,1,0:T(8,128)(2,1)S(1)}, u32[]{:S(2)}, u32[]{:S(2)}) collective-permute-start(bf16[32,8,512]{2,1,0:T(8,128)(2,1)S(1)} %get-tuple-element.20.refs_1_), channel_id=1, source_target_pairs={{0,192},{64,128},{128,64},{192,0},{1,193},{65,129},{129,65},{193,1... | collective-permute-start | bytes 786440 | tf_op jit(solution)/shard_map/ppermute | solution.py:242
  109.8 13.8 %collective-permute-start.11 = (bf16[32,8,512]{2,1,0:T(8,128)(2,1)S(1)}, bf16[32,8,512]{2,1,0:T(8,128)(2,1)S(1)}, u32[]{:S(2)}, u32[]{:S(2)}) collective-permute-start(bf16[32,8,512]{2,1,0:T(8,128)(2,1)S(1)} %get-tuple-element.19.refs_0_), channel_id=1, source_target_pairs={{0,192},{64,128},{128,64},{192,0},{1,193},{65,129},{129,65},{193,1... | collective-permute-start | bytes 786440 | tf_op jit(solution)/shard_map/ppermute | solution.py:244
  110.9 12.7 %collective-permute-start.10 = (bf16[32,8,512]{2,1,0:T(8,128)(2,1)S(1)}, bf16[32,8,512]{2,1,0:T(8,128)(2,1)S(1)}, u32[]{:S(2)}, u32[]{:S(2)}) collective-permute-start(bf16[32,8,512]{2,1,0:T(8,128)(2,1)S(1)} %get-tuple-element.20.refs_1_), channel_id=1, source_target_pairs={{0,64},{64,0},{128,192},{192,128},{1,65},{65,1},{129,193},{193,129... | collective-permute-start | bytes 786440 | tf_op jit(solution)/shard_map/ppermute | solution.py:243
  116.7 11.9 %collective-permute-start.7 = (bf16[32,8,512]{2,1,0:T(8,128)(2,1)S(1)}, bf16[32,8,512]{2,1,0:T(8,128)(2,1)S(1)}, u32[]{:S(2)}, u32[]{:S(2)}) collective-permute-start(bf16[32,8,512]{2,1,0:T(8,128)(2,1)S(1)} %collective-permute-done.6.refs_2_), channel_id=1, source_target_pairs={{0,192},{64,128},{128,64},{192,0},{1,193},{65,129},{129,65},{193,1... | collective-permute-start | bytes 786440 | tf_op jit(solution)/shard_map/ppermute | solution.py:246
  118.9 9.7 %collective-permute-start.9 = (bf16[32,8,512]{2,1,0:T(8,128)(2,1)S(1)}, bf16[32,8,512]{2,1,0:T(8,128)(2,1)S(1)}, u32[]{:S(2)}, u32[]{:S(2)}) collective-permute-start(bf16[32,8,512]{2,1,0:T(8,128)(2,1)S(1)} %collective-permute-done.8.refs_3_), channel_id=1, source_target_pairs={{0,64},{64,0},{128,192},{192,128},{1,65},{65,1},{129,193},{193,129... | collective-permute-start | bytes 786440 | tf_op jit(solution)/shard_map/ppermute | solution.py:245

commit v12 on v10

--- a/solution.py
+++ b/solution.py
@@ -41,17 +41,20 @@
         out[k * half : (k + 1) * half] = own[k].astype(F32) + direct[0].astype(F32)
 
 
-def pack_kernel(table, presum, second_a, second_b, out):
+def pack_kernel(table, presum, second_a, second_b, out, held, slots, sem):
     half = second_a.shape[0]
+    fetch = pltpu.make_async_copy(table, slots, sem)
+    fetch.start()
     out[...] = jnp.zeros(out.shape, out.dtype)
-    for k, second in enumerate((second_a, second_b)):
-
-        def move(j, carry, k=k, second=second):
-            total = presum[k * half + j] + second[j].astype(F32)
-            out[table[k * half + j]] = total.astype(BF16)
-            return carry
-
-        lax.fori_loop(0, half, move, 0, unroll=8)
+    held[:half] = (presum[:half] + second_a[...].astype(F32)).astype(BF16)
+    held[half:] = (presum[half:] + second_b[...].astype(F32)).astype(BF16)
+    fetch.wait()
+
+    def move(j, carry):
+        out[slots[j]] = held[j]
+        return carry
+
+    lax.fori_loop(0, 2 * half, move, 0, unroll=8)
 
 
 def dot(a, b, ca=1, cb=0):
@@ -197,10 +200,14 @@
 
     outgoing = pl.pallas_call(
         pack_kernel,
+        in_specs=[pl.BlockSpec(memory_space=pl.ANY)] + [in_vmem] * 3,
+        out_specs=in_vmem,
         out_shape=jax.ShapeDtypeStruct((fsdp * capacity, rows, width), BF16),
-        grid_spec=pltpu.PrefetchScalarGridSpec(
-            num_scalar_prefetch=1, grid=(1,), in_specs=[in_vmem] * 3, out_specs=in_vmem
-        ),
+        scratch_shapes=[
+            pltpu.VMEM((per_row, rows, width), BF16),
+            pltpu.SMEM((per_row,), jnp.int32),
+            pltpu.SemaphoreType.DMA,
+        ],
         compiler_params=params,
         name="pack",
     )(slot_of, presum, second_a, second_b).reshape(fsdp, capacity, rows, width)

time: 130 us -> 130 us (level)
  no operation moved by 1% of the time
where the time goes in v12:
time: 130 us; the launch traced here: 129 us
  blocking collectives  73.6 us (57%)
  waiting for transfers between devices  20.4 us (16%)
  starting transfers between devices  17.8 us (14%)
  Pallas kernels  13.8 us (11%)
  local copies, waits for them, and re-layouts  2.68 us (2%)
    all_to_all x1, blocking collectives, shards(): lax.all_to_all(outgoing, 'fsdp', split_axis=0, concat_axis=0, tiled=True)  39.3 us
    all_to_all x1, blocking collectives, shards(): lax.all_to_all(slot_update, 'fsdp', split_axis=0, concat_axis=0, tiled=True)  34.2 us
    pallas_call x1, Pallas kernels, shards(): pl.pallas_call(owner_kernel, in_specs=[in_vmem, in_vmem, in_vmem], out_sp...  8.87 us
    ppermute x1, waiting for transfers between devices, shards(): left_a = lax.ppermute(mine_a, 'rep', plus)  5.08 us
    ppermute x1, waiting for transfers between devices, shards(): far_a = lax.ppermute(left_a, 'rep', plus)  4.13 us
    ppermute x1, waiting for transfers between devices, shards(): second_a = lax.ppermute(relay(kept_a, relayed_a), 'rep', swap3)  4.09 us
    ppermute x1, starting transfers between devices, shards(): second_a = lax.ppermute(relay(kept_a, relayed_a), 'rep', swap3)  3.75 us
    ppermute x1, starting transfers between devices, shards(): far_b = lax.ppermute(right_b, 'rep', minus)  3.27 us
  transfers between devices with their start and end apart: 12, of which 8 were waited for; matrix products, arithmetic and copies ran while one was open for 0% of the time, Pallas kernels for 2%

profile of v12, /device:TPU:32, one launch (start us, length us, event | category | flops | bytes accessed | tf_op | source)
XLA Modules:
  0.0 129.2 jit_solution(1205462908098236605)
XLA Ops:
  0.6 0.0 copy-start.3
  0.6 1.1 dynamic-slice_bitcast_fusion
  1.7 1.7 %collective-permute-start.2 = (bf16[32,8,512]{2,1,0:T(8,128)(2,1)S(1)}, bf16[32,8,512]{2,1,0:T(8,128)(2,1)S(1)}, u32[]{:S(2)}, u32[]{:S(2)}) collective-permute-start(bf16[32,8,512]{2,1,0:T(8,128)(2,1)S(1)} %get-tuple-element.24), channel_id=1, source_target_pairs={{0,64},{64,0},{128,192},{192,128},{1,65},{65,1},{129,193},{193,129... | collective-permute-start | bytes 786440 | tf_op jit(solution)/shard_map/ppermute | solution.py:172
  3.4 2.2 %collective-permute-start.4 = (bf16[32,8,512]{2,1,0:T(8,128)(2,1)S(1)}, bf16[32,8,512]{2,1,0:T(8,128)(2,1)S(1)}, u32[]{:S(2)}, u32[]{:S(2)}) collective-permute-start(bf16[32,8,512]{2,1,0:T(8,128)(2,1)S(1)} %get-tuple-element.23), channel_id=1, source_target_pairs={{0,192},{64,128},{128,64},{192,0},{1,193},{65,129},{129,65},{193,1... | collective-permute-start | bytes 786440 | tf_op jit(solution)/shard_map/ppermute | solution.py:173
  5.6 0.0 copy-start
  5.6 1.6 %copy-done = bf16[1,256,8,512]{3,2,1,0:T(8,128)(2,1)S(1)} copy-done((bf16[1,256,8,512]{3,2,1,0:T(8,128)(2,1)S(1)}, bf16[1,256,8,512]{3,2,1,0:T(8,128)(2,1)}, u32[]{:S(2)}) %copy-start) | copy-done | bytes 2097176
  7.2 0.2 pick.1
  7.3 0.8 collective-permute-start
  8.1 0.6 collective-permute-start.1
  8.7 0.0 copy-done.3
  8.7 1.6 %collective-permute-done.2.relayed = bf16[32,8,512]{2,1,0:T(8,128)(2,1)S(1)} collective-permute-done((bf16[32,8,512]{2,1,0:T(8,128)(2,1)S(1)}, bf16[32,8,512]{2,1,0:T(8,128)(2,1)S(1)}, u32[]{:S(2)}, u32[]{:S(2)}) %collective-permute-start.2) | collective-permute-done | bytes 262176 | tf_op jit(solution)/shard_map/ppermute | solution.py:172
  10.3 0.1 relay.2
  10.4 3.8 %collective-permute-start.3 = (bf16[32,8,512]{2,1,0:T(8,128)(2,1)S(1)}, bf16[32,8,512]{2,1,0:T(8,128)(2,1)S(1)}, u32[]{:S(2)}, u32[]{:S(2)}) collective-permute-start(bf16[32,8,512]{2,1,0:T(8,128)(2,1)S(1)} %relay.2), channel_id=1, source_target_pairs={{0,192},{64,128},{128,64},{192,0},{1,193},{65,129},{129,65},{193,1... | collective-permute-start | bytes 786440 | tf_op jit(solution)/shard_map/ppermute | solution.py:190
  14.2 0.0 collective-permute-done.4.relayed
  14.2 0.1 relay.3
  14.2 0.2 collective-permute-start.5
  14.5 0.2 convert_reduce_fusion
  14.7 1.8 %collective-permute-done.direct_a = bf16[1,32,8,512]{3,2,1,0:T(8,128)(2,1)S(1)} collective-permute-done((bf16[1,32,8,512]{3,2,1,0:T(8,128)(2,1)S(1)}, bf16[1,32,8,512]{3,2,1,0:T(8,128)(2,1)S(1)}, u32[]{:S(2)}, u32[]{:S(2)}) %collective-permute-start) | collective-permute-done | bytes 262176 | tf_op jit(solution)/shard_map/ppermute | solution.py:177
  16.4 3.0 %collective-permute-done.1.direct_b = bf16[1,32,8,512]{3,2,1,0:T(8,128)(2,1)S(1)} collective-permute-done((bf16[1,32,8,512]{3,2,1,0:T(8,128)(2,1)S(1)}, bf16[1,32,8,512]{3,2,1,0:T(8,128)(2,1)S(1)}, u32[]{:S(2)}, u32[]{:S(2)}) %collective-permute-start.1) | collective-permute-done | bytes 262176 | tf_op jit(solution)/shard_map/ppermute | solution.py:178
  19.4 0.1 presum.1
  19.5 0.0 copy-start.1
  19.5 0.0 copy-start.2
  19.5 4.1 %collective-permute-done.3.second_a = bf16[32,8,512]{2,1,0:T(8,128)(2,1)S(1)} collective-permute-done((bf16[32,8,512]{2,1,0:T(8,128)(2,1)S(1)}, bf16[32,8,512]{2,1,0:T(8,128)(2,1)S(1)}, u32[]{:S(2)}, u32[]{:S(2)}) %collective-permute-start.3) | collective-permute-done | bytes 262176 | tf_op jit(solution)/shard_map/ppermute | solution.py:190
  23.6 0.0 collective-permute-done.5.second_b
  23.6 0.7 pack.1
  24.3 39.3 %all_to_all.10.arrived = bf16[64,2,8,512]{3,2,1,0:T(8,128)(2,1)S(1)} all-to-all(bf16[64,2,8,512]{3,2,1,0:T(8,128)(2,1)S(1)} %bitcast.18), channel_id=1, replica_groups=mesh['rep'=4,'fsdp'=64] {'fsdp'}, dimensions={0} | all-to-all | bytes 2097152 | tf_op jit(solution)/shard_map/all_to_all | solution.py:215
  63.6 0.0 copy-done.1
  63.6 0.0 copy-done.2
  63.6 8.9 %owner.1 = (f32[2,512,512]{2,1,0:T(8,128)}, f32[2,512,512]{2,1,0:T(8,128)}, bf16[64,2,8,512]{3,2,1,0:T(8,128)(2,1)S(1)}) custom-call(bf16[64,2,8,512]{3,2,1,0:T(8,128)(2,1)S(1)} %all_to_all.10.arrived, f32[2,512,512]{2,1,0:T(8,128)S(1)} %bitcast.21, f32[2,512,512]{2,1,0:T(8,128)S(1)} %bitcast.22), custom_call_target="tpu_custom_call" | custom-call | tf_op jit(solution)/shard_map/owner/pallas_call | solution.py:219
  72.5 34.2 %all_to_all.11 = bf16[64,2,8,512]{3,2,1,0:T(8,128)(2,1)S(1)} all-to-all(bf16[64,2,8,512]{3,2,1,0:T(8,128)(2,1)S(1)} %get-tuple-element.18), channel_id=1, replica_groups=mesh['rep'=4,'fsdp'=64] {'fsdp'}, dimensions={0} | all-to-all | bytes 2097152 | tf_op jit(solution)/shard_map/all_to_all | solution.py:233
  106.7 0.6 unpack.1
  107.4 0.1 collective-permute-start.6
  107.5 3.2 %collective-permute-start.8 = (bf16[32,8,512]{2,1,0:T(8,128)(2,1)S(1)}, bf16[32,8,512]{2,1,0:T(8,128)(2,1)S(1)}, u32[]{:S(2)}, u32[]{:S(2)}) collective-permute-start(bf16[32,8,512]{2,1,0:T(8,128)(2,1)S(1)} %get-tuple-element.20.refs_1_), channel_id=1, source_target_pairs={{0,192},{64,0},{128,64},{192,128},{1,193},{65,1},{129,65},{193,129... | collective-permute-start | bytes 786440 | tf_op jit(solution)/shard_map/ppermute | solution.py:251
  110.7 1.0 collective-permute-start.11
  111.7 1.1 collective-permute-start.10
  112.7 5.1 %collective-permute-done.6.refs_2_ = bf16[32,8,512]{2,1,0:T(8,128)(2,1)S(1)} collective-permute-done((bf16[32,8,512]{2,1,0:T(8,128)(2,1)S(1)}, bf16[32,8,512]{2,1,0:T(8,128)(2,1)S(1)}, u32[]{:S(2)}, u32[]{:S(2)}) %collective-permute-start.6) | collective-permute-done | bytes 262176 | tf_op jit(solution)/shard_map/ppermute | solution.py:250
  117.8 0.0 collective-permute-start.7
  117.8 0.0 collective-permute-done.8.refs_3_
  117.8 3.3 %collective-permute-start.9 = (bf16[32,8,512]{2,1,0:T(8,128)(2,1)S(1)}, bf16[32,8,512]{2,1,0:T(8,128)(2,1)S(1)}, u32[]{:S(2)}, u32[]{:S(2)}) collective-permute-start(bf16[32,8,512]{2,1,0:T(8,128)(2,1)S(1)} %collective-permute-done.8.refs_3_), channel_id=1, source_target_pairs={{0,192},{64,0},{128,64},{192,128},{1,193},{65,1},{129,65},{193,129... | collective-permute-start | bytes 786440 | tf_op jit(solution)/shard_map/ppermute | solution.py:255
  121.1 1.6 %place_first.1.refs_2_ = bf16[4,2,32,8,512]{4,3,2,1,0:T(8,128)(2,1)} custom-call(s32[1]{0:T(128)} %bitcast.table, bf16[32,8,512]{2,1,0:T(8,128)(2,1)S(1)} %get-tuple-element.19.refs_0_, bf16[32,8,512]{2,1,0:T(8,128)(2,1)S(1)} %get-tuple-element.20.refs_1_, bf16[32,8,512]{2,1,0:T(8,128)(2,1)S(1)} %collective-permute-done.6.refs_2_, ...), custom_call_target="tpu_custom_call" | custom-call | tf_op jit(solution)/shard_map/place_first/pallas_call | solution.py:268
  122.6 0.4 collective-permute-done.11.refs_1_
  123.0 0.4 collective-permute-done.10.refs_0_
  123.4 0.8 place_second.1.refs_2_
  124.2 4.1 %collective-permute-done.7.refs_0_ = bf16[32,8,512]{2,1,0:T(8,128)(2,1)S(1)} collective-permute-done((bf16[32,8,512]{2,1,0:T(8,128)(2,1)S(1)}, bf16[32,8,512]{2,1,0:T(8,128)(2,1)S(1)}, u32[]{:S(2)}, u32[]{:S(2)}) %collective-permute-start.7) | collective-permute-done | bytes 262176 | tf_op jit(solution)/shard_map/ppermute | solution.py:254
  128.4 0.0 collective-permute-done.9.refs_1_
  128.4 0.8 place_far.1
  (2 shorter events, 0.0 us)
Async XLA Ops:
  0.6 8.1 %copy-start.3 = (s32[4,64,1]{1,2,0:T(1,128)S(1)}, s32[4,64,1]{1,2,0:T(1,128)}, u32[]{:S(2)}) copy-start(s32[4,64,1]{1,2,0:T(1,128)} %param.7) | copy-start | bytes 3076
  1.7 8.6 %collective-permute-start.2 = (bf16[32,8,512]{2,1,0:T(8,128)(2,1)S(1)}, bf16[32,8,512]{2,1,0:T(8,128)(2,1)S(1)}, u32[]{:S(2)}, u32[]{:S(2)}) collective-permute-start(bf16[32,8,512]{2,1,0:T(8,128)(2,1)S(1)} %get-tuple-element.24), channel_id=1, source_target_pairs={{0,64},{64,0},{128,192},{192,128},{1,65},{65,1},{129,193},{193,129... | collective-permute-start | bytes 786440 | tf_op jit(solution)/shard_map/ppermute | solution.py:172
  3.4 10.8 %collective-permute-start.4 = (bf16[32,8,512]{2,1,0:T(8,128)(2,1)S(1)}, bf16[32,8,512]{2,1,0:T(8,128)(2,1)S(1)}, u32[]{:S(2)}, u32[]{:S(2)}) collective-permute-start(bf16[32,8,512]{2,1,0:T(8,128)(2,1)S(1)} %get-tuple-element.23), channel_id=1, source_target_pairs={{0,192},{64,128},{128,64},{192,0},{1,193},{65,129},{129,65},{193,1... | collective-permute-start | bytes 786440 | tf_op jit(solution)/shard_map/ppermute | solution.py:173
  5.6 1.6 %copy-start = (bf16[1,256,8,512]{3,2,1,0:T(8,128)(2,1)S(1)}, bf16[1,256,8,512]{3,2,1,0:T(8,128)(2,1)}, u32[]{:S(2)}) copy-start(bf16[1,256,8,512]{3,2,1,0:T(8,128)(2,1)} %param.4) | copy-start | bytes 6291460
  7.3 9.1 %collective-permute-start = (bf16[1,32,8,512]{3,2,1,0:T(8,128)(2,1)S(1)}, bf16[1,32,8,512]{3,2,1,0:T(8,128)(2,1)S(1)}, u32[]{:S(2)}, u32[]{:S(2)}) collective-permute-start(bf16[1,32,8,512]{3,2,1,0:T(8,128)(2,1)S(1)} %get-tuple-element.14), channel_id=1, source_target_pairs={{0,64},{64,0},{128,192},{192,128},{1,65},{65,1},{129,193},{193,129... | collective-permute-start | bytes 786440 | tf_op jit(solution)/shard_map/ppermute | solution.py:177
  8.1 11.3 %collective-permute-start.1 = (bf16[1,32,8,512]{3,2,1,0:T(8,128)(2,1)S(1)}, bf16[1,32,8,512]{3,2,1,0:T(8,128)(2,1)S(1)}, u32[]{:S(2)}, u32[]{:S(2)}) collective-permute-start(bf16[1,32,8,512]{3,2,1,0:T(8,128)(2,1)S(1)} %get-tuple-element.15), channel_id=1, source_target_pairs={{0,192},{64,128},{128,64},{192,0},{1,193},{65,129},{129,65},{193,1... | collective-permute-start | bytes 786440 | tf_op jit(solution)/shard_map/ppermute | solution.py:178
  10.4 13.2 %collective-permute-start.3 = (bf16[32,8,512]{2,1,0:T(8,128)(2,1)S(1)}, bf16[32,8,512]{2,1,0:T(8,128)(2,1)S(1)}, u32[]{:S(2)}, u32[]{:S(2)}) collective-permute-start(bf16[32,8,512]{2,1,0:T(8,128)(2,1)S(1)} %relay.2), channel_id=1, source_target_pairs={{0,192},{64,128},{128,64},{192,0},{1,193},{65,129},{129,65},{193,1... | collective-permute-start | bytes 786440 | tf_op jit(solution)/shard_map/ppermute | solution.py:190
  14.2 9.4 %collective-permute-start.5 = (bf16[32,8,512]{2,1,0:T(8,128)(2,1)S(1)}, bf16[32,8,512]{2,1,0:T(8,128)(2,1)S(1)}, u32[]{:S(2)}, u32[]{:S(2)}) collective-permute-start(bf16[32,8,512]{2,1,0:T(8,128)(2,1)S(1)} %relay.3), channel_id=1, source_target_pairs={{0,64},{64,0},{128,192},{192,128},{1,65},{65,1},{129,193},{193,129... | collective-permute-start | bytes 786440 | tf_op jit(solution)/shard_map/ppermute | solution.py:191
  19.5 44.1 %copy-start.1 = (f32[1,1,2,512,512]{4,3,2,1,0:T(8,128)S(1)}, f32[1,1,2,512,512]{4,3,2,1,0:T(8,128)}, u32[]{:S(2)}) copy-start(f32[1,1,2,512,512]{4,3,2,1,0:T(8,128)} %param.5) | copy-start | bytes 6291460
  19.5 44.1 %copy-start.2 = (f32[1,1,2,512,512]{4,3,2,1,0:T(8,128)S(1)}, f32[1,1,2,512,512]{4,3,2,1,0:T(8,128)}, u32[]{:S(2)}) copy-start(f32[1,1,2,512,512]{4,3,2,1,0:T(8,128)} %param.6) | copy-start | bytes 6291460
  107.4 10.4 %collective-permute-start.6 = (bf16[32,8,512]{2,1,0:T(8,128)(2,1)S(1)}, bf16[32,8,512]{2,1,0:T(8,128)(2,1)S(1)}, u32[]{:S(2)}, u32[]{:S(2)}) collective-permute-start(bf16[32,8,512]{2,1,0:T(8,128)(2,1)S(1)} %get-tuple-element.19.refs_0_), channel_id=1, source_target_pairs={{0,64},{64,128},{128,192},{192,0},{1,65},{65,129},{129,193},{193,1... | collective-permute-start | bytes 786440 | tf_op jit(solution)/shard_map/ppermute | solution.py:250
  107.5 10.3 %collective-permute-start.8 = (bf16[32,8,512]{2,1,0:T(8,128)(2,1)S(1)}, bf16[32,8,512]{2,1,0:T(8,128)(2,1)S(1)}, u32[]{:S(2)}, u32[]{:S(2)}) collective-permute-start(bf16[32,8,512]{2,1,0:T(8,128)(2,1)S(1)} %get-tuple-element.20.refs_1_), channel_id=1, source_target_pairs={{0,192},{64,0},{128,64},{192,128},{1,193},{65,1},{129,65},{193,129... | collective-permute-start | bytes 786440 | tf_op jit(solution)/shard_map/ppermute | solution.py:251
  110.7 12.3 %collective-permute-start.11 = (bf16[32,8,512]{2,1,0:T(8,128)(2,1)S(1)}, bf16[32,8,512]{2,1,0:T(8,128)(2,1)S(1)}, u32[]{:S(2)}, u32[]{:S(2)}) collective-permute-start(bf16[32,8,512]{2,1,0:T(8,128)(2,1)S(1)} %get-tuple-element.19.refs_0_), channel_id=1, source_target_pairs={{0,192},{64,0},{128,64},{192,128},{1,193},{65,1},{129,65},{193,129... | collective-permute-start | bytes 786440 | tf_op jit(solution)/shard_map/ppermute | solution.py:253
  111.7 11.8 %collective-permute-start.10 = (bf16[32,8,512]{2,1,0:T(8,128)(2,1)S(1)}, bf16[32,8,512]{2,1,0:T(8,128)(2,1)S(1)}, u32[]{:S(2)}, u32[]{:S(2)}) collective-permute-start(bf16[32,8,512]{2,1,0:T(8,128)(2,1)S(1)} %get-tuple-element.20.refs_1_), channel_id=1, source_target_pairs={{0,64},{64,128},{128,192},{192,0},{1,65},{65,129},{129,193},{193,1... | collective-permute-start | bytes 786440 | tf_op jit(solution)/shard_map/ppermute | solution.py:252
  117.8 10.6 %collective-permute-start.7 = (bf16[32,8,512]{2,1,0:T(8,128)(2,1)S(1)}, bf16[32,8,512]{2,1,0:T(8,128)(2,1)S(1)}, u32[]{:S(2)}, u32[]{:S(2)}) collective-permute-start(bf16[32,8,512]{2,1,0:T(8,128)(2,1)S(1)} %collective-permute-done.6.refs_2_), channel_id=1, source_target_pairs={{0,64},{64,128},{128,192},{192,0},{1,65},{65,129},{129,193},{193,1... | collective-permute-start | bytes 786440 | tf_op jit(solution)/shard_map/ppermute | solution.py:254
  117.8 10.6 %collective-permute-start.9 = (bf16[32,8,512]{2,1,0:T(8,128)(2,1)S(1)}, bf16[32,8,512]{2,1,0:T(8,128)(2,1)S(1)}, u32[]{:S(2)}, u32[]{:S(2)}) collective-permute-start(bf16[32,8,512]{2,1,0:T(8,128)(2,1)S(1)} %collective-permute-done.8.refs_3_), channel_id=1, source_target_pairs={{0,192},{64,0},{128,64},{192,128},{1,193},{65,1},{129,65},{193,129... | collective-permute-start | bytes 786440 | tf_op jit(solution)/shard_map/ppermute | solution.py:255

commit v13 on v12

--- a/solution.py
+++ b/solution.py
@@ -109,15 +109,18 @@
         copy.wait()
 
 
-def unpack_kernel(table, slots, out_a, out_b):
+def unpack_kernel(table, rows, out_a, out_b, slots, sem):
     half = out_a.shape[0]
+    fetch = pltpu.make_async_copy(table, slots, sem)
+    fetch.start()
+    fetch.wait()
 
     def move(j, carry):
-        out_a[j] = slots[table[j]]
-        out_b[j] = slots[table[half + j]]
+        out_a[j] = rows[slots[j]]
+        out_b[j] = rows[slots[half + j]]
         return carry
 
-    lax.fori_loop(0, half, move, 0, unroll=4)
+    lax.fori_loop(0, half, move, 0, unroll=8)
 
 
 def place_kernel(steps, table, *refs):
@@ -234,13 +237,10 @@
 
     mine_a, mine_b = pl.pallas_call(
         unpack_kernel,
+        in_specs=[anywhere, in_vmem],
+        out_specs=[in_vmem, in_vmem],
         out_shape=[half_shape] * 2,
-        grid_spec=pltpu.PrefetchScalarGridSpec(
-            num_scalar_prefetch=1,
-            grid=(1,),
-            in_specs=[in_vmem],
-            out_specs=[in_vmem, in_vmem],
-        ),
+        scratch_shapes=[pltpu.SMEM((per_row,), jnp.int32), pltpu.SemaphoreType.DMA],
         compiler_params=params,
         name="unpack",
     )(slot_of, returned.reshape(fsdp * capacity, rows, width))

time: 130 us -> 130 us (level)
  no operation moved by 1% of the time
where the time goes in v13:
time: 130 us; the launch traced here: 129 us
  blocking collectives  73.6 us (57%)
  waiting for transfers between devices  20.4 us (16%)
  starting transfers between devices  17.8 us (14%)
  Pallas kernels  13.8 us (11%)
  local copies, waits for them, and re-layouts  2.68 us (2%)
    all_to_all x1, blocking collectives, shards(): lax.all_to_all(outgoing, 'fsdp', split_axis=0, concat_axis=0, tiled=True)  39.3 us
    all_to_all x1, blocking collectives, shards(): lax.all_to_all(slot_update, 'fsdp', split_axis=0, concat_axis=0, tiled=True)  34.2 us
    pallas_call x1, Pallas kernels, shards(): pl.pallas_call(owner_kernel, in_specs=[in_vmem, in_vmem, in_vmem], out_sp...  8.87 us
    ppermute x1, waiting for transfers between devices, shards(): left_a = lax.ppermute(mine_a, 'rep', plus)  5.08 us
    ppermute x1, waiting for transfers between devices, shards(): far_a = lax.ppermute(left_a, 'rep', plus)  4.13 us
    ppermute x1, waiting for transfers between devices, shards(): second_a = lax.ppermute(relay(kept_a, relayed_a), 'rep', swap3)  4.09 us
    ppermute x1, starting transfers between devices, shards(): second_a = lax.ppermute(relay(kept_a, relayed_a), 'rep', swap3)  3.75 us
    ppermute x1, starting transfers between devices, shards(): far_b = lax.ppermute(right_b, 'rep', minus)  3.27 us
  transfers between devices with their start and end apart: 12, of which 8 were waited for; matrix products, arithmetic and copies ran while one was open for 0% of the time, Pallas kernels for 2%

profile of v13, /device:TPU:32, one launch (start us, length us, event | category | flops | bytes accessed | tf_op | source)
XLA Modules:
  0.0 129.2 jit_solution(1266981746567802863)
XLA Ops:
  0.6 0.0 copy-start.3
  0.6 1.1 dynamic-slice_bitcast_fusion
  1.7 1.7 %collective-permute-start.2 = (bf16[32,8,512]{2,1,0:T(8,128)(2,1)S(1)}, bf16[32,8,512]{2,1,0:T(8,128)(2,1)S(1)}, u32[]{:S(2)}, u32[]{:S(2)}) collective-permute-start(bf16[32,8,512]{2,1,0:T(8,128)(2,1)S(1)} %get-tuple-element.24), channel_id=1, source_target_pairs={{0,64},{64,0},{128,192},{192,128},{1,65},{65,1},{129,193},{193,129... | collective-permute-start | bytes 786440 | tf_op jit(solution)/shard_map/ppermute | solution.py:175
  3.4 2.2 %collective-permute-start.4 = (bf16[32,8,512]{2,1,0:T(8,128)(2,1)S(1)}, bf16[32,8,512]{2,1,0:T(8,128)(2,1)S(1)}, u32[]{:S(2)}, u32[]{:S(2)}) collective-permute-start(bf16[32,8,512]{2,1,0:T(8,128)(2,1)S(1)} %get-tuple-element.23), channel_id=1, source_target_pairs={{0,192},{64,128},{128,64},{192,0},{1,193},{65,129},{129,65},{193,1... | collective-permute-start | bytes 786440 | tf_op jit(solution)/shard_map/ppermute | solution.py:176
  5.6 0.0 copy-start
  5.6 1.6 %copy-done = bf16[1,256,8,512]{3,2,1,0:T(8,128)(2,1)S(1)} copy-done((bf16[1,256,8,512]{3,2,1,0:T(8,128)(2,1)S(1)}, bf16[1,256,8,512]{3,2,1,0:T(8,128)(2,1)}, u32[]{:S(2)}) %copy-start) | copy-done | bytes 2097176
  7.2 0.2 pick.1
  7.3 0.8 collective-permute-start
  8.1 0.6 collective-permute-start.1
  8.7 0.0 copy-done.3
  8.7 1.6 %collective-permute-done.2.relayed = bf16[32,8,512]{2,1,0:T(8,128)(2,1)S(1)} collective-permute-done((bf16[32,8,512]{2,1,0:T(8,128)(2,1)S(1)}, bf16[32,8,512]{2,1,0:T(8,128)(2,1)S(1)}, u32[]{:S(2)}, u32[]{:S(2)}) %collective-permute-start.2) | collective-permute-done | bytes 262176 | tf_op jit(solution)/shard_map/ppermute | solution.py:175
  10.3 0.1 relay.2
  10.4 3.8 %collective-permute-start.3 = (bf16[32,8,512]{2,1,0:T(8,128)(2,1)S(1)}, bf16[32,8,512]{2,1,0:T(8,128)(2,1)S(1)}, u32[]{:S(2)}, u32[]{:S(2)}) collective-permute-start(bf16[32,8,512]{2,1,0:T(8,128)(2,1)S(1)} %relay.2), channel_id=1, source_target_pairs={{0,192},{64,128},{128,64},{192,0},{1,193},{65,129},{129,65},{193,1... | collective-permute-start | bytes 786440 | tf_op jit(solution)/shard_map/ppermute | solution.py:193
  14.2 0.0 collective-permute-done.4.relayed
  14.2 0.1 relay.3
  14.2 0.2 collective-permute-start.5
  14.5 0.2 convert_reduce_fusion
  14.7 1.8 %collective-permute-done.direct_a = bf16[1,32,8,512]{3,2,1,0:T(8,128)(2,1)S(1)} collective-permute-done((bf16[1,32,8,512]{3,2,1,0:T(8,128)(2,1)S(1)}, bf16[1,32,8,512]{3,2,1,0:T(8,128)(2,1)S(1)}, u32[]{:S(2)}, u32[]{:S(2)}) %collective-permute-start) | collective-permute-done | bytes 262176 | tf_op jit(solution)/shard_map/ppermute | solution.py:180
  16.4 3.0 %collective-permute-done.1.direct_b = bf16[1,32,8,512]{3,2,1,0:T(8,128)(2,1)S(1)} collective-permute-done((bf16[1,32,8,512]{3,2,1,0:T(8,128)(2,1)S(1)}, bf16[1,32,8,512]{3,2,1,0:T(8,128)(2,1)S(1)}, u32[]{:S(2)}, u32[]{:S(2)}) %collective-permute-start.1) | collective-permute-done | bytes 262176 | tf_op jit(solution)/shard_map/ppermute | solution.py:181
  19.4 0.1 presum.1
  19.5 0.0 copy-start.1
  19.5 0.0 copy-start.2
  19.5 4.1 %collective-permute-done.3.second_a = bf16[32,8,512]{2,1,0:T(8,128)(2,1)S(1)} collective-permute-done((bf16[32,8,512]{2,1,0:T(8,128)(2,1)S(1)}, bf16[32,8,512]{2,1,0:T(8,128)(2,1)S(1)}, u32[]{:S(2)}, u32[]{:S(2)}) %collective-permute-start.3) | collective-permute-done | bytes 262176 | tf_op jit(solution)/shard_map/ppermute | solution.py:193
  23.6 0.0 collective-permute-done.5.second_b
  23.6 0.7 pack.1
  24.3 39.3 %all_to_all.10.arrived = bf16[64,2,8,512]{3,2,1,0:T(8,128)(2,1)S(1)} all-to-all(bf16[64,2,8,512]{3,2,1,0:T(8,128)(2,1)S(1)} %bitcast.18), channel_id=1, replica_groups=mesh['rep'=4,'fsdp'=64] {'fsdp'}, dimensions={0} | all-to-all | bytes 2097152 | tf_op jit(solution)/shard_map/all_to_all | solution.py:218
  63.6 0.0 copy-done.1
  63.6 0.0 copy-done.2
  63.6 8.9 %owner.1 = (f32[2,512,512]{2,1,0:T(8,128)}, f32[2,512,512]{2,1,0:T(8,128)}, bf16[64,2,8,512]{3,2,1,0:T(8,128)(2,1)S(1)}) custom-call(bf16[64,2,8,512]{3,2,1,0:T(8,128)(2,1)S(1)} %all_to_all.10.arrived, f32[2,512,512]{2,1,0:T(8,128)S(1)} %bitcast.21, f32[2,512,512]{2,1,0:T(8,128)S(1)} %bitcast.22), custom_call_target="tpu_custom_call" | custom-call | tf_op jit(solution)/shard_map/owner/pallas_call | solution.py:222
  72.5 34.2 %all_to_all.11 = bf16[64,2,8,512]{3,2,1,0:T(8,128)(2,1)S(1)} all-to-all(bf16[64,2,8,512]{3,2,1,0:T(8,128)(2,1)S(1)} %get-tuple-element.18), channel_id=1, replica_groups=mesh['rep'=4,'fsdp'=64] {'fsdp'}, dimensions={0} | all-to-all | bytes 2097152 | tf_op jit(solution)/shard_map/all_to_all | solution.py:236
  106.7 0.6 unpack.1
  107.4 0.1 collective-permute-start.6
  107.5 3.2 %collective-permute-start.8 = (bf16[32,8,512]{2,1,0:T(8,128)(2,1)S(1)}, bf16[32,8,512]{2,1,0:T(8,128)(2,1)S(1)}, u32[]{:S(2)}, u32[]{:S(2)}) collective-permute-start(bf16[32,8,512]{2,1,0:T(8,128)(2,1)S(1)} %get-tuple-element.20.refs_1_), channel_id=1, source_target_pairs={{0,192},{64,0},{128,64},{192,128},{1,193},{65,1},{129,65},{193,129... | collective-permute-start | bytes 786440 | tf_op jit(solution)/shard_map/ppermute | solution.py:251
  110.7 1.0 collective-permute-start.11
  111.6 1.1 collective-permute-start.10
  112.7 5.1 %collective-permute-done.6.refs_2_ = bf16[32,8,512]{2,1,0:T(8,128)(2,1)S(1)} collective-permute-done((bf16[32,8,512]{2,1,0:T(8,128)(2,1)S(1)}, bf16[32,8,512]{2,1,0:T(8,128)(2,1)S(1)}, u32[]{:S(2)}, u32[]{:S(2)}) %collective-permute-start.6) | collective-permute-done | bytes 262176 | tf_op jit(solution)/shard_map/ppermute | solution.py:250
  117.8 0.0 collective-permute-start.7
  117.8 0.0 collective-permute-done.8.refs_3_
  117.8 3.3 %collective-permute-start.9 = (bf16[32,8,512]{2,1,0:T(8,128)(2,1)S(1)}, bf16[32,8,512]{2,1,0:T(8,128)(2,1)S(1)}, u32[]{:S(2)}, u32[]{:S(2)}) collective-permute-start(bf16[32,8,512]{2,1,0:T(8,128)(2,1)S(1)} %collective-permute-done.8.refs_3_), channel_id=1, source_target_pairs={{0,192},{64,0},{128,64},{192,128},{1,193},{65,1},{129,65},{193,129... | collective-permute-start | bytes 786440 | tf_op jit(solution)/shard_map/ppermute | solution.py:255
  121.1 1.6 %place_first.1.refs_2_ = bf16[4,2,32,8,512]{4,3,2,1,0:T(8,128)(2,1)} custom-call(s32[1]{0:T(128)} %bitcast.table, bf16[32,8,512]{2,1,0:T(8,128)(2,1)S(1)} %get-tuple-element.19.refs_0_, bf16[32,8,512]{2,1,0:T(8,128)(2,1)S(1)} %get-tuple-element.20.refs_1_, bf16[32,8,512]{2,1,0:T(8,128)(2,1)S(1)} %collective-permute-done.6.refs_2_, ...), custom_call_target="tpu_custom_call" | custom-call | tf_op jit(solution)/shard_map/place_first/pallas_call | solution.py:268
  122.6 0.4 collective-permute-done.11.refs_1_
  123.0 0.4 collective-permute-done.10.refs_0_
  123.4 0.8 place_second.1.refs_2_
  124.2 4.1 %collective-permute-done.7.refs_0_ = bf16[32,8,512]{2,1,0:T(8,128)(2,1)S(1)} collective-permute-done((bf16[32,8,512]{2,1,0:T(8,128)(2,1)S(1)}, bf16[32,8,512]{2,1,0:T(8,128)(2,1)S(1)}, u32[]{:S(2)}, u32[]{:S(2)}) %collective-permute-start.7) | collective-permute-done | bytes 262176 | tf_op jit(solution)/shard_map/ppermute | solution.py:254
  128.3 0.0 collective-permute-done.9.refs_1_
  128.3 0.8 place_far.1
  (2 shorter events, 0.0 us)
Async XLA Ops:
  0.6 8.1 %copy-start.3 = (s32[4,64,1]{1,2,0:T(1,128)S(1)}, s32[4,64,1]{1,2,0:T(1,128)}, u32[]{:S(2)}) copy-start(s32[4,64,1]{1,2,0:T(1,128)} %param.7) | copy-start | bytes 3076
  1.7 8.6 %collective-permute-start.2 = (bf16[32,8,512]{2,1,0:T(8,128)(2,1)S(1)}, bf16[32,8,512]{2,1,0:T(8,128)(2,1)S(1)}, u32[]{:S(2)}, u32[]{:S(2)}) collective-permute-start(bf16[32,8,512]{2,1,0:T(8,128)(2,1)S(1)} %get-tuple-element.24), channel_id=1, source_target_pairs={{0,64},{64,0},{128,192},{192,128},{1,65},{65,1},{129,193},{193,129... | collective-permute-start | bytes 786440 | tf_op jit(solution)/shard_map/ppermute | solution.py:175
  3.4 10.8 %collective-permute-start.4 = (bf16[32,8,512]{2,1,0:T(8,128)(2,1)S(1)}, bf16[32,8,512]{2,1,0:T(8,128)(2,1)S(1)}, u32[]{:S(2)}, u32[]{:S(2)}) collective-permute-start(bf16[32,8,512]{2,1,0:T(8,128)(2,1)S(1)} %get-tuple-element.23), channel_id=1, source_target_pairs={{0,192},{64,128},{128,64},{192,0},{1,193},{65,129},{129,65},{193,1... | collective-permute-start | bytes 786440 | tf_op jit(solution)/shard_map/ppermute | solution.py:176
  5.6 1.6 %copy-start = (bf16[1,256,8,512]{3,2,1,0:T(8,128)(2,1)S(1)}, bf16[1,256,8,512]{3,2,1,0:T(8,128)(2,1)}, u32[]{:S(2)}) copy-start(bf16[1,256,8,512]{3,2,1,0:T(8,128)(2,1)} %param.4) | copy-start | bytes 6291460
  7.3 9.1 %collective-permute-start = (bf16[1,32,8,512]{3,2,1,0:T(8,128)(2,1)S(1)}, bf16[1,32,8,512]{3,2,1,0:T(8,128)(2,1)S(1)}, u32[]{:S(2)}, u32[]{:S(2)}) collective-permute-start(bf16[1,32,8,512]{3,2,1,0:T(8,128)(2,1)S(1)} %get-tuple-element.14), channel_id=1, source_target_pairs={{0,64},{64,0},{128,192},{192,128},{1,65},{65,1},{129,193},{193,129... | collective-permute-start | bytes 786440 | tf_op jit(solution)/shard_map/ppermute | solution.py:180
  8.1 11.3 %collective-permute-start.1 = (bf16[1,32,8,512]{3,2,1,0:T(8,128)(2,1)S(1)}, bf16[1,32,8,512]{3,2,1,0:T(8,128)(2,1)S(1)}, u32[]{:S(2)}, u32[]{:S(2)}) collective-permute-start(bf16[1,32,8,512]{3,2,1,0:T(8,128)(2,1)S(1)} %get-tuple-element.15), channel_id=1, source_target_pairs={{0,192},{64,128},{128,64},{192,0},{1,193},{65,129},{129,65},{193,1... | collective-permute-start | bytes 786440 | tf_op jit(solution)/shard_map/ppermute | solution.py:181
  10.4 13.2 %collective-permute-start.3 = (bf16[32,8,512]{2,1,0:T(8,128)(2,1)S(1)}, bf16[32,8,512]{2,1,0:T(8,128)(2,1)S(1)}, u32[]{:S(2)}, u32[]{:S(2)}) collective-permute-start(bf16[32,8,512]{2,1,0:T(8,128)(2,1)S(1)} %relay.2), channel_id=1, source_target_pairs={{0,192},{64,128},{128,64},{192,0},{1,193},{65,129},{129,65},{193,1... | collective-permute-start | bytes 786440 | tf_op jit(solution)/shard_map/ppermute | solution.py:193
  14.2 9.4 %collective-permute-start.5 = (bf16[32,8,512]{2,1,0:T(8,128)(2,1)S(1)}, bf16[32,8,512]{2,1,0:T(8,128)(2,1)S(1)}, u32[]{:S(2)}, u32[]{:S(2)}) collective-permute-start(bf16[32,8,512]{2,1,0:T(8,128)(2,1)S(1)} %relay.3), channel_id=1, source_target_pairs={{0,64},{64,0},{128,192},{192,128},{1,65},{65,1},{129,193},{193,129... | collective-permute-start | bytes 786440 | tf_op jit(solution)/shard_map/ppermute | solution.py:194
  19.5 44.1 %copy-start.1 = (f32[1,1,2,512,512]{4,3,2,1,0:T(8,128)S(1)}, f32[1,1,2,512,512]{4,3,2,1,0:T(8,128)}, u32[]{:S(2)}) copy-start(f32[1,1,2,512,512]{4,3,2,1,0:T(8,128)} %param.5) | copy-start | bytes 6291460
  19.5 44.1 %copy-start.2 = (f32[1,1,2,512,512]{4,3,2,1,0:T(8,128)S(1)}, f32[1,1,2,512,512]{4,3,2,1,0:T(8,128)}, u32[]{:S(2)}) copy-start(f32[1,1,2,512,512]{4,3,2,1,0:T(8,128)} %param.6) | copy-start | bytes 6291460
  107.4 10.4 %collective-permute-start.6 = (bf16[32,8,512]{2,1,0:T(8,128)(2,1)S(1)}, bf16[32,8,512]{2,1,0:T(8,128)(2,1)S(1)}, u32[]{:S(2)}, u32[]{:S(2)}) collective-permute-start(bf16[32,8,512]{2,1,0:T(8,128)(2,1)S(1)} %get-tuple-element.19.refs_0_), channel_id=1, source_target_pairs={{0,64},{64,128},{128,192},{192,0},{1,65},{65,129},{129,193},{193,1... | collective-permute-start | bytes 786440 | tf_op jit(solution)/shard_map/ppermute | solution.py:250
  107.5 10.3 %collective-permute-start.8 = (bf16[32,8,512]{2,1,0:T(8,128)(2,1)S(1)}, bf16[32,8,512]{2,1,0:T(8,128)(2,1)S(1)}, u32[]{:S(2)}, u32[]{:S(2)}) collective-permute-start(bf16[32,8,512]{2,1,0:T(8,128)(2,1)S(1)} %get-tuple-element.20.refs_1_), channel_id=1, source_target_pairs={{0,192},{64,0},{128,64},{192,128},{1,193},{65,1},{129,65},{193,129... | collective-permute-start | bytes 786440 | tf_op jit(solution)/shard_map/ppermute | solution.py:251
  110.7 12.3 %collective-permute-start.11 = (bf16[32,8,512]{2,1,0:T(8,128)(2,1)S(1)}, bf16[32,8,512]{2,1,0:T(8,128)(2,1)S(1)}, u32[]{:S(2)}, u32[]{:S(2)}) collective-permute-start(bf16[32,8,512]{2,1,0:T(8,128)(2,1)S(1)} %get-tuple-element.19.refs_0_), channel_id=1, source_target_pairs={{0,192},{64,0},{128,64},{192,128},{1,193},{65,1},{129,65},{193,129... | collective-permute-start | bytes 786440 | tf_op jit(solution)/shard_map/ppermute | solution.py:253
  111.6 11.8 %collective-permute-start.10 = (bf16[32,8,512]{2,1,0:T(8,128)(2,1)S(1)}, bf16[32,8,512]{2,1,0:T(8,128)(2,1)S(1)}, u32[]{:S(2)}, u32[]{:S(2)}) collective-permute-start(bf16[32,8,512]{2,1,0:T(8,128)(2,1)S(1)} %get-tuple-element.20.refs_1_), channel_id=1, source_target_pairs={{0,64},{64,128},{128,192},{192,0},{1,65},{65,129},{129,193},{193,1... | collective-permute-start | bytes 786440 | tf_op jit(solution)/shard_map/ppermute | solution.py:252
  117.8 10.6 %collective-permute-start.7 = (bf16[32,8,512]{2,1,0:T(8,128)(2,1)S(1)}, bf16[32,8,512]{2,1,0:T(8,128)(2,1)S(1)}, u32[]{:S(2)}, u32[]{:S(2)}) collective-permute-start(bf16[32,8,512]{2,1,0:T(8,128)(2,1)S(1)} %collective-permute-done.6.refs_2_), channel_id=1, source_target_pairs={{0,64},{64,128},{128,192},{192,0},{1,65},{65,129},{129,193},{193,1... | collective-permute-start | bytes 786440 | tf_op jit(solution)/shard_map/ppermute | solution.py:254
  117.8 10.6 %collective-permute-start.9 = (bf16[32,8,512]{2,1,0:T(8,128)(2,1)S(1)}, bf16[32,8,512]{2,1,0:T(8,128)(2,1)S(1)}, u32[]{:S(2)}, u32[]{:S(2)}) collective-permute-start(bf16[32,8,512]{2,1,0:T(8,128)(2,1)S(1)} %collective-permute-done.8.refs_3_), channel_id=1, source_target_pairs={{0,192},{64,0},{128,64},{192,128},{1,193},{65,1},{129,65},{193,129... | collective-permute-start | bytes 786440 | tf_op jit(solution)/shard_map/ppermute | solution.py:255
